TPU v7x, 128 devices: a whole 4x4x4 slice. The times are simulated.
128 devices in a mesh: tm: 16 (over y_lo, x, core), row: 8 (over z, y_hi).
Axes of the slice: x: 4, y: 4 (y_hi: 2, y_lo: 2; y = y_hi * 2 + y_lo), z: 4, core: 2. Of those that a mesh axis runs over, the one named last changes fastest.
Arguments:
- feature: bfloat16 [64, 32, 128, 384], P('tm', 'row'), may hold values from -6 to 6
- conv_weight: bfloat16 [3, 3, 3, 384, 384], replicated, may hold values from -0.0625 to 0.0625
- conv_bias: float32 [384], replicated, may hold values from -3 to 3
- down_weight: bfloat16 [3, 2, 2, 384, 16], replicated, may hold values from -0.09375 to 0.09375
- down_bias: float32 [16], replicated, may hold values from -3 to 3
Outputs:
- tokens: float32 [8192, 64], P(('tm', 'row'))
All inputs are finite; a program needn't handle non-finite values.
Results may differ from a plain program's by a relative error of at most 0.0022.
Values may be sent and summed in bfloat16 or wider, within the bound.
No kernel may reach another device: no remote copies, remote signals or barrier semaphores. Data moves between devices by JAX's collectives and lax.ppermute only.
A program may use at most 128 MiB of HBM per device.

v0:
```python
import jax
import jax.numpy as jnp
from jax import lax
from jax.sharding import PartitionSpec as P

Z = 16


def with_halo(block, sides, width):
    for axis, dim in sides:
        count = lax.axis_size(axis)
        forward = [(i, i + 1) for i in range(count - 1)]
        backward = [(target, source) for source, target in forward]
        low = lax.ppermute(
            lax.slice_in_dim(block, block.shape[dim] - width, None, axis=dim), axis, forward
        )
        high = lax.ppermute(lax.slice_in_dim(block, 0, width, axis=dim), axis, backward)
        block = jnp.concatenate([low, block, high], axis=dim)
    return block


def passed_along(shard, axis, by):
    length = lax.axis_size(axis)
    pairs = [(i, i + by) for i in range(length) if 0 <= i + by < length]
    return lax.ppermute(shard, axis, pairs)


def convolve(extended, conv_weight, conv_bias, frames):
    channels = extended.shape[-1]
    height = extended.shape[1] - 2
    width = extended.shape[2]
    total = jnp.zeros((frames * height * width, 3 * channels), jnp.float32)
    for tap_time in range(3):
        for tap_row in range(3):
            slab = extended[tap_time : tap_time + frames, tap_row : tap_row + height].reshape(
                frames * height * width, channels
            )
            mixed = (
                conv_weight[tap_time, tap_row].transpose(1, 0, 2).reshape(channels, 3 * channels)
            )
            total = total + jnp.dot(slab, mixed, preferred_element_type=jnp.float32)
    total = total.reshape(frames * height, width, 3 * channels)
    left_part = total[:, : width - 1, :channels]
    centre = total[:, :, channels : 2 * channels]
    right_part = total[:, 1:, 2 * channels :]
    pre = (
        centre
        + jnp.pad(left_part, ((0, 0), (1, 0), (0, 0)))
        + jnp.pad(right_part, ((0, 0), (0, 1), (0, 0)))
    )
    return (
        jax.nn.silu(pre + conv_bias).astype(jnp.bfloat16).reshape(frames, height, width, channels)
    )


def on_device(feature, conv_weight, conv_bias, down_weight, down_bias):
    channels = feature.shape[-1]
    own_frames = feature.shape[0]
    own_rows = feature.shape[1]
    depth = 2
    banded = with_halo(feature, (("row", 1),), 1)
    earlier = passed_along(banded[own_frames - depth :], "tm", 1)
    extended = jnp.concatenate([earlier, banded], axis=0)
    activated = convolve(extended, conv_weight, conv_bias, own_frames)
    previous = passed_along(activated[own_frames - 1 :], "tm", 1)
    shifted = jnp.concatenate([previous, activated], axis=0)
    lat_frames = own_frames // 2
    lat_rows = own_rows // 2
    lat_cols = feature.shape[2] // 2
    latent = jnp.zeros((lat_frames, lat_rows, lat_cols, Z), jnp.float32)
    for tap_time in range(3):
        part = shifted[tap_time : tap_time + own_frames : 2].reshape(
            lat_frames, lat_rows, 2, lat_cols, 2, channels
        )
        latent = latent + jnp.einsum(
            "fidjek,dekz->fijz", part, down_weight[tap_time], preferred_element_type=jnp.float32
        )
    latent = latent + down_bias
    patch_cols = lat_cols // 2
    mine = (
        latent.reshape(lat_frames, 2, patch_cols, 2, Z)
        .transpose(0, 2, 1, 3, 4)
        .reshape(lat_frames, patch_cols, 4 * Z)
    )
    band = lax.axis_index("row")
    n_bands = lax.axis_size("row")
    frame_range = jnp.arange(lat_frames, dtype=jnp.int32)
    slot_ids = jnp.arange(n_bands * lat_frames, dtype=jnp.int32)
    select = (slot_ids % n_bands == band)[:, None] & (
        (slot_ids // n_bands)[:, None] == frame_range[None, :]
    )
    outgoing = jnp.sum(jnp.where(select[:, :, None, None], mine[None], 0.0), axis=1)
    outgoing = outgoing.reshape(n_bands, lat_frames, patch_cols, 4 * Z)
    incoming = lax.all_to_all(outgoing, "row", split_axis=0, concat_axis=0, tiled=True)
    result = jnp.sum(incoming, axis=0)
    return result.reshape(lat_frames * patch_cols, 4 * Z)


def solution(mesh):
    return jax.shard_map(
        on_device,
        mesh=mesh,
        in_specs=(P("tm", "row", None, None), P(), P(), P(), P()),
        out_specs=P(("tm", "row"), None),
        check_vma=False,
    )
```

profile of v0, /device:TPU:8, one launch (start us, length us, event | category | flops | bytes accessed | tf_op | source)
XLA Modules:
  0.0 130.0 jit_solution(8389303198584256636)
XLA Ops:
  0.0 2.1 %fusion.24 = (bf16[4,1,128,384]{3,2,1,0:T(8,128)(2,1)}, bf16[4,1,128,384]{3,2,1,0:T(8,128)(2,1)}) fusion(bf16[4,4,128,384]{3,2,1,0:T(8,128)(2,1)} %param.5), kind=kLoop, calls=%fused_computation.60 | loop fusion | bytes 1572864 | tf_op jit(solution)/shard_map/slice | solution.py:15
  2.1 5.0 %collective-permute-start = (bf16[4,1,128,384]{3,2,1,0:T(8,128)(2,1)}, bf16[4,1,128,384]{3,2,1,0:T(8,128)(2,1)}, u32[]{:S(2)}, u32[]{:S(2)}) collective-permute-start(bf16[4,1,128,384]{3,2,1,0:T(8,128)(2,1)} %get-tuple-element.27), channel_id=1, source_target_pairs={{0,1},{1,2},{2,3},{3,4},{4,5},{5,6},{6,7},{8,9},{9,10},{10,11},{11... | collective-permute-start | bytes 1179656 | tf_op jit(solution)/shard_map/ppermute | solution.py:14
  7.1 1.3 collective-permute-start.1
  8.3 5.3 %fusion.22 = (bf16[1,1,3,384,384]{4,3,2,1,0:T(8,128)(2,1)S(1)}, bf16[1,1,3,384,384]{4,3,2,1,0:T(8,128)(2,1)}, bf16[1,1,3,384,384]{4,3,2,1,0:T(8,128)(2,1)S(1)}, ...) fusion(bf16[3,3,3,384,384]{4,3,2,1,0:T(8,128)(2,1)} %param.6), kind=kLoop, calls=%fused_computation.58 | loop fusion | bytes 15925248 | tf_op jit(solution)/shard_map/slice | solution.py:39
  13.6 2.3 %copy.64 = bf16[1,1,3,384,384]{3,4,2,1,0:T(8,128)(2,1)} copy(bf16[1,1,3,384,384]{4,3,2,1,0:T(8,128)(2,1)} %get-tuple-element.13) | data formatting | bytes 1769472
  15.9 2.3 %copy.63 = bf16[1,1,3,384,384]{3,4,2,1,0:T(8,128)(2,1)} copy(bf16[1,1,3,384,384]{4,3,2,1,0:T(8,128)(2,1)} %get-tuple-element.14) | data formatting | bytes 1769472
  18.2 2.3 %copy.65 = bf16[1,1,3,384,384]{3,4,2,1,0:T(8,128)(2,1)} copy(bf16[1,1,3,384,384]{4,3,2,1,0:T(8,128)(2,1)} %get-tuple-element.12) | data formatting | bytes 1769472
  20.5 2.1 %copy.66 = bf16[1,1,3,384,384]{3,4,2,1,0:T(8,128)(2,1)} copy(bf16[1,1,3,384,384]{4,3,2,1,0:T(8,128)(2,1)S(1)} %get-tuple-element.11) | data formatting | bytes 1769472
  22.6 2.2 %copy.67 = bf16[1,1,3,384,384]{3,4,2,1,0:T(8,128)(2,1)} copy(bf16[1,1,3,384,384]{4,3,2,1,0:T(8,128)(2,1)S(1)} %get-tuple-element.10) | data formatting | bytes 1769472
  24.8 2.1 %copy.68 = bf16[1,1,3,384,384]{3,4,2,1,0:T(8,128)(2,1)} copy(bf16[1,1,3,384,384]{4,3,2,1,0:T(8,128)(2,1)S(1)} %get-tuple-element.9) | data formatting | bytes 1769472
  26.9 2.3 %copy.69 = bf16[1,1,3,384,384]{3,4,2,1,0:T(8,128)(2,1)S(1)} copy(bf16[1,1,3,384,384]{4,3,2,1,0:T(8,128)(2,1)S(1)} %get-tuple-element.7) | data formatting | bytes 1769472
  29.2 2.6 %copy.70 = bf16[1,1,3,384,384]{3,4,2,1,0:T(8,128)(2,1)S(1)} copy(bf16[1,1,3,384,384]{4,3,2,1,0:T(8,128)(2,1)} %get-tuple-element.8) | data formatting | bytes 1769472
  31.8 2.3 %copy.71 = bf16[1,1,3,384,384]{3,4,2,1,0:T(8,128)(2,1)} copy(bf16[1,1,3,384,384]{4,3,2,1,0:T(8,128)(2,1)} %get-tuple-element.15) | data formatting | bytes 1769472
  35.2 2.9 %pad_maximum_fusion.2 = (bf16[4,4,128,384]{3,2,1,0:T(8,128)(2,1)S(1)}, bf16[4,4,128,384]{3,2,1,0:T(8,128)(2,1)}, bf16[4,6,128,384]{3,2,1,0:T(8,128)(2,1)S(1)}) fusion(bf16[4,4,128,384]{3,2,1,0:T(8,128)(2,1)S(1)} %copy-done, bf16[4,1,128,384]{3,2,1,0:T(8,128)(2,1)} %collective-permute-done, bf16[4,1,128,384]{3,2,1,0:T(8,128)(2,1)} %collective-permute-done.1, ...), kind=kLoop, calls=%fused_computation.27 | loop fusion | flops 6291456 | bytes 7077888 | tf_op jit(solution)/shard_map/concatenate | solution.py:18
  38.1 1.1 constant_dynamic-update-slice_fusion
  39.3 1.9 %collective-permute-start.2 = (bf16[2,6,128,384]{3,2,1,0:T(8,128)(2,1)S(1)}, bf16[2,6,128,384]{3,2,1,0:T(8,128)(2,1)S(1)}, u32[]{:S(2)}, u32[]{:S(2)}) collective-permute-start(bf16[2,6,128,384]{3,2,1,0:T(8,128)(2,1)S(1)} %slice.126), channel_id=1, source_target_pairs={{0,8},{8,16},{16,24},{24,32},{32,40},{40,48},{48,56},{56,64},{64,7... | collective-permute-start | bytes 3538952 | tf_op jit(solution)/shard_map/ppermute | solution.py:25
  41.3 5.1 %fusion.27 = f32[2048,1152]{1,0:T(8,128)} fusion(bf16[2048,384]{1,0:T(8,128)(2,1)S(1)} %bitcast.133, bf16[384,1152]{0,1:T(8,128)(2,1)S(1)} %bitcast.139), kind=kOutput, calls=%fused_computation.63 | convolution fusion | flops 1811939328 | bytes 11894784 | tf_op jit(solution)/shard_map/dot_general | solution.py:41
  46.5 5.1 %fusion.26 = f32[2048,1152]{1,0:T(8,128)} fusion(bf16[2048,384]{1,0:T(8,128)(2,1)S(1)} %bitcast.134, bf16[384,1152]{0,1:T(8,128)(2,1)S(1)} %bitcast.138), kind=kOutput, calls=%fused_computation.62 | convolution fusion | flops 1811939328 | bytes 11894784 | tf_op jit(solution)/shard_map/dot_general | solution.py:41
  51.6 7.4 %collective-permute-done.2 = bf16[2,6,128,384]{3,2,1,0:T(8,128)(2,1)S(1)} collective-permute-done((bf16[2,6,128,384]{3,2,1,0:T(8,128)(2,1)S(1)}, bf16[2,6,128,384]{3,2,1,0:T(8,128)(2,1)S(1)}, u32[]{:S(2)}, u32[]{:S(2)}) %collective-permute-start.2) | collective-permute-done | bytes 1179680 | tf_op jit(solution)/shard_map/ppermute | solution.py:25
  59.0 1.4 %pad_maximum_fusion.3 = (bf16[4,4,128,384]{3,2,1,0:T(8,128)(2,1)S(1)}, bf16[4,4,128,384]{3,2,1,0:T(8,128)(2,1)S(1)}, bf16[4,4,128,384]{3,2,1,0:T(8,128)(2,1)S(1)...) fusion(bf16[4,6,128,384]{3,2,1,0:T(8,128)(2,1)S(1)} %constant_d, ...), kind=kLoop, calls=%fused_computation.28 | loop fusion | flops 4718592 | bytes 12976128 | tf_op jit(solution)/shard_map/concatenate | solution.py:63
  60.4 2.8 %fusion.25 = f32[2048,1152]{1,0:T(8,128)S(1)} fusion(bf16[2048,384]{1,0:T(8,128)(2,1)S(1)} %bitcast.135, bf16[384,1152]{0,1:T(8,128)(2,1)S(1)} %bitcast.137), kind=kOutput, calls=%fused_computation.61 | convolution fusion | flops 1811939328 | bytes 11894784 | tf_op jit(solution)/shard_map/dot_general | solution.py:41
  63.1 2.8 %convolution_add_fusion.5 = f32[2048,1152]{1,0:T(8,128)S(1)} fusion(f32[2048,1152]{1,0:T(8,128)S(1)} %fusion.25, bf16[2048,384]{1,0:T(8,128)(2,1)S(1)} %bitcast.132, bf16[384,1152]{0,1:T(8,128)(2,1)S(1)} %bitcast.145), kind=kOutput, calls=%fused_computation.5 | convolution fusion | flops 1814298624 | bytes 21331968 | tf_op jit(solution)/shard_map/dot_general | solution.py:41
  65.9 2.8 %convolution_add_fusion.4 = f32[2048,1152]{1,0:T(8,128)S(1)} fusion(f32[2048,1152]{1,0:T(8,128)S(1)} %convolution_add_fusion.5, bf16[2048,384]{1,0:T(8,128)(2,1)S(1)} %bitcast.131, bf16[384,1152]{0,1:T(8,128)(2,1)S(1)} %bitcast.144), kind=kOutput, calls=%fused_computation.4 | convolution fusion | flops 1814298624 | bytes 21331968 | tf_op jit(solution)/shard_map/dot_general | solution.py:41
  68.7 4.1 %convolution_add_fusion.3 = f32[2048,1152]{1,0:T(8,128)S(1)} fusion(f32[2048,1152]{1,0:T(8,128)S(1)} %convolution_add_fusion.4, bf16[2048,384]{1,0:T(8,128)(2,1)S(1)} %bitcast.130, bf16[384,1152]{0,1:T(8,128)(2,1)} %bitcast.143), kind=kOutput, calls=%fused_computation.3 | convolution fusion | flops 1814298624 | bytes 21331968 | tf_op jit(solution)/shard_map/dot_general | solution.py:41
  72.8 4.4 %convolution_add_fusion.2 = f32[2048,1152]{1,0:T(8,128)S(1)} fusion(f32[2048,1152]{1,0:T(8,128)S(1)} %convolution_add_fusion.3, bf16[2048,384]{1,0:T(8,128)(2,1)S(1)} %bitcast.129, bf16[384,1152]{0,1:T(8,128)(2,1)} %bitcast.142), kind=kOutput, calls=%fused_computation.2 | convolution fusion | flops 1814298624 | bytes 21331968 | tf_op jit(solution)/shard_map/dot_general | solution.py:41
  77.3 3.0 %convolution_add_fusion.1 = f32[2048,1152]{1,0:T(8,128)S(1)} fusion(f32[2048,1152]{1,0:T(8,128)S(1)} %convolution_add_fusion.2, bf16[2048,384]{1,0:T(8,128)(2,1)S(1)} %bitcast.128, bf16[384,1152]{0,1:T(8,128)(2,1)S(1)} %bitcast.140), kind=kOutput, calls=%fused_computation.1 | convolution fusion | flops 1814298624 | bytes 21331968 | tf_op jit(solution)/shard_map/dot_general | solution.py:41
  80.3 10.5 %convolution_add_fusion = f32[2048,1152]{1,0:T(8,128)} fusion(bf16[2048,384]{1,0:T(8,128)(2,1)S(1)} %bitcast.136, bf16[384,1152]{0,1:T(8,128)(2,1)S(1)} %bitcast.141, f32[2048,1152]{1,0:T(8,128)} %fusion.27, f32[2048,1152]{1,0:T(8,128)S(1)} %convolution_add_fusion.1, f32[2048,1152]{1,0:T(8,128)} %fusion.26), kind=kOutput, calls=%fused_computation | convolution fusion | flops 1819017216 | bytes 40206336 | tf_op jit(solution)/shard_map/dot_general | solution.py:41
  90.8 3.5 %fusion.21 = (f32[16,127,384]{2,1,0:T(8,128)S(1)}, f32[16,127,384]{2,1,0:T(8,128)S(1)}) fusion(f32[16,128,1152]{2,1,0:T(8,128)} %bitcast.124), kind=kLoop, calls=%fused_computation.57 | loop fusion | bytes 12484608 | tf_op jit(solution)/shard_map/slice | solution.py:43
  94.4 3.1 %multiply_convert_fusion = bf16[16,128,384]{2,1,0:T(8,128)(2,1)S(1)} fusion(f32[16,128,1152]{2,1,0:T(8,128)} %bitcast.125, f32[16,127,384]{2,1,0:T(8,128)S(1)} %get-tuple-element.6, f32[16,127,384]{2,1,0:T(8,128)S(1)} %get-tuple-element.5, f32[384]{0:T(512)S(1)} %copy-done.7), kind=kLoop, calls=%fused_computation.19 | loop fusion | flops 6291456 | bytes 10962432 | tf_op jit(solution)/shard_map/convert_element_type | solution.py:52
  97.5 1.9 %collective-permute-start.3 = (bf16[1,4,128,384]{3,2,1,0:T(8,128)(2,1)S(1)}, bf16[1,4,128,384]{3,2,1,0:T(8,128)(2,1)S(1)}, u32[]{:S(2)}, u32[]{:S(2)}) collective-permute-start(bf16[1,4,128,384]{3,2,1,0:T(8,128)(2,1)S(1)} %slice_bitcast_fusion), channel_id=1, source_target_pairs={{0,8},{8,16},{16,24},{24,32},{32,40},{40,48},{48,56},{56,64},{64,7... | collective-permute-start | bytes 1179656 | tf_op jit(solution)/shard_map/ppermute | solution.py:25
  102.1 6.6 %collective-permute-done.3 = bf16[1,4,128,384]{3,2,1,0:T(8,128)(2,1)S(1)} collective-permute-done((bf16[1,4,128,384]{3,2,1,0:T(8,128)(2,1)S(1)}, bf16[1,4,128,384]{3,2,1,0:T(8,128)(2,1)S(1)}, u32[]{:S(2)}, u32[]{:S(2)}) %collective-permute-start.3) | collective-permute-done | bytes 393248 | tf_op jit(solution)/shard_map/ppermute | solution.py:25
  110.9 16.9 %all_to_all.5 = f32[8,1,4096]{2,1,0:T(1,128)S(1)} all-to-all(f32[8,1,4096]{2,1,0:T(1,128)S(1)} %reshape.172), channel_id=1, replica_groups=mesh['tm'=16,'row'=8] {'row'}, dimensions={0} | all-to-all | bytes 262144 | tf_op jit(solution)/shard_map/all_to_all | solution.py:94
  (46 shorter events, 8.3 us)
Async XLA Ops:
  2.1 32.1 %collective-permute-start = (bf16[4,1,128,384]{3,2,1,0:T(8,128)(2,1)}, bf16[4,1,128,384]{3,2,1,0:T(8,128)(2,1)}, u32[]{:S(2)}, u32[]{:S(2)}) collective-permute-start(bf16[4,1,128,384]{3,2,1,0:T(8,128)(2,1)} %get-tuple-element.27), channel_id=1, source_target_pairs={{0,1},{1,2},{2,3},{3,4},{4,5},{5,6},{6,7},{8,9},{9,10},{10,11},{11... | collective-permute-start | bytes 1179656 | tf_op jit(solution)/shard_map/ppermute | solution.py:14
  7.1 28.2 %collective-permute-start.1 = (bf16[4,1,128,384]{3,2,1,0:T(8,128)(2,1)}, bf16[4,1,128,384]{3,2,1,0:T(8,128)(2,1)}, u32[]{:S(2)}, u32[]{:S(2)}) collective-permute-start(bf16[4,1,128,384]{3,2,1,0:T(8,128)(2,1)} %get-tuple-element.28), channel_id=1, source_target_pairs={{1,0},{2,1},{3,2},{4,3},{5,4},{6,5},{7,6},{9,8},{10,9},{11,10},{12... | collective-permute-start | bytes 1179656 | tf_op jit(solution)/shard_map/ppermute | solution.py:17
  29.2 6.0 %copy-start = (bf16[4,4,128,384]{3,2,1,0:T(8,128)(2,1)S(1)}, bf16[4,4,128,384]{3,2,1,0:T(8,128)(2,1)}, u32[]{:S(2)}) copy-start(bf16[4,4,128,384]{3,2,1,0:T(8,128)(2,1)} %param.5) | copy-start | bytes 4718596
  39.3 19.6 %collective-permute-start.2 = (bf16[2,6,128,384]{3,2,1,0:T(8,128)(2,1)S(1)}, bf16[2,6,128,384]{3,2,1,0:T(8,128)(2,1)S(1)}, u32[]{:S(2)}, u32[]{:S(2)}) collective-permute-start(bf16[2,6,128,384]{3,2,1,0:T(8,128)(2,1)S(1)} %slice.126), channel_id=1, source_target_pairs={{0,8},{8,16},{16,24},{24,32},{32,40},{40,48},{48,56},{56,64},{64,7... | collective-permute-start | bytes 3538952 | tf_op jit(solution)/shard_map/ppermute | solution.py:25
  51.6 8.8 %copy-start.2 = (bf16[1,1,3,384,384]{3,4,2,1,0:T(8,128)(2,1)S(1)}, bf16[1,1,3,384,384]{3,4,2,1,0:T(8,128)(2,1)}, u32[]{:S(2)}) copy-start(bf16[1,1,3,384,384]{3,4,2,1,0:T(8,128)(2,1)} %copy.64) | copy-start | bytes 2654212
  60.3 2.8 %copy-start.6 = (bf16[1,1,3,384,384]{3,4,2,1,0:T(8,128)(2,1)S(1)}, bf16[1,1,3,384,384]{3,4,2,1,0:T(8,128)(2,1)}, u32[]{:S(2)}) copy-start(bf16[1,1,3,384,384]{3,4,2,1,0:T(8,128)(2,1)} %copy.63) | copy-start | bytes 2654212
  63.1 2.8 %copy-start.5 = (bf16[1,1,3,384,384]{3,4,2,1,0:T(8,128)(2,1)S(1)}, bf16[1,1,3,384,384]{3,4,2,1,0:T(8,128)(2,1)}, u32[]{:S(2)}) copy-start(bf16[1,1,3,384,384]{3,4,2,1,0:T(8,128)(2,1)} %copy.65) | copy-start | bytes 2654212
  72.8 4.4 %copy-start.3 = (bf16[1,1,3,384,384]{3,4,2,1,0:T(8,128)(2,1)S(1)}, bf16[1,1,3,384,384]{3,4,2,1,0:T(8,128)(2,1)}, u32[]{:S(2)}) copy-start(bf16[1,1,3,384,384]{3,4,2,1,0:T(8,128)(2,1)} %copy.68) | copy-start | bytes 2654212
  77.3 3.0 %copy-start.1 = (bf16[4,4,128,384]{3,2,1,0:T(8,128)(2,1)S(1)}, bf16[4,4,128,384]{3,2,1,0:T(8,128)(2,1)}, u32[]{:S(2)}) copy-start(bf16[4,4,128,384]{3,2,1,0:T(8,128)(2,1)} %get-tuple-element.25) | copy-start | bytes 4718596
  77.3 3.0 %copy-start.4 = (bf16[1,1,3,384,384]{3,4,2,1,0:T(8,128)(2,1)S(1)}, bf16[1,1,3,384,384]{3,4,2,1,0:T(8,128)(2,1)}, u32[]{:S(2)}) copy-start(bf16[1,1,3,384,384]{3,4,2,1,0:T(8,128)(2,1)} %copy.71) | copy-start | bytes 2654212
  90.8 3.6 %copy-start.7 = (f32[384]{0:T(512)S(1)}, f32[384]{0:T(512)}, u32[]{:S(2)}) copy-start(f32[384]{0:T(512)} %param.7) | copy-start | bytes 4612
  97.5 11.2 %collective-permute-start.3 = (bf16[1,4,128,384]{3,2,1,0:T(8,128)(2,1)S(1)}, bf16[1,4,128,384]{3,2,1,0:T(8,128)(2,1)S(1)}, u32[]{:S(2)}, u32[]{:S(2)}) collective-permute-start(bf16[1,4,128,384]{3,2,1,0:T(8,128)(2,1)S(1)} %slice_bitcast_fusion), channel_id=1, source_target_pairs={{0,8},{8,16},{16,24},{24,32},{32,40},{40,48},{48,56},{56,64},{64,7... | collective-permute-start | bytes 1179656 | tf_op jit(solution)/shard_map/ppermute | solution.py:25
  99.6 1.7 %copy-start.8 = (bf16[3,2,2,384,16]{3,4,2,1,0:T(8,128)(2,1)S(1)}, bf16[3,2,2,384,16]{3,4,2,1,0:T(8,128)(2,1)}, u32[]{:S(2)}) copy-start(bf16[3,2,2,384,16]{3,4,2,1,0:T(8,128)(2,1)} %param.8) | copy-start | bytes 442372
  108.9 0.9 copy-start.9
where the time goes:
time: 131 us; the launch traced here: 130 us
  matrix products  41.8 us (32%)
  local copies, waits for them, and re-layouts  37.5 us (29%)
  blocking collectives  16.9 us (13%)
  waiting for transfers between devices  14 us (11%)
  starting transfers between devices  10.1 us (8%)
  other arithmetic  9.41 us (7%)
    dot_general x9, matrix products, convolve(): total = total + jnp.dot(slab, mixed, preferred_element_type=jnp.float32)  40.6 us
    unnamed x32, local copies, waits for them, and re-layouts  21.8 us
    all_to_all x1, blocking collectives, on_device(): lax.all_to_all(outgoing, 'row', split_axis=0, concat_axis=0, tiled=True)  16.9 us
    ppermute x2, waiting for transfers between devices, passed_along(): return lax.ppermute(shard, axis, pairs)  14 us
    slice x1, local copies, waits for them, and re-layouts, convolve(): conv_weight[tap_time, tap_row].transpose(1, 0, 2)  5.3 us
    ppermute x1, starting transfers between devices, with_halo(): lax.ppermute(lax.slice_in_dim(block, block.shape[dim] - width, None, axis...  4.97 us
    ppermute x2, starting transfers between devices, passed_along(): return lax.ppermute(shard, axis, pairs)  3.84 us
    slice x1, local copies, waits for them, and re-layouts, convolve(): left_part = total[:, :width - 1, :channels]  3.54 us
  transfers between devices with their start and end apart: 4, of which 2 were waited for; matrix products, arithmetic and copies ran while one was open for 31% of the time, Pallas kernels for 0%

commit v1 on v0

v1 whole, which is shorter than its diff:
```python
import jax
import jax.numpy as jnp
from jax import lax
from jax.experimental import pallas as pl
from jax.experimental.pallas import tpu as pltpu
from jax.sharding import PartitionSpec as P

F32 = jnp.float32
BF16 = jnp.bfloat16
VMEM_LIMIT = 48 * 1024 * 1024


def widen(rows, store, width, channels):
    value = rows.astype(F32)
    column = lax.broadcasted_iota(jnp.int32, (width, channels), 0)
    before = jnp.where(column == 0, 0.0, pltpu.roll(value, 1, 0))
    after = jnp.where(column == width - 1, 0.0, pltpu.roll(value, width - 1, 0))
    store(slice(0, channels), before.astype(BF16))
    store(slice(channels, 2 * channels), rows)
    store(slice(2 * channels, 3 * channels), after.astype(BF16))


def silu(pre):
    return pre / (1.0 + jnp.exp(-pre))


def token_rows(product, d_ref, half, i):
    d_ref[half] = product
    count = product.shape[0] // 4
    lane = lax.broadcasted_iota(jnp.int32, (count, 128), 1)
    right_row = (lane // 32) % 2 == i // 2
    total = jnp.zeros((count, 128), F32)
    for s in range(4):
        keep = right_row & (lane // 64 == s % 2) & ((lane // 16) % 2 == s // 2)
        total = total + jnp.where(keep, d_ref[half, pl.ds(s, count, stride=4), :], 0.0)
    return total


def project(pre, bias_ref, even_ref, odd_ref, d_ref, f, i):
    act = silu(pre + bias_ref[...]).astype(BF16)
    if f % 2 == 0:
        product = jnp.dot(act, even_ref[i % 2], preferred_element_type=F32)
        return token_rows(product, d_ref, 0, i), None
    product = jnp.dot(act, odd_ref[i % 2], preferred_element_type=F32)
    return token_rows(product[:, :128], d_ref, 0, i), token_rows(product[:, 128:], d_ref, 1, i)


def own_kernel(x_ref, w_ref, bias_ref, even_ref, odd_ref, early_ref, edge_ref, tok_ref, acc, wide, d_ref):
    step = pl.program_id(0)
    frames, height, width, channels = x_ref.shape
    tap_time = 2 - step // 3

    @pl.when(step == 0)
    def _():
        def one(n, carry):
            f, h = n // height, n % height

            def store(lanes, value):
                wide[f, h, :, lanes] = value

            widen(x_ref[f, h], store, width, channels)
            return carry

        lax.fori_loop(0, frames * height, one, 0)

    def tap(first, count, shift, init):
        weight = w_ref[0, 0].reshape(3 * channels, channels)

        def one(g, carry):
            left = wide[g, first : first + count].reshape(count * width, 3 * channels)
            product = jnp.dot(left, weight, preferred_element_type=F32).reshape(count, width, channels)
            target = (g + 2 - tap_time, slice(first + shift, first + shift + count))
            if init:
                acc[target] = product
            else:
                acc[target] += product
            return carry

        lax.fori_loop(0, frames - 2 + tap_time, one, 0)

    pl.when(step == 0)(lambda: tap(0, height, 0, True))
    pl.when((step % 3 == 0) & (step > 0))(lambda: tap(0, height, 0, False))
    pl.when(step % 3 == 1)(lambda: tap(0, height - 1, 1, False))
    pl.when(step % 3 == 2)(lambda: tap(1, height - 1, -1, False))

    @pl.when(step == 8)
    def _():
        early_ref[...] = acc[:2]
        for side, i in enumerate((0, height - 1)):
            for f in (2, 3):
                edge_ref[f - 2, side] = acc[f, i]
        late = jnp.zeros((width // 4, 128), F32)
        coming = jnp.zeros((width // 4, 128), F32)
        for i in range(1, height - 1):
            for f in (2, 3):
                main, other = project(acc[f, i], bias_ref, even_ref, odd_ref, d_ref, f, i)
                late = late + main
                if other is not None:
                    coming = coming + other
        tok_ref[0] = late
        tok_ref[1] = coming


def earlier_kernel(x_ref, early_in, w_ref, bias_ref, even_ref, odd_ref, edge_ref, tok_ref, acc, wide, d_ref):
    step = pl.program_id(0)
    frames, height, width, channels = x_ref.shape
    tap_time = step // 3

    @pl.when(step == 0)
    def _():
        def one(n, carry):
            f, h = n // height, n % height

            def store(lanes, value):
                wide[f, h, :, lanes] = value

            widen(x_ref[f, h], store, width, channels)
            return carry

        lax.fori_loop(0, frames * height, one, 0)
        acc[...] = early_in[...]

    def tap(first, count, shift):
        weight = w_ref[0, 0].reshape(3 * channels, channels)

        def one(f, carry):
            left = wide[f + tap_time, first : first + count].reshape(count * width, 3 * channels)
            product = jnp.dot(left, weight, preferred_element_type=F32).reshape(count, width, channels)
            acc[f, first + shift : first + shift + count] += product
            return carry

        lax.fori_loop(0, 2 - tap_time, one, 0)

    pl.when(step % 3 == 0)(lambda: tap(0, height, 0))
    pl.when(step % 3 == 1)(lambda: tap(0, height - 1, 1))
    pl.when(step % 3 == 2)(lambda: tap(1, height - 1, -1))

    @pl.when(step == 5)
    def _():
        for side, i in enumerate((0, height - 1)):
            for f in (0, 1):
                edge_ref[f, side] = acc[f, i]
        first = jnp.zeros((width // 4, 128), F32)
        late = jnp.zeros((width // 4, 128), F32)
        for i in range(1, height - 1):
            for f in (0, 1):
                main, other = project(acc[f, i], bias_ref, even_ref, odd_ref, d_ref, f, i)
                first = first + main
                if other is not None:
                    late = late + other
        tok_ref[0] = first
        tok_ref[1] = late


def edge_kernel(
    odd_row_ref, up23, dn23, up01, dn01, corner, edge01, edge23, tok_a, tok_b, w_ref, bias_ref, even_ref, odd_ref,
    down_bias_ref, out_ref, acc, wide, d_ref,
):
    step = pl.program_id(0)
    width, channels = up23.shape[2:]
    tap_time = step // 2

    @pl.when(step == 0)
    def _():
        for side in range(2):
            sources = [corner.at[0, side], corner.at[1, side]]
            sources += [(up01, dn01)[side].at[f, 0] for f in range(2)]
            sources += [(up23, dn23)[side].at[f, 0] for f in range(2)]
            for n, source in enumerate(sources):

                def store(lanes, value):
                    wide[side, n, :, lanes] = value

                widen(source[...], store, width, channels)
            for f in range(2):
                acc[side, f] = edge01[f, side]
                acc[side, f + 2] = edge23[f, side]

    def tap(side):
        weight = w_ref[0, 0].reshape(3 * channels, channels)
        left = wide[side, pl.ds(tap_time, 4)].reshape(4 * width, 3 * channels)
        acc[side] += jnp.dot(left, weight, preferred_element_type=F32).reshape(4, width, channels)

    pl.when(step % 2 == 0)(lambda: tap(0))
    pl.when(step % 2 == 1)(lambda: tap(1))

    @pl.when(step == 5)
    def _():
        first = tok_b[0]
        late = tok_a[0] + tok_b[1]
        coming = tok_a[1]
        for side, i in enumerate((0, 3)):
            for f in range(4):
                main, other = project(acc[side, f], bias_ref, even_ref, odd_ref, d_ref, f, i)
                if f < 2:
                    first = first + main
                else:
                    late = late + main
                if f == 1:
                    late = late + other
                if f == 3:
                    coming = coming + other

        def fold(value):
            return (value + pltpu.roll(value, 64, 1))[:, :64]

        first = fold(first) + down_bias_ref[...]
        late = fold(late) + down_bias_ref[...]
        odd = odd_row_ref[0] == 1
        out_ref[0] = jnp.where(odd, late, first)
        out_ref[1] = jnp.where(odd, first, late)
        out_ref[2] = fold(coming)


def whole(shape):
    return pl.BlockSpec(shape, lambda s: (0,) * len(shape))


def params():
    return pltpu.CompilerParams(vmem_limit_bytes=VMEM_LIMIT, dimension_semantics=("arbitrary",))


def cost(units, width, channels):
    return pl.CostEstimate(flops=units * width * 3 * channels * channels * 2, bytes_accessed=10_000_000, transcendentals=0)


def on_device(feature, conv_weight, conv_bias, down_weight, down_bias):
    frames, height, width, channels = feature.shape
    z = down_bias.shape[0]
    n_tm, n_row = lax.axis_size("tm"), lax.axis_size("row")
    axes = ("tm", "row")

    def shifted(value, by_tm, by_row):
        pairs = [
            (t * n_row + r, (t + by_tm) * n_row + r + by_row)
            for t in range(n_tm)
            for r in range(n_row)
            if 0 <= t + by_tm < n_tm and 0 <= r + by_row < n_row
        ]
        return lax.ppermute(value, axes, pairs)

    up23 = shifted(feature[2:, height - 1 :], 0, 1)
    dn23 = shifted(feature[2:, :1], 0, -1)
    earlier = shifted(feature[2:], 1, 0)
    up01 = shifted(feature[:2, height - 1 :], 0, 1)
    dn01 = shifted(feature[:2, :1], 0, -1)
    corner = shifted(jnp.concatenate([up23, dn23], axis=1), 1, 0)

    spread = jnp.broadcast_to(
        down_weight.transpose(0, 1, 3, 2, 4)[:, :, :, :, None, :], (3, 2, channels, 2, 4, z)
    ).reshape(3, 2, channels, 8 * z)
    even = spread[1]
    odd = jnp.concatenate([spread[2], spread[0]], axis=-1)
    bias = conv_bias.reshape(1, channels)
    patch_bias = jnp.tile(down_bias, 4).reshape(1, 4 * z)
    quarter = width // 4
    lanes = 8 * z
    tok = jax.ShapeDtypeStruct((2, quarter, lanes), F32)
    edges = jax.ShapeDtypeStruct((2, 2, width, channels), F32)
    early_shape = jax.ShapeDtypeStruct((2, height, width, channels), F32)

    def weight_spec(where):
        return pl.BlockSpec((1, 1, 3, channels, channels), lambda s: where(s) + (0, 0, 0))

    small = [whole((1, channels)), whole((2, channels, lanes)), whole((2, channels, 2 * lanes))]
    early, edge23, tok_a = pl.pallas_call(
        own_kernel,
        grid=(9,),
        in_specs=[whole(feature.shape), weight_spec(lambda s: (2 - s // 3, (1 + 2 * (s % 3)) % 3)), *small],
        out_specs=[whole(early_shape.shape), whole(edges.shape), whole(tok.shape)],
        out_shape=[early_shape, edges, tok],
        scratch_shapes=[
            pltpu.VMEM((frames, height, width, channels), F32),
            pltpu.VMEM((frames, height, width, 3 * channels), BF16),
            pltpu.VMEM((2, width, 128), F32),
        ],
        compiler_params=params(),
        cost_estimate=cost(90, width, channels),
        name="own",
    )(feature, conv_weight, bias, even, odd)
    edge01, tok_b = pl.pallas_call(
        earlier_kernel,
        grid=(6,),
        in_specs=[
            whole(earlier.shape), whole(early_shape.shape),
            weight_spec(lambda s: (s // 3, (1 + 2 * (s % 3)) % 3)), *small,
        ],
        out_specs=[whole(edges.shape), whole(tok.shape)],
        out_shape=[edges, tok],
        scratch_shapes=[
            pltpu.VMEM((2, height, width, channels), F32),
            pltpu.VMEM((2, height, width, 3 * channels), BF16),
            pltpu.VMEM((2, width, 128), F32),
        ],
        compiler_params=params(),
        cost_estimate=cost(30, width, channels),
        name="earlier",
    )(earlier, early, conv_weight, bias, even, odd)
    row = lax.axis_index("row")
    odd_row = (row % 2).reshape(1).astype(jnp.int32)
    halo = (2, 1, width, channels)
    out = pl.pallas_call(
        edge_kernel,
        grid=(6,),
        in_specs=[
            pl.BlockSpec(memory_space=pltpu.SMEM),
            whole(halo), whole(halo), whole(halo), whole(halo), whole(corner.shape),
            whole(edges.shape), whole(edges.shape), whole(tok.shape), whole(tok.shape),
            weight_spec(lambda s: (s // 2, 2 * (s % 2))), *small, whole((1, 4 * z)),
        ],
        out_specs=whole((3, quarter, 4 * z)),
        out_shape=jax.ShapeDtypeStruct((3, quarter, 4 * z), F32),
        scratch_shapes=[
            pltpu.VMEM((2, frames, width, channels), F32),
            pltpu.VMEM((2, frames + 2, width, 3 * channels), BF16),
            pltpu.VMEM((2, width, 128), F32),
        ],
        compiler_params=params(),
        cost_estimate=cost(24, width, channels),
        name="edges",
    )(odd_row, up23, dn23, up01, dn01, corner, edge01, edge23, tok_a, tok_b, conv_weight, bias, even, odd, patch_bias)

    half = n_row // 2

    def routed(value, by_tm, slot, rows):
        pairs = []
        for t in range(n_tm - by_tm):
            for r in rows:
                first = (r % 2 == 0) == (slot == 0)
                target = r // 2 if by_tm or first else half + r // 2
                pairs.append((t * n_row + r, (t + by_tm) * n_row + target))
        return lax.ppermute(value, axes, pairs)

    got_a = routed(out[0], 0, 0, range(n_row))
    got_b = routed(out[1], 0, 1, range(n_row))
    prev_even = routed(out[2], 1, 0, range(0, n_row, 2))
    prev_odd = routed(out[2], 1, 0, range(1, n_row, 2))
    low = row < half
    return jnp.concatenate(
        [jnp.where(low, got_a, got_b) + prev_even, jnp.where(low, got_b, got_a) + prev_odd], axis=0
    )


def solution(mesh):
    return jax.shard_map(
        on_device,
        mesh=mesh,
        in_specs=(P("tm", "row", None, None), P(), P(), P(), P()),
        out_specs=P(("tm", "row"), None),
        check_vma=False,
    )
```

time: 131 us -> 92.8 us (0.71)
  the two profiles are of different devices: /device:TPU:8 before, /device:TPU:1 now
where the time goes in v1:
time: 92.8 us; the launch traced here: 92.3 us
  Pallas kernels  41.4 us (45%)
  starting transfers between devices  28.4 us (31%)
  waiting for transfers between devices  13.9 us (15%)
  local copies, waits for them, and re-layouts  6.95 us (7%)
  other arithmetic  1.46 us (2%)
    pallas_call x1, Pallas kernels, on_device(): pl.pallas_call(own_kernel, grid=(9,), in_specs=[whole(feature.shape), wei...  22.9 us
    ppermute x6, starting transfers between devices, shifted(): return lax.ppermute(value, axes, pairs)  19.6 us
    pallas_call x1, Pallas kernels, on_device(): pl.pallas_call(earlier_kernel, grid=(6,), in_specs=[whole(earlier.shape),...  9.95 us
    ppermute x4, starting transfers between devices, routed(): return lax.ppermute(value, axes, pairs)  8.81 us
    ppermute x6, waiting for transfers between devices, shifted(): return lax.ppermute(value, axes, pairs)  8.61 us
    pallas_call x1, Pallas kernels, on_device(): pl.pallas_call(edge_kernel, grid=(6,), in_specs=[pl.BlockSpec(memory_spac...  8.47 us
    ppermute x4, waiting for transfers between devices, routed(): return lax.ppermute(value, axes, pairs)  5.25 us
    unnamed x16, local copies, waits for them, and re-layouts  3.2 us
  transfers between devices with their start and end apart: 10, of which 4 were waited for; matrix products, arithmetic and copies ran while one was open for 3% of the time, Pallas kernels for 36%

profile of v1, /device:TPU:1, one launch (start us, length us, event | category | flops | bytes accessed | tf_op | source)
XLA Modules:
  0.0 92.3 jit_solution(583450015785969514)
XLA Ops:
  0.0 2.2 %slice.50 = bf16[2,4,128,384]{3,2,1,0:T(8,128)(2,1)} slice(bf16[4,4,128,384]{3,2,1,0:T(8,128)(2,1)} %x_ref.1), slice={[2:4], [0:4], [0:128], [0:384]} | slice | bytes 1572864 | tf_op jit(solution)/shard_map/slice | solution.py:244
  2.2 4.6 %collective-permute-start.5 = (bf16[2,4,128,384]{3,2,1,0:T(8,128)(2,1)}, bf16[2,4,128,384]{3,2,1,0:T(8,128)(2,1)}, u32[]{:S(2)}, u32[]{:S(2)}) collective-permute-start(bf16[2,4,128,384]{3,2,1,0:T(8,128)(2,1)} %slice.50), channel_id=1, source_target_pairs={{0,8},{1,9},{2,10},{3,11},{4,12},{5,13},{6,14},{7,15},{8,16},{9,17... | collective-permute-start | bytes 2359304 | tf_op jit(solution)/shard_map/ppermute | solution.py:240
  6.9 0.8 fusion
  7.7 4.8 %collective-permute-start = (bf16[2,1,128,384]{3,2,1,0:T(8,128)(2,1)S(1)}, bf16[2,1,128,384]{3,2,1,0:T(8,128)(2,1)S(1)}, u32[]{:S(2)}, u32[]{:S(2)}) collective-permute-start(bf16[2,1,128,384]{3,2,1,0:T(8,128)(2,1)S(1)} %get-tuple-element.18), channel_id=1, source_target_pairs={{0,1},{1,2},{2,3},{3,4},{4,5},{5,6},{6,7},{8,9},{9,10},{10,11},{11... | collective-permute-start | bytes 589832 | tf_op jit(solution)/shard_map/ppermute | solution.py:240
  12.6 1.3 %collective-permute-start.1 = (bf16[2,1,128,384]{3,2,1,0:T(8,128)(2,1)S(1)}, bf16[2,1,128,384]{3,2,1,0:T(8,128)(2,1)S(1)}, u32[]{:S(2)}, u32[]{:S(2)}) collective-permute-start(bf16[2,1,128,384]{3,2,1,0:T(8,128)(2,1)S(1)} %get-tuple-element.17), channel_id=1, source_target_pairs={{1,0},{2,1},{3,2},{4,3},{5,4},{6,5},{7,6},{9,8},{10,9},{11,10},{12... | collective-permute-start | bytes 589832 | tf_op jit(solution)/shard_map/ppermute | solution.py:240
  13.9 5.5 %collective-permute-start.2 = (bf16[2,1,128,384]{3,2,1,0:T(8,128)(2,1)}, bf16[2,1,128,384]{3,2,1,0:T(8,128)(2,1)S(1)}, u32[]{:S(2)}, u32[]{:S(2)}) collective-permute-start(bf16[2,1,128,384]{3,2,1,0:T(8,128)(2,1)} %get-tuple-element.16), channel_id=1, source_target_pairs={{0,1},{1,2},{2,3},{3,4},{4,5},{5,6},{6,7},{8,9},{9,10},{10,11},{11... | collective-permute-start | bytes 589832 | tf_op jit(solution)/shard_map/ppermute | solution.py:240
  19.4 1.3 %collective-permute-start.3 = (bf16[2,1,128,384]{3,2,1,0:T(8,128)(2,1)}, bf16[2,1,128,384]{3,2,1,0:T(8,128)(2,1)}, u32[]{:S(2)}, u32[]{:S(2)}) collective-permute-start(bf16[2,1,128,384]{3,2,1,0:T(8,128)(2,1)} %get-tuple-element.15), channel_id=1, source_target_pairs={{1,0},{2,1},{3,2},{4,3},{5,4},{6,5},{7,6},{9,8},{10,9},{11,10},{12... | collective-permute-start | bytes 589832 | tf_op jit(solution)/shard_map/ppermute | solution.py:240
  20.7 0.2 copy.10
  20.9 0.2 copy.9
  21.1 0.2 copy.11.even_ref
  21.4 1.0 %collective-permute-done.up23 = bf16[2,1,128,384]{3,2,1,0:T(8,128)(2,1)S(1)} collective-permute-done((bf16[2,1,128,384]{3,2,1,0:T(8,128)(2,1)S(1)}, bf16[2,1,128,384]{3,2,1,0:T(8,128)(2,1)S(1)}, u32[]{:S(2)}, u32[]{:S(2)}) %collective-permute-start) | collective-permute-done | bytes 196640 | tf_op jit(solution)/shard_map/ppermute | solution.py:240
  22.4 7.6 %collective-permute-done.1.dn23 = bf16[2,1,128,384]{3,2,1,0:T(8,128)(2,1)S(1)} collective-permute-done((bf16[2,1,128,384]{3,2,1,0:T(8,128)(2,1)S(1)}, bf16[2,1,128,384]{3,2,1,0:T(8,128)(2,1)S(1)}, u32[]{:S(2)}, u32[]{:S(2)}) %collective-permute-start.1) | collective-permute-done | bytes 196640 | tf_op jit(solution)/shard_map/ppermute | solution.py:240
  30.0 0.8 pad_maximum_fusion
  30.8 2.0 %collective-permute-start.4 = (bf16[2,2,128,384]{3,2,1,0:T(8,128)(2,1)}, bf16[2,2,128,384]{3,2,1,0:T(8,128)(2,1)}, u32[]{:S(2)}, u32[]{:S(2)}) collective-permute-start(bf16[2,2,128,384]{3,2,1,0:T(8,128)(2,1)} %pad_maximum_fusion), channel_id=1, source_target_pairs={{0,8},{1,9},{2,10},{3,11},{4,12},{5,13},{6,14},{7,15},{8,16},{9,17... | collective-permute-start | bytes 1179656 | tf_op jit(solution)/shard_map/ppermute | solution.py:240
  32.8 22.9 %own.1 = (f32[2,4,128,384]{3,2,1,0:T(8,128)S(1)}, f32[2,2,128,384]{3,2,1,0:T(8,128)S(1)}, f32[2,32,128]{2,1,0:T(8,128)S(1)}) custom-call(bf16[4,4,128,384]{3,2,1,0:T(8,128)(2,1)S(1)} %copy-done, bf16[3,3,3,384,384]{4,3,2,1,0:T(8,128)(2,1)} %w_ref.5, f32[1,384]{1,0:T(1,128)S(1)} %reshape.22.bias_ref, bf16[2,384,128]{2,1,0:T(8,128)(2,1)S(1)} %copy.11.even_ref, ...), custom_call_target="tpu_custom_call" | custom-call | flops 10192158720 | bytes 10000000 | tf_op jit(solution)/shard_map/own/pallas_call | solution.py:266
  55.8 0.0 copy-start.1
  55.8 0.6 copy-done.1
  56.4 1.2 %copy-done.3 = f32[2,4,128,384]{3,2,1,0:T(8,128)} copy-done((f32[2,4,128,384]{3,2,1,0:T(8,128)}, f32[2,4,128,384]{3,2,1,0:T(8,128)S(1)}, u32[]{:S(2)}) %copy-start.3) | copy-done | bytes 1572888
  57.5 0.1 reshape_tile.3.down_bias_ref
  57.6 0.0 collective-permute-done.5.x_ref
  57.6 1.4 %copy-done.4 = f32[2,4,128,384]{3,2,1,0:T(8,128)S(1)} copy-done((f32[2,4,128,384]{3,2,1,0:T(8,128)S(1)}, f32[2,4,128,384]{3,2,1,0:T(8,128)}, u32[]{:S(2)}) %copy-start.4) | copy-done | bytes 1572888
  59.0 10.0 %earlier.1 = (f32[2,2,128,384]{3,2,1,0:T(8,128)S(1)}, f32[2,32,128]{2,1,0:T(8,128)S(1)}) custom-call(bf16[2,4,128,384]{3,2,1,0:T(8,128)(2,1)} %collective-permute-done.5.x_ref, f32[2,4,128,384]{3,2,1,0:T(8,128)S(1)} %copy-done.4, bf16[3,3,3,384,384]{4,3,2,1,0:T(8,128)(2,1)} %w_ref.5, f32[1,384]{1,0:T(1,128)S(1)} %reshape.22.bias_ref, ...), custom_call_target="tpu_custom_call" | custom-call | flops 3397386240 | bytes 10000000 | tf_op jit(solution)/shard_map/earlier/pallas_call | solution.py:281
  69.0 0.0 collective-permute-done.2.up01
  69.0 0.0 collective-permute-done.4.corner
  69.0 8.5 %edges.1 = f32[3,32,64]{2,1,0:T(8,128)S(1)} custom-call(s32[1]{0:T(128)} %bitcast.odd_row_ref, bf16[2,1,128,384]{3,2,1,0:T(8,128)(2,1)S(1)} %collective-permute-done.up23, bf16[2,1,128,384]{3,2,1,0:T(8,128)(2,1)S(1)} %collective-permute-done.1.dn23, bf16[2,1,128,384]{3,2,1,0:T(8,128)(2,1)S(1)} %collective-permute-done.2.up01, ...), custom_call_target="tpu_custom_call" | custom-call | flops 2717908992 | bytes 10000000 | tf_op jit(solution)/shard_map/edges/pallas_call | solution.py:302
  77.5 0.7 collective-permute-start.6
  78.2 4.9 %collective-permute-start.7 = (f32[32,64]{1,0:T(8,128)S(1)}, f32[32,64]{1,0:T(8,128)S(1)}, u32[]{:S(2)}, u32[]{:S(2)}) collective-permute-start(f32[32,64]{1,0:T(8,128)S(1)} %get-tuple-element.24), channel_id=1, source_target_pairs={{0,4},{1,0},{2,5},{3,1},{4,6},{5,2},{6,7},{7,3},{8,12},{9,8},{10,1... | collective-permute-start | bytes 24584 | tf_op jit(solution)/shard_map/ppermute | solution.py:332
  83.2 1.9 %collective-permute-start.8 = (f32[32,64]{1,0:T(8,128)S(1)}, f32[32,64]{1,0:T(8,128)S(1)}, u32[]{:S(2)}, u32[]{:S(2)}) collective-permute-start(f32[32,64]{1,0:T(8,128)S(1)} %get-tuple-element.23), channel_id=1, source_target_pairs={{0,8},{2,9},{4,10},{6,11},{8,16},{10,17},{12,18},{14,19},{16,24},{... | collective-permute-start | bytes 24584 | tf_op jit(solution)/shard_map/ppermute | solution.py:332
  85.1 1.3 %collective-permute-start.9 = (f32[32,64]{1,0:T(8,128)S(1)}, f32[32,64]{1,0:T(8,128)S(1)}, u32[]{:S(2)}, u32[]{:S(2)}) collective-permute-start(f32[32,64]{1,0:T(8,128)S(1)} %get-tuple-element.23), channel_id=1, source_target_pairs={{1,8},{3,9},{5,10},{7,11},{9,16},{11,17},{13,18},{15,19},{17,24},{... | collective-permute-start | bytes 24584 | tf_op jit(solution)/shard_map/ppermute | solution.py:332
  86.4 0.6 collective-permute-done.7
  87.0 4.6 %collective-permute-done.9 = f32[32,64]{1,0:T(8,128)S(1)} collective-permute-done((f32[32,64]{1,0:T(8,128)S(1)}, f32[32,64]{1,0:T(8,128)S(1)}, u32[]{:S(2)}, u32[]{:S(2)}) %collective-permute-start.9) | collective-permute-done | bytes 8224 | tf_op jit(solution)/shard_map/ppermute | solution.py:332
  91.6 0.6 pad_maximum_fusion.2
  (24 shorter events, 0.2 us)
Async XLA Ops:
  0.0 6.9 %copy-start = (bf16[4,4,128,384]{3,2,1,0:T(8,128)(2,1)S(1)}, bf16[4,4,128,384]{3,2,1,0:T(8,128)(2,1)}, u32[]{:S(2)}) copy-start(bf16[4,4,128,384]{3,2,1,0:T(8,128)(2,1)} %x_ref.1) | copy-start | bytes 4718596
  0.0 20.7 %copy-start.5 = (bf16[3,2,2,384,16]{3,4,2,1,0:T(8,128)(2,1)S(1)}, bf16[3,2,2,384,16]{3,4,2,1,0:T(8,128)(2,1)}, u32[]{:S(2)}) copy-start(bf16[3,2,2,384,16]{3,4,2,1,0:T(8,128)(2,1)} %param.8) | copy-start | bytes 442372
  2.2 19.1 %copy-start.6 = (f32[384]{0:T(512)S(1)}, f32[384]{0:T(512)}, u32[]{:S(2)}) copy-start(f32[384]{0:T(512)} %param.7) | copy-start | bytes 4612
  2.2 55.4 %collective-permute-start.5 = (bf16[2,4,128,384]{3,2,1,0:T(8,128)(2,1)}, bf16[2,4,128,384]{3,2,1,0:T(8,128)(2,1)}, u32[]{:S(2)}, u32[]{:S(2)}) collective-permute-start(bf16[2,4,128,384]{3,2,1,0:T(8,128)(2,1)} %slice.50), channel_id=1, source_target_pairs={{0,8},{1,9},{2,10},{3,11},{4,12},{5,13},{6,14},{7,15},{8,16},{9,17... | collective-permute-start | bytes 2359304 | tf_op jit(solution)/shard_map/ppermute | solution.py:240
  7.7 14.7 %collective-permute-start = (bf16[2,1,128,384]{3,2,1,0:T(8,128)(2,1)S(1)}, bf16[2,1,128,384]{3,2,1,0:T(8,128)(2,1)S(1)}, u32[]{:S(2)}, u32[]{:S(2)}) collective-permute-start(bf16[2,1,128,384]{3,2,1,0:T(8,128)(2,1)S(1)} %get-tuple-element.18), channel_id=1, source_target_pairs={{0,1},{1,2},{2,3},{3,4},{4,5},{5,6},{6,7},{8,9},{9,10},{10,11},{11... | collective-permute-start | bytes 589832 | tf_op jit(solution)/shard_map/ppermute | solution.py:240
  12.6 17.4 %collective-permute-start.1 = (bf16[2,1,128,384]{3,2,1,0:T(8,128)(2,1)S(1)}, bf16[2,1,128,384]{3,2,1,0:T(8,128)(2,1)S(1)}, u32[]{:S(2)}, u32[]{:S(2)}) collective-permute-start(bf16[2,1,128,384]{3,2,1,0:T(8,128)(2,1)S(1)} %get-tuple-element.17), channel_id=1, source_target_pairs={{1,0},{2,1},{3,2},{4,3},{5,4},{6,5},{7,6},{9,8},{10,9},{11,10},{12... | collective-permute-start | bytes 589832 | tf_op jit(solution)/shard_map/ppermute | solution.py:240
  13.9 55.2 %collective-permute-start.2 = (bf16[2,1,128,384]{3,2,1,0:T(8,128)(2,1)}, bf16[2,1,128,384]{3,2,1,0:T(8,128)(2,1)S(1)}, u32[]{:S(2)}, u32[]{:S(2)}) collective-permute-start(bf16[2,1,128,384]{3,2,1,0:T(8,128)(2,1)} %get-tuple-element.16), channel_id=1, source_target_pairs={{0,1},{1,2},{2,3},{3,4},{4,5},{5,6},{6,7},{8,9},{9,10},{10,11},{11... | collective-permute-start | bytes 589832 | tf_op jit(solution)/shard_map/ppermute | solution.py:240
  19.4 49.7 %collective-permute-start.3 = (bf16[2,1,128,384]{3,2,1,0:T(8,128)(2,1)}, bf16[2,1,128,384]{3,2,1,0:T(8,128)(2,1)}, u32[]{:S(2)}, u32[]{:S(2)}) collective-permute-start(bf16[2,1,128,384]{3,2,1,0:T(8,128)(2,1)} %get-tuple-element.15), channel_id=1, source_target_pairs={{1,0},{2,1},{3,2},{4,3},{5,4},{6,5},{7,6},{9,8},{10,9},{11,10},{12... | collective-permute-start | bytes 589832 | tf_op jit(solution)/shard_map/ppermute | solution.py:240
  30.8 26.8 %copy-start.7 = (f32[16]{0:T(128)S(1)}, f32[16]{0:T(128)}, u32[]{:S(2)}) copy-start(f32[16]{0:T(128)} %param.9) | copy-start | bytes 196
  30.8 38.3 %collective-permute-start.4 = (bf16[2,2,128,384]{3,2,1,0:T(8,128)(2,1)}, bf16[2,2,128,384]{3,2,1,0:T(8,128)(2,1)}, u32[]{:S(2)}, u32[]{:S(2)}) collective-permute-start(bf16[2,2,128,384]{3,2,1,0:T(8,128)(2,1)} %pad_maximum_fusion), channel_id=1, source_target_pairs={{0,8},{1,9},{2,10},{3,11},{4,12},{5,13},{6,14},{7,15},{8,16},{9,17... | collective-permute-start | bytes 1179656 | tf_op jit(solution)/shard_map/ppermute | solution.py:240
  55.8 0.6 copy-start.1
  56.4 1.2 %copy-start.3 = (f32[2,4,128,384]{3,2,1,0:T(8,128)}, f32[2,4,128,384]{3,2,1,0:T(8,128)S(1)}, u32[]{:S(2)}) copy-start(f32[2,4,128,384]{3,2,1,0:T(8,128)S(1)} %get-tuple-element.10.early_in) | copy-start | bytes 4718596
  57.6 1.4 %copy-start.4 = (f32[2,4,128,384]{3,2,1,0:T(8,128)S(1)}, f32[2,4,128,384]{3,2,1,0:T(8,128)}, u32[]{:S(2)}) copy-start(f32[2,4,128,384]{3,2,1,0:T(8,128)} %copy-done.3) | copy-start | bytes 4718596
  59.0 10.0 %copy-start.2 = (f32[2,32,128]{2,1,0:T(8,128)S(1)}, f32[2,32,128]{2,1,0:T(8,128)}, u32[]{:S(2)}) copy-start(f32[2,32,128]{2,1,0:T(8,128)} %copy-done.1) | copy-start | bytes 98308
  77.5 8.8 %collective-permute-start.6 = (f32[32,64]{1,0:T(8,128)S(1)}, f32[32,64]{1,0:T(8,128)S(1)}, u32[]{:S(2)}, u32[]{:S(2)}) collective-permute-start(f32[32,64]{1,0:T(8,128)S(1)} %get-tuple-element.22), channel_id=1, source_target_pairs={{0,0},{1,4},{2,1},{3,5},{4,2},{5,6},{6,3},{7,7},{8,8},{9,12},{10,9... | collective-permute-start | bytes 24584 | tf_op jit(solution)/shard_map/ppermute | solution.py:332
  78.2 8.8 %collective-permute-start.7 = (f32[32,64]{1,0:T(8,128)S(1)}, f32[32,64]{1,0:T(8,128)S(1)}, u32[]{:S(2)}, u32[]{:S(2)}) collective-permute-start(f32[32,64]{1,0:T(8,128)S(1)} %get-tuple-element.24), channel_id=1, source_target_pairs={{0,4},{1,0},{2,5},{3,1},{4,6},{5,2},{6,7},{7,3},{8,12},{9,8},{10,1... | collective-permute-start | bytes 24584 | tf_op jit(solution)/shard_map/ppermute | solution.py:332
  83.2 3.9 %collective-permute-start.8 = (f32[32,64]{1,0:T(8,128)S(1)}, f32[32,64]{1,0:T(8,128)S(1)}, u32[]{:S(2)}, u32[]{:S(2)}) collective-permute-start(f32[32,64]{1,0:T(8,128)S(1)} %get-tuple-element.23), channel_id=1, source_target_pairs={{0,8},{2,9},{4,10},{6,11},{8,16},{10,17},{12,18},{14,19},{16,24},{... | collective-permute-start | bytes 24584 | tf_op jit(solution)/shard_map/ppermute | solution.py:332
  85.1 6.6 %collective-permute-start.9 = (f32[32,64]{1,0:T(8,128)S(1)}, f32[32,64]{1,0:T(8,128)S(1)}, u32[]{:S(2)}, u32[]{:S(2)}) collective-permute-start(f32[32,64]{1,0:T(8,128)S(1)} %get-tuple-element.23), channel_id=1, source_target_pairs={{1,8},{3,9},{5,10},{7,11},{9,16},{11,17},{13,18},{15,19},{17,24},{... | collective-permute-start | bytes 24584 | tf_op jit(solution)/shard_map/ppermute | solution.py:332

commit v2 on v0

v2 whole, which is shorter than its diff:
```python
import jax
import jax.numpy as jnp
from jax import lax
from jax.experimental import pallas as pl
from jax.experimental.pallas import tpu as pltpu
from jax.sharding import PartitionSpec as P

F32 = jnp.float32
BF16 = jnp.bfloat16
VMEM_LIMIT = 28 * 1024 * 1024
AXES = ("tm", "row")


def widen(rows, target, keep=None):
    width, channels = rows.shape
    if keep is not None:
        rows = jnp.where(keep, rows.astype(F32), 0.0).astype(BF16)
    value = rows.astype(F32)
    column = lax.broadcasted_iota(jnp.int32, (width, channels), 0)
    before = jnp.where(column == 0, 0.0, pltpu.roll(value, 1, 0))
    after = jnp.where(column == width - 1, 0.0, pltpu.roll(value, width - 1, 0))
    target[:, 0:channels] = before.astype(BF16)
    target[:, channels : 2 * channels] = rows
    target[:, 2 * channels : 3 * channels] = after.astype(BF16)


def tap_product(w_ref, positions):
    channels = w_ref.shape[-1]
    weight = w_ref[0, 0].reshape(3 * channels, channels)
    positions = positions.reshape(-1, 3 * channels)
    return lax.dot_general(weight, positions, (((0,), (1,)), ((), ())), preferred_element_type=F32)


def projected(pre, bias, down_ref, f, rows):
    taps = (1,) if f % 2 == 0 else (2, 0)
    act = []
    for value in pre:
        value = value + bias
        act.append((value / (1.0 + jnp.exp(-value))).astype(BF16))
    weight = []
    for a in taps:
        for i in rows:
            parts = [down_ref[a, i % 2, dx] for dx in (0, 0, 1, 1)]
            weight.append(jnp.concatenate(parts, axis=0))
    product = jnp.dot(jnp.concatenate(weight, axis=0), jnp.concatenate(act, axis=1), preferred_element_type=F32)
    width = pre[0].shape[1]
    size = weight[0].shape[0]
    found = {}
    for n, a in enumerate(taps):
        for half in range(2):
            first = (2 * n + half) * size
            found[a, half] = product[first : first + size, half * width : (half + 1) * width]
    return found


def add_products(found, a, total_ref):
    for half in range(2):
        value = found[a, half]
        size = value.shape[0] // 2
        for dx in range(2):
            first = dx * 2 * size + half * size
            total_ref[first : first + size, :] += value[dx * size : (dx + 1) * size]


def fold(total, d_ref):
    d_ref[...] = total.T
    lanes = total.shape[0]
    count = total.shape[1] // 4
    lane = lax.broadcasted_iota(jnp.int32, (count, lanes), 1)
    result = jnp.zeros((count, lanes), F32)
    for s in range(4):
        keep = (lane // (lanes // 2) == s % 2) & ((lane // (lanes // 8)) % 2 == s // 2)
        result = result + jnp.where(keep, d_ref[pl.ds(s, count, stride=4), :], 0.0)
    return (result + pltpu.roll(result, lanes // 2, 1))[:, : lanes // 2]


def bias_columns(bias_ref, width):
    return jnp.broadcast_to(bias_ref[...], (width, bias_ref.shape[1])).T


def own_kernel(x_ref, w_ref, bias_ref, down_ref, early_ref, edge_ref, total_ref, acc, wide):
    step = pl.program_id(0)
    frames, height, width, channels = x_ref.shape

    @pl.when(step == 0)
    def _():
        def one(n, carry):
            f, h = n // height, n % height
            widen(x_ref[f, h], wide.at[h, f])
            return carry

        lax.fori_loop(0, frames * height, one, 0)

    def tap(n):
        tap_time, tap_row = 2 - n // 3, (1 + 2 * (n % 3)) % 3
        count = frames - 2 + tap_time
        rows = range(max(0, tap_row - 1), min(height, height + tap_row - 1))
        product = tap_product(w_ref, wide[rows[0] : rows[-1] + 1, :count])
        for m, h in enumerate(rows):
            for g in range(count):
                first = (m * count + g) * width
                value = product[:, first : first + width]
                target = (h + 1 - tap_row, g + 2 - tap_time)
                if n == 0:
                    acc[target] = value
                else:
                    acc[target] += value

    for n in range(9):
        pl.when(step == n)(lambda n=n: tap(n))

    @pl.when(step == 8)
    def _():
        early_ref[...] = acc[:, :2]
        for side, i in enumerate((0, height - 1)):
            for f in (2, 3):
                edge_ref[side, f - 2] = acc[i, f]
        bias = bias_columns(bias_ref, width)
        total_ref[...] = jnp.zeros_like(total_ref)
        for f in (2, 3):
            found = projected([acc[1, f], acc[2, f]], bias, down_ref, f, (1, 2))
            add_products(found, 2 - (f + 1) % 2, total_ref.at[0])
            if f == 3:
                add_products(found, 0, total_ref.at[1])


def earlier_kernel(flag_ref, x_ref, early_in, w_ref, bias_ref, down_ref, edge_ref, total_ref, acc, wide):
    step = pl.program_id(0)
    frames, height, width, channels = x_ref.shape

    @pl.when(step == 0)
    def _():
        keep = flag_ref[2] == 1

        def one(n, carry):
            f, h = n // height, n % height
            widen(x_ref[f, h], wide.at[h, f], keep)
            return carry

        lax.fori_loop(0, frames * height, one, 0)

    def tap(n):
        tap_time, tap_row = n // 3, (1 + 2 * (n % 3)) % 3
        rows = range(max(0, tap_row - 1), min(height, height + tap_row - 1))
        count = frames - tap_time
        product = tap_product(w_ref, wide[rows[0] : rows[-1] + 1, tap_time:])
        for m, h in enumerate(rows):
            for f in range(count):
                first = (m * count + f) * width
                value = product[:, first : first + width]
                target = (h + 1 - tap_row, f)
                if n == 0:
                    acc[target] = early_in[target] + value
                else:
                    acc[target] += value

    for n in range(6):
        pl.when(step == n)(lambda n=n: tap(n))

    @pl.when(step == 5)
    def _():
        for side, i in enumerate((0, height - 1)):
            for f in (0, 1):
                edge_ref[side, f] = acc[i, f]
        bias = bias_columns(bias_ref, width)
        total_ref[...] = jnp.zeros_like(total_ref)
        for f in (0, 1):
            found = projected([acc[1, f], acc[2, f]], bias, down_ref, f, (1, 2))
            add_products(found, 2 - (f + 1) % 2, total_ref.at[0])
            if f == 1:
                add_products(found, 0, total_ref.at[1])


def edge_taps(sources, edge_in, w_ref, acc, wide):
    step = pl.program_id(0)

    @pl.when(step == 0)
    def _():
        for side in range(2):
            for n, (source, keep) in enumerate(sources[side]):
                widen(source[...], wide.at[side, n], keep)

    def tap(n):
        tap_time, side = n // 2, n % 2
        product = tap_product(w_ref, wide[side, tap_time : tap_time + 2])
        width = product.shape[1] // 2
        for f in range(2):
            value = product[:, f * width : (f + 1) * width]
            if tap_time == 0:
                acc[side, f] = edge_in[side, f] + value
            else:
                acc[side, f] += value

    for n in range(6):
        pl.when(step == n)(lambda n=n: tap(n))


def late_edge_kernel(flag_ref, up, dn, edge_in, total_in, w_ref, bias_ref, down_ref, late_ref, carry_ref, acc, wide, total, d_ref):
    flags = [flag_ref[side] == 1 for side in range(2)]
    edge_taps([[(ref.at[f, 0], flags[side]) for f in range(4)] for side, ref in enumerate((up, dn))], edge_in, w_ref, acc, wide)

    @pl.when(pl.program_id(0) == 5)
    def _():
        bias = bias_columns(bias_ref, acc.shape[-1])
        total[...] = total_in[...]
        for f in (0, 1):
            found = projected([acc[0, f], acc[1, f]], bias, down_ref, f, (0, 3))
            add_products(found, 2 - (f + 1) % 2, total.at[0])
            if f == 1:
                add_products(found, 0, total.at[1])
        late_ref[...] = total[0]
        carry_ref[...] = fold(total[1], d_ref)


def early_edge_kernel(
    flag_ref, up, dn, corner, edge_in, total_in, late_in, w_ref, bias_ref, down_ref, down_bias_ref, out_ref, acc, wide, total, d_ref
):
    flags = [flag_ref[side] == 1 for side in range(2)]
    before = [flag & (flag_ref[2] == 1) for flag in flags]
    edge_taps(
        [
            [(corner.at[f, side], before[side]) for f in range(2)] + [(ref.at[f, 0], flags[side]) for f in range(2)]
            for side, ref in enumerate((up, dn))
        ],
        edge_in, w_ref, acc, wide,
    )

    @pl.when(pl.program_id(0) == 5)
    def _():
        bias = bias_columns(bias_ref, acc.shape[-1])
        total[...] = total_in[...]
        for f in (0, 1):
            found = projected([acc[0, f], acc[1, f]], bias, down_ref, f, (0, 3))
            add_products(found, 2 - (f + 1) % 2, total.at[0])
            if f == 1:
                add_products(found, 0, total.at[1])
        out_ref[0] = fold(total[0], d_ref) + down_bias_ref[...]
        out_ref[1] = fold(total[1] + late_in[...], d_ref) + down_bias_ref[...]


def whole(shape):
    return pl.BlockSpec(tuple(shape), lambda s: (0,) * len(shape))


def on_device(feature, conv_weight, conv_bias, down_weight, down_bias):
    frames, height, width, channels = feature.shape
    z = down_bias.shape[0]
    n_tm, n_row = lax.axis_size("tm"), lax.axis_size("row")
    tm, row = lax.axis_index("tm"), lax.axis_index("row")
    quarter, lanes = width // 4, 8 * z

    def shifted(value, by_tm, by_row):
        pairs = [
            (t * n_row + r, (t + by_tm) % n_tm * n_row + (r + by_row) % n_row) for t in range(n_tm) for r in range(n_row)
        ]
        return lax.ppermute(value, AXES, pairs)

    flags = jnp.stack([row > 0, row < n_row - 1, tm > 0]).astype(jnp.int32)
    up = shifted(feature[:, height - 1 :], 0, 1)
    dn = shifted(feature[:, :1], 0, -1)
    earlier = shifted(feature[2:], 1, 0)

    bias = conv_bias.reshape(1, channels)
    down = down_weight.transpose(0, 1, 2, 4, 3)
    patch_bias = jnp.tile(down_bias, 4).reshape(1, 4 * z)
    edges = jax.ShapeDtypeStruct((2, 2, channels, width), F32)
    totals = jax.ShapeDtypeStruct((2, lanes, width), F32)
    early_shape = jax.ShapeDtypeStruct((height, 2, channels, width), F32)
    flag_spec = pl.BlockSpec(memory_space=pltpu.SMEM)

    def weights(where):
        return [
            pl.BlockSpec((1, 1, 3, channels, channels), lambda s: where(s) + (0, 0, 0)), whole(bias.shape), whole(down.shape)
        ]

    def call(kernel, name, steps, units, ins, specs, outs, scratch):
        return pl.pallas_call(
            kernel,
            grid=(steps,),
            in_specs=specs,
            out_specs=[whole(o.shape) for o in outs],
            out_shape=outs,
            scratch_shapes=scratch,
            compiler_params=pltpu.CompilerParams(vmem_limit_bytes=VMEM_LIMIT, dimension_semantics=("arbitrary",)),
            cost_estimate=pl.CostEstimate(
                flops=units * width * 6 * channels * channels, bytes_accessed=10_000_000, transcendentals=0
            ),
            name=name,
        )(*ins)

    early, edge23, total_a = call(
        own_kernel, "own", 9, 90,
        (feature, conv_weight, bias, down),
        [whole(feature.shape), *weights(lambda s: (2 - s // 3, (1 + 2 * (s % 3)) % 3))],
        [early_shape, edges, totals],
        [pltpu.VMEM((height, frames, channels, width), F32), pltpu.VMEM((height, frames, width, 3 * channels), BF16)],
    )
    edge01, total_b = call(
        earlier_kernel, "earlier", 6, 30,
        (flags, earlier, early, conv_weight, bias, down),
        [flag_spec, whole(earlier.shape), whole(early_shape.shape), *weights(lambda s: (s // 3, (1 + 2 * (s % 3)) % 3))],
        [edges, totals],
        [pltpu.VMEM((height, 2, channels, width), F32), pltpu.VMEM((height, 2, width, 3 * channels), BF16)],
    )
    up, dn, edge01, edge23 = lax.optimization_barrier((up, dn, edge01, edge23))
    corner = shifted(jnp.concatenate([up[2:], dn[2:]], axis=1), 1, 0)
    edge_scratch = [
        pltpu.VMEM((2, 2, channels, width), F32),
        pltpu.VMEM((2, 4, width, 3 * channels), BF16),
        pltpu.VMEM((2, lanes, width), F32),
        pltpu.VMEM((width, lanes), F32),
    ]
    edge_weights = weights(lambda s: (s // 2, 2 * (s % 2)))
    late, carry = call(
        late_edge_kernel, "late_edges", 6, 12,
        (flags, up, dn, edge23, total_a, conv_weight, bias, down),
        [flag_spec, whole(up.shape), whole(dn.shape), whole(edges.shape), whole(totals.shape), *edge_weights],
        [jax.ShapeDtypeStruct((lanes, width), F32), jax.ShapeDtypeStruct((quarter, 4 * z), F32)],
        edge_scratch,
    )
    carry = shifted(carry, 1, 0)
    halo_spec = whole((2, 1, width, channels))
    (out,) = call(
        early_edge_kernel, "early_edges", 6, 12,
        (flags, up, dn, corner, edge01, total_b, late, conv_weight, bias, down, patch_bias),
        [
            flag_spec, halo_spec, halo_spec, whole(corner.shape), whole(edges.shape), whole(totals.shape),
            whole(late.shape), *edge_weights, whole(patch_bias.shape),
        ],
        [jax.ShapeDtypeStruct((2, quarter, 4 * z), F32)],
        edge_scratch,
    )

    half = n_row // 2

    def routed(value, slot):
        pairs = []
        for t in range(n_tm):
            for r in range(n_row):
                target = r // 2 if (r % 2 == 0) == (slot == 0) else half + r // 2
                pairs.append((t * n_row + r, t * n_row + target))
        return lax.ppermute(value, AXES, pairs)

    first = out[0] + jnp.where(tm > 0, carry, 0.0)
    last = out[1]
    is_even = row % 2 == 0
    got_a = routed(jnp.where(is_even, first, last), 0)
    got_b = routed(jnp.where(is_even, last, first), 1)
    low = row < half
    return jnp.concatenate([jnp.where(low, got_a, got_b), jnp.where(low, got_b, got_a)], axis=0)


def solution(mesh):
    return jax.shard_map(
        on_device,
        mesh=mesh,
        in_specs=(P("tm", "row", None, None), P(), P(), P(), P()),
        out_specs=P(AXES, None),
        check_vma=False,
    )
```

time: 131 us -> 62.6 us (0.48)
  the two profiles are of different devices: /device:TPU:8 before, /device:TPU:1 now
where the time goes in v2:
time: 62.6 us; the launch traced here: 62.3 us
  Pallas kernels  32.7 us (52%)
  starting transfers between devices  13.7 us (22%)
  local copies, waits for them, and re-layouts  9.87 us (16%)
  waiting for transfers between devices  4.45 us (7%)
  other arithmetic  1.51 us (2%)
    pallas_call x4, Pallas kernels, call(): pl.pallas_call(kernel, grid=(steps,), in_specs=specs, out_specs=[whole(o....  32.7 us
    ppermute x5, starting transfers between devices, shifted(): return lax.ppermute(value, AXES, pairs)  10.6 us
    unnamed x14, local copies, waits for them, and re-layouts  6.54 us
    ppermute x2, waiting for transfers between devices, routed(): return lax.ppermute(value, AXES, pairs)  4.44 us
    ppermute x2, starting transfers between devices, routed(): return lax.ppermute(value, AXES, pairs)  3.1 us
    slice x1, local copies, waits for them, and re-layouts, on_device(): earlier = shifted(feature[2:], 1, 0)  2.23 us
  transfers between devices with their start and end apart: 7, of which 1 were waited for; matrix products, arithmetic and copies ran while one was open for 2% of the time, Pallas kernels for 52%

profile of v2, /device:TPU:1, one launch (start us, length us, event | category | flops | bytes accessed | tf_op | source)
XLA Modules:
  0.0 62.3 jit_solution(17282124886623240788)
XLA Ops:
  0.0 2.2 %slice.23 = bf16[2,4,128,384]{3,2,1,0:T(8,128)(2,1)} slice(bf16[4,4,128,384]{3,2,1,0:T(8,128)(2,1)} %x_ref.1), slice={[2:4], [0:4], [0:128], [0:384]} | slice | bytes 1572864 | tf_op jit(solution)/shard_map/slice | solution.py:261
  2.2 2.6 %collective-permute-start.2 = (bf16[2,4,128,384]{3,2,1,0:T(8,128)(2,1)}, bf16[2,4,128,384]{3,2,1,0:T(8,128)(2,1)}, u32[]{:S(2)}, u32[]{:S(2)}) collective-permute-start(bf16[2,4,128,384]{3,2,1,0:T(8,128)(2,1)} %slice.23), channel_id=1, source_target_pairs={{0,8},{1,9},{2,10},{3,11},{4,12},{5,13},{6,14},{7,15},{8,16},{9,17... | collective-permute-start | bytes 2359304 | tf_op jit(solution)/shard_map/ppermute | solution.py:256
  4.8 0.0 copy-done.3
  4.8 1.0 %fusion.3 = (bf16[4,1,128,384]{3,2,1,0:T(8,128)(2,1)}, bf16[4,1,128,384]{3,2,1,0:T(8,128)(2,1)}) fusion(bf16[4,4,128,384]{3,2,1,0:T(8,128)(2,1)S(1)} %copy-done.3), kind=kLoop, calls=%fused_computation.10 | loop fusion | bytes 1572864 | tf_op jit(solution)/shard_map/slice | solution.py:260
  5.8 2.9 %collective-permute-start = (bf16[4,1,128,384]{3,2,1,0:T(8,128)(2,1)}, bf16[4,1,128,384]{3,2,1,0:T(8,128)(2,1)S(1)}, u32[]{:S(2)}, u32[]{:S(2)}) collective-permute-start(bf16[4,1,128,384]{3,2,1,0:T(8,128)(2,1)} %get-tuple-element.28), channel_id=1, source_target_pairs={{0,1},{1,2},{2,3},{3,4},{4,5},{5,6},{6,7},{7,0},{8,9},{9,10},{10,1... | collective-permute-start | bytes 1179656 | tf_op jit(solution)/shard_map/ppermute | solution.py:256
  8.7 3.5 %collective-permute-start.1 = (bf16[4,1,128,384]{3,2,1,0:T(8,128)(2,1)}, bf16[4,1,128,384]{3,2,1,0:T(8,128)(2,1)S(1)}, u32[]{:S(2)}, u32[]{:S(2)}) collective-permute-start(bf16[4,1,128,384]{3,2,1,0:T(8,128)(2,1)} %get-tuple-element.27), channel_id=1, source_target_pairs={{0,7},{1,0},{2,1},{3,2},{4,3},{5,4},{6,5},{7,6},{8,15},{9,8},{10,9... | collective-permute-start | bytes 1179656 | tf_op jit(solution)/shard_map/ppermute | solution.py:256
  12.2 0.0 copy-done.5
  12.2 0.0 copy-done.4
  12.2 3.3 %copy-done = bf16[3,3,3,384,384]{4,3,2,1,0:T(8,128)(2,1)S(1)} copy-done((bf16[3,3,3,384,384]{4,3,2,1,0:T(8,128)(2,1)S(1)}, bf16[3,3,3,384,384]{4,3,2,1,0:T(8,128)(2,1)}, u32[]{:S(2)}) %copy-start) | copy-done | bytes 7962648
  15.5 15.4 %own.1 = (f32[4,2,384,128]{3,2,1,0:T(8,128)S(1)}, f32[2,2,384,128]{3,2,1,0:T(8,128)S(1)}, f32[2,128,128]{2,1,0:T(8,128)S(1)}) custom-call(bf16[4,4,128,384]{3,2,1,0:T(8,128)(2,1)S(1)} %copy-done.3, bf16[3,3,3,384,384]{4,3,2,1,0:T(8,128)(2,1)S(1)} %copy-done, f32[1,384]{1,0:T(1,128)S(1)} %reshape.4.bias_ref, bf16[3,2,2,16,384]{4,3,2,1,0:T(8,128)(2,1)S(1)} %bitcast.18), custom_call_target="tpu_custom_call" | custom-call | flops 10192158720 | bytes 10000000 | tf_op jit(solution)/shard_map/own/pallas_call | solution.py:277
  30.9 0.1 add_convert_fusion.flag_ref
  31.0 0.0 collective-permute-done.2.x_ref
  31.0 0.0 copy-done.1
  31.0 8.0 %earlier.1 = (f32[2,2,384,128]{3,2,1,0:T(8,128)S(1)}, f32[2,128,128]{2,1,0:T(8,128)S(1)}) custom-call(s32[3]{0:T(128)S(1)} %add_convert_fusion.flag_ref, bf16[2,4,128,384]{3,2,1,0:T(8,128)(2,1)} %collective-permute-done.2.x_ref, f32[4,2,384,128]{3,2,1,0:T(8,128)S(1)} %get-tuple-element.16.early_in, bf16[3,3,3,384,384]{4,3,2,1,0:T(8,128)(2,1)S(1)} %copy-done.1, ...), custom_call_target="tpu_custom_call" | custom-call | flops 3397386240 | bytes 10000000 | tf_op jit(solution)/shard_map/earlier/pallas_call | solution.py:277
  39.0 0.0 copy-start.6
  39.0 0.0 collective-permute-done.up
  39.0 0.0 collective-permute-done.1.dn
  39.1 0.8 %pad_maximum_fusion = bf16[2,2,128,384]{3,2,1,0:T(8,128)(2,1)} fusion(bf16[2,1,128,384]{3,2,1,0:T(8,128)(2,1)S(1)} %slice.25, bf16[2,1,128,384]{3,2,1,0:T(8,128)(2,1)S(1)} %slice.24), kind=kLoop, calls=%fused_computation | loop fusion | flops 196608 | bytes 786432 | tf_op jit(solution)/shard_map/concatenate | solution.py:306
  39.9 0.3 collective-permute-start.3
  40.2 0.0 copy-done.6
  40.2 0.1 reshape_tile.3.down_bias_ref
  40.3 3.3 %copy-done.2 = bf16[3,3,3,384,384]{4,3,2,1,0:T(8,128)(2,1)S(1)} copy-done((bf16[3,3,3,384,384]{4,3,2,1,0:T(8,128)(2,1)S(1)}, bf16[3,3,3,384,384]{4,3,2,1,0:T(8,128)(2,1)}, u32[]{:S(2)}) %copy-start.2) | copy-done | bytes 7962648
  43.5 4.6 %late_edges.1 = (f32[128,128]{1,0:T(8,128)S(1)}, f32[32,64]{1,0:T(8,128)S(1)}) custom-call(s32[3]{0:T(128)S(1)} %add_convert_fusion.flag_ref, bf16[4,1,128,384]{3,2,1,0:T(8,128)(2,1)S(1)} %collective-permute-done.up, bf16[4,1,128,384]{3,2,1,0:T(8,128)(2,1)S(1)} %collective-permute-done.1.dn, f32[2,2,384,128]{3,2,1,0:T(8,128)S(1)} %get-tuple-element.23.edge_in, ...), custom_call_target="tpu_custom_call" | custom-call | flops 1358954496 | bytes 10000000 | tf_op jit(solution)/shard_map/late_edges/pallas_call | solution.py:277
  48.1 1.3 %collective-permute-start.4 = (f32[32,64]{1,0:T(8,128)S(1)}, f32[32,64]{1,0:T(8,128)S(1)}, u32[]{:S(2)}, u32[]{:S(2)}) collective-permute-start(f32[32,64]{1,0:T(8,128)S(1)} %get-tuple-element.26), channel_id=1, source_target_pairs={{0,8},{1,9},{2,10},{3,11},{4,12},{5,13},{6,14},{7,15},{8,16},{9,17... | collective-permute-start | bytes 24584 | tf_op jit(solution)/shard_map/ppermute | solution.py:256
  49.5 0.0 collective-permute-done.3.corner
  49.5 4.6 %early_edges.1 = f32[2,32,64]{2,1,0:T(8,128)S(1)} custom-call(s32[3]{0:T(128)S(1)} %add_convert_fusion.flag_ref, bf16[4,1,128,384]{3,2,1,0:T(8,128)(2,1)S(1)} %collective-permute-done.up, bf16[4,1,128,384]{3,2,1,0:T(8,128)(2,1)S(1)} %collective-permute-done.1.dn, bf16[2,2,128,384]{3,2,1,0:T(8,128)(2,1)S(1)} %collective-permute-done.3.corner, ...), custom_call_target="tpu_custom_call" | custom-call | flops 1358954496 | bytes 10000000 | tf_op jit(solution)/shard_map/early_edges/pallas_call | solution.py:277
  54.1 0.0 collective-permute-done.4
  54.2 0.7 %collective-permute-start.5 = (f32[32,64]{1,0:T(8,128)S(1)}, f32[32,64]{1,0:T(8,128)S(1)}, u32[]{:S(2)}, u32[]{:S(2)}) collective-permute-start(f32[32,64]{1,0:T(8,128)S(1)} %get-tuple-element.29), channel_id=1, source_target_pairs={{0,0},{1,4},{2,1},{3,5},{4,2},{5,6},{6,3},{7,7},{8,8},{9,12},{10,9... | collective-permute-start | bytes 24584 | tf_op jit(solution)/shard_map/ppermute | solution.py:342
  54.8 2.4 %collective-permute-start.6 = (f32[32,64]{1,0:T(8,128)S(1)}, f32[32,64]{1,0:T(8,128)S(1)}, u32[]{:S(2)}, u32[]{:S(2)}) collective-permute-start(f32[32,64]{1,0:T(8,128)S(1)} %get-tuple-element.30), channel_id=1, source_target_pairs={{0,4},{1,0},{2,5},{3,1},{4,6},{5,2},{6,7},{7,3},{8,12},{9,8},{10,1... | collective-permute-start | bytes 24584 | tf_op jit(solution)/shard_map/ppermute | solution.py:342
  57.3 0.0 collective-permute-done.5
  57.3 4.4 %collective-permute-done.6 = f32[32,64]{1,0:T(8,128)S(1)} collective-permute-done((f32[32,64]{1,0:T(8,128)S(1)}, f32[32,64]{1,0:T(8,128)S(1)}, u32[]{:S(2)}, u32[]{:S(2)}) %collective-permute-start.6) | collective-permute-done | bytes 8224 | tf_op jit(solution)/shard_map/ppermute | solution.py:342
  61.7 0.6 pad_maximum_fusion.1
  (12 shorter events, 0.1 us)
Async XLA Ops:
  0.0 4.8 %copy-start.3 = (bf16[4,4,128,384]{3,2,1,0:T(8,128)(2,1)S(1)}, bf16[4,4,128,384]{3,2,1,0:T(8,128)(2,1)}, u32[]{:S(2)}) copy-start(bf16[4,4,128,384]{3,2,1,0:T(8,128)(2,1)} %x_ref.1) | copy-start | bytes 4718596
  0.0 12.2 %copy-start.5 = (f32[384]{0:T(512)S(1)}, f32[384]{0:T(512)}, u32[]{:S(2)}) copy-start(f32[384]{0:T(512)} %param.7) | copy-start | bytes 4612
  0.0 12.2 %copy-start.4 = (bf16[3,2,2,384,16]{3,4,2,1,0:T(8,128)(2,1)S(1)}, bf16[3,2,2,384,16]{3,4,2,1,0:T(8,128)(2,1)}, u32[]{:S(2)}) copy-start(bf16[3,2,2,384,16]{3,4,2,1,0:T(8,128)(2,1)} %param.8) | copy-start | bytes 442372
  2.2 28.7 %collective-permute-start.2 = (bf16[2,4,128,384]{3,2,1,0:T(8,128)(2,1)}, bf16[2,4,128,384]{3,2,1,0:T(8,128)(2,1)}, u32[]{:S(2)}, u32[]{:S(2)}) collective-permute-start(bf16[2,4,128,384]{3,2,1,0:T(8,128)(2,1)} %slice.23), channel_id=1, source_target_pairs={{0,8},{1,9},{2,10},{3,11},{4,12},{5,13},{6,14},{7,15},{8,16},{9,17... | collective-permute-start | bytes 2359304 | tf_op jit(solution)/shard_map/ppermute | solution.py:256
  5.8 33.2 %collective-permute-start = (bf16[4,1,128,384]{3,2,1,0:T(8,128)(2,1)}, bf16[4,1,128,384]{3,2,1,0:T(8,128)(2,1)S(1)}, u32[]{:S(2)}, u32[]{:S(2)}) collective-permute-start(bf16[4,1,128,384]{3,2,1,0:T(8,128)(2,1)} %get-tuple-element.28), channel_id=1, source_target_pairs={{0,1},{1,2},{2,3},{3,4},{4,5},{5,6},{6,7},{7,0},{8,9},{9,10},{10,1... | collective-permute-start | bytes 1179656 | tf_op jit(solution)/shard_map/ppermute | solution.py:256
  8.7 30.3 %collective-permute-start.1 = (bf16[4,1,128,384]{3,2,1,0:T(8,128)(2,1)}, bf16[4,1,128,384]{3,2,1,0:T(8,128)(2,1)S(1)}, u32[]{:S(2)}, u32[]{:S(2)}) collective-permute-start(bf16[4,1,128,384]{3,2,1,0:T(8,128)(2,1)} %get-tuple-element.27), channel_id=1, source_target_pairs={{0,7},{1,0},{2,1},{3,2},{4,3},{5,4},{6,5},{7,6},{8,15},{9,8},{10,9... | collective-permute-start | bytes 1179656 | tf_op jit(solution)/shard_map/ppermute | solution.py:256
  12.2 3.3 %copy-start = (bf16[3,3,3,384,384]{4,3,2,1,0:T(8,128)(2,1)S(1)}, bf16[3,3,3,384,384]{4,3,2,1,0:T(8,128)(2,1)}, u32[]{:S(2)}) copy-start(bf16[3,3,3,384,384]{4,3,2,1,0:T(8,128)(2,1)} %w_ref.7) | copy-start | bytes 23887876
  15.5 15.5 %copy-start.1 = (bf16[3,3,3,384,384]{4,3,2,1,0:T(8,128)(2,1)S(1)}, bf16[3,3,3,384,384]{4,3,2,1,0:T(8,128)(2,1)}, u32[]{:S(2)}) copy-start(bf16[3,3,3,384,384]{4,3,2,1,0:T(8,128)(2,1)} %w_ref.7) | copy-start | bytes 23887876
  39.0 1.2 %copy-start.6 = (f32[16]{0:T(128)S(1)}, f32[16]{0:T(128)}, u32[]{:S(2)}) copy-start(f32[16]{0:T(128)} %param.9) | copy-start | bytes 196
  39.9 9.6 %collective-permute-start.3 = (bf16[2,2,128,384]{3,2,1,0:T(8,128)(2,1)}, bf16[2,2,128,384]{3,2,1,0:T(8,128)(2,1)S(1)}, u32[]{:S(2)}, u32[]{:S(2)}) collective-permute-start(bf16[2,2,128,384]{3,2,1,0:T(8,128)(2,1)} %pad_maximum_fusion), channel_id=1, source_target_pairs={{0,8},{1,9},{2,10},{3,11},{4,12},{5,13},{6,14},{7,15},{8,16},{9,17... | collective-permute-start | bytes 1179656 | tf_op jit(solution)/shard_map/ppermute | solution.py:256
  40.3 3.3 %copy-start.2 = (bf16[3,3,3,384,384]{4,3,2,1,0:T(8,128)(2,1)S(1)}, bf16[3,3,3,384,384]{4,3,2,1,0:T(8,128)(2,1)}, u32[]{:S(2)}) copy-start(bf16[3,3,3,384,384]{4,3,2,1,0:T(8,128)(2,1)} %w_ref.7) | copy-start | bytes 23887876
  48.1 6.0 %collective-permute-start.4 = (f32[32,64]{1,0:T(8,128)S(1)}, f32[32,64]{1,0:T(8,128)S(1)}, u32[]{:S(2)}, u32[]{:S(2)}) collective-permute-start(f32[32,64]{1,0:T(8,128)S(1)} %get-tuple-element.26), channel_id=1, source_target_pairs={{0,8},{1,9},{2,10},{3,11},{4,12},{5,13},{6,14},{7,15},{8,16},{9,17... | collective-permute-start | bytes 24584 | tf_op jit(solution)/shard_map/ppermute | solution.py:256
  54.2 3.1 %collective-permute-start.5 = (f32[32,64]{1,0:T(8,128)S(1)}, f32[32,64]{1,0:T(8,128)S(1)}, u32[]{:S(2)}, u32[]{:S(2)}) collective-permute-start(f32[32,64]{1,0:T(8,128)S(1)} %get-tuple-element.29), channel_id=1, source_target_pairs={{0,0},{1,4},{2,1},{3,5},{4,2},{5,6},{6,3},{7,7},{8,8},{9,12},{10,9... | collective-permute-start | bytes 24584 | tf_op jit(solution)/shard_map/ppermute | solution.py:342
  54.8 6.9 %collective-permute-start.6 = (f32[32,64]{1,0:T(8,128)S(1)}, f32[32,64]{1,0:T(8,128)S(1)}, u32[]{:S(2)}, u32[]{:S(2)}) collective-permute-start(f32[32,64]{1,0:T(8,128)S(1)} %get-tuple-element.30), channel_id=1, source_target_pairs={{0,4},{1,0},{2,5},{3,1},{4,6},{5,2},{6,7},{7,3},{8,12},{9,8},{10,1... | collective-permute-start | bytes 24584 | tf_op jit(solution)/shard_map/ppermute | solution.py:342

commit v3 on v2

v3 whole, which is shorter than its diff:
```python
import jax
import jax.numpy as jnp
from jax import lax
from jax.experimental import pallas as pl
from jax.experimental.pallas import tpu as pltpu
from jax.sharding import PartitionSpec as P

F32 = jnp.float32
BF16 = jnp.bfloat16
VMEM_LIMIT = 28 * 1024 * 1024
AXES = ("tm", "row")


def widen(rows, target, keep=None):
    width, channels = rows.shape
    if keep is not None:
        rows = jnp.where(keep, rows.astype(F32), 0.0).astype(BF16)
    value = rows.astype(F32)
    column = lax.broadcasted_iota(jnp.int32, (width, channels), 0)
    before = jnp.where(column == 0, 0.0, pltpu.roll(value, 1, 0))
    after = jnp.where(column == width - 1, 0.0, pltpu.roll(value, width - 1, 0))
    target[:, 0:channels] = before.astype(BF16)
    target[:, channels : 2 * channels] = rows
    target[:, 2 * channels : 3 * channels] = after.astype(BF16)


def tap_product(weight, positions):
    channels = weight.shape[-1]
    weight = weight.reshape(3 * channels, channels)
    positions = positions.reshape(-1, 3 * channels)
    return lax.dot_general(weight, positions, (((0,), (1,)), ((), ())), preferred_element_type=F32)


def projected(pre, bias, down_ref, f, rows):
    taps = (1,) if f % 2 == 0 else (2, 0)
    act = []
    for value in pre:
        value = value + bias
        act.append((value / (1.0 + jnp.exp(-value))).astype(BF16))
    weight = []
    for a in taps:
        for i in rows:
            parts = [down_ref[a, i % 2, dx] for dx in (0, 0, 1, 1)]
            weight.append(jnp.concatenate(parts, axis=0))
    product = jnp.dot(jnp.concatenate(weight, axis=0), jnp.concatenate(act, axis=1), preferred_element_type=F32)
    width = pre[0].shape[1]
    size = weight[0].shape[0]
    found = {}
    for n, a in enumerate(taps):
        for half in range(2):
            first = (2 * n + half) * size
            found[a, half] = product[first : first + size, half * width : (half + 1) * width]
    return found


def add_products(found, a, total_ref):
    for half in range(2):
        value = found[a, half]
        size = value.shape[0] // 2
        for dx in range(2):
            first = dx * 2 * size + half * size
            total_ref[first : first + size, :] += value[dx * size : (dx + 1) * size]


def fold(total, d_ref):
    d_ref[...] = total.T
    lanes = total.shape[0]
    count = total.shape[1] // 4
    lane = lax.broadcasted_iota(jnp.int32, (count, lanes), 1)
    result = jnp.zeros((count, lanes), F32)
    for s in range(4):
        keep = (lane // (lanes // 2) == s % 2) & ((lane // (lanes // 8)) % 2 == s // 2)
        result = result + jnp.where(keep, d_ref[pl.ds(s, count, stride=4), :], 0.0)
    return (result + pltpu.roll(result, lanes // 2, 1))[:, : lanes // 2]


def bias_columns(bias_ref, width):
    return jnp.broadcast_to(bias_ref[...], (width, bias_ref.shape[1])).T


def copies(pairs, sems, first=0):
    started = []
    for n, (source, target) in enumerate(pairs):
        started.append(pltpu.make_async_copy(source, target, sems.at[first + n]))
        started[-1].start()
    return started


def tap_rows(tap_row, height):
    return range(max(0, tap_row - 1), min(height, height + tap_row - 1))


def send_kernel(x_ref, up_ref, dn_ref, late_ref, sems):
    height = x_ref.shape[1]
    pairs = [(x_ref.at[:, height - 1 :], up_ref), (x_ref.at[:, :1], dn_ref), (x_ref.at[2:], late_ref)]
    for copy in copies(pairs, sems):
        copy.wait()


def own_kernel(x_ref, w_ref, bias_ref, down_ref, acc, weights, total_ref, rows_in, wide, sems):
    frames, height, width, channels = x_ref.shape
    order = [(a, b) for a in (2, 1, 0) for b in (1, 0, 2)]
    fetch = copies([(x_ref, rows_in)] + [(w_ref.at[t], weights.at[t]) for t in order], sems)
    fetch[0].wait()

    def one(n, carry):
        f, h = n // height, n % height
        widen(rows_in[f, h], wide.at[h, f])
        return carry

    lax.fori_loop(0, frames * height, one, 0)
    for n, (tap_time, tap_row) in enumerate(order):
        fetch[1 + n].wait()
        count = frames - 2 + tap_time
        rows = tap_rows(tap_row, height)
        product = tap_product(weights[tap_time, tap_row], wide[rows[0] : rows[-1] + 1, :count])
        for m, h in enumerate(rows):
            for g in range(count):
                first = (m * count + g) * width
                value = product[:, first : first + width]
                target = (h + 1 - tap_row, g + 2 - tap_time)
                if n == 0:
                    acc[target] = value
                else:
                    acc[target] += value
    bias = bias_columns(bias_ref, width)
    total_ref[...] = jnp.zeros_like(total_ref)
    for f in (2, 3):
        found = projected([acc[1, f], acc[2, f]], bias, down_ref, f, (1, 2))
        add_products(found, 2 - (f + 1) % 2, total_ref.at[0])
        if f == 3:
            add_products(found, 0, total_ref.at[1])


def earlier_kernel(flag_ref, x_ref, acc_in, weights, bias_ref, down_ref, edge_ref, total_ref, acc, rows_in, wide, sems):
    frames, height, width, channels = x_ref.shape
    (fetch,) = copies([(x_ref, rows_in)], sems)
    fetch.wait()
    keep = flag_ref[2] == 1

    def one(n, carry):
        f, h = n // height, n % height
        widen(rows_in[f, h], wide.at[h, f], keep)
        return carry

    lax.fori_loop(0, frames * height, one, 0)
    for tap_time in (0, 1):
        for tap_row in (1, 0, 2):
            rows = tap_rows(tap_row, height)
            count = frames - tap_time
            product = tap_product(weights[tap_time, tap_row], wide[rows[0] : rows[-1] + 1, tap_time:])
            for m, h in enumerate(rows):
                for f in range(count):
                    first = (m * count + f) * width
                    value = product[:, first : first + width]
                    target = (h + 1 - tap_row, f)
                    if (tap_time, tap_row) == (0, 1):
                        acc[target] = acc_in[target] + value
                    else:
                        acc[target] += value
    for side, i in enumerate((0, height - 1)):
        for f in (0, 1):
            edge_ref[side, f] = acc[i, f]
    bias = bias_columns(bias_ref, width)
    total_ref[...] = jnp.zeros_like(total_ref)
    for f in (0, 1):
        found = projected([acc[1, f], acc[2, f]], bias, down_ref, f, (1, 2))
        add_products(found, 2 - (f + 1) % 2, total_ref.at[0])
        if f == 1:
            add_products(found, 0, total_ref.at[1])


def edge_taps(keep, initial, weights, bias_ref, down_ref, acc, rows_in, wide, total):
    width = wide.shape[2]
    for side in range(2):
        for n in range(4):
            widen(rows_in[side, n], wide.at[side, n], keep(side, n))
    for tap_time in range(3):
        for side in range(2):
            product = tap_product(weights[tap_time, 2 * side], wide[side, tap_time : tap_time + 2])
            for f in range(2):
                value = product[:, f * width : (f + 1) * width]
                if tap_time == 0:
                    acc[side, f] = initial(side, f) + value
                else:
                    acc[side, f] += value
    bias = bias_columns(bias_ref, width)
    for f in (0, 1):
        found = projected([acc[0, f], acc[1, f]], bias, down_ref, f, (0, 3))
        add_products(found, 2 - (f + 1) % 2, total.at[0])
        if f == 1:
            add_products(found, 0, total.at[1])


def late_edge_kernel(
    flag_ref, up, dn, acc_in, total_in, weights, bias_ref, down_ref, late_ref, carry_ref, acc, rows_in, wide, total, d_ref, sems
):
    for copy in copies([(up.at[:, 0], rows_in.at[0]), (dn.at[:, 0], rows_in.at[1])], sems):
        copy.wait()
    total[...] = total_in[...]
    edge_taps(
        lambda side, n: flag_ref[side] == 1, lambda side, f: acc_in[3 * side, f + 2], weights, bias_ref, down_ref, acc, rows_in,
        wide, total,
    )
    late_ref[...] = total[0]
    carry_ref[...] = fold(total[1], d_ref)


def early_edge_kernel(
    flag_ref, up, dn, corner, edge_in, total_in, late_in, weights, bias_ref, down_ref, down_bias_ref, out_ref, acc, rows_in, wide,
    total, d_ref, sems,
):
    pairs = []
    for side, ref in enumerate((up, dn)):
        pairs += [(corner.at[:, side], rows_in.at[side, :2]), (ref.at[:2, 0], rows_in.at[side, 2:])]
    for copy in copies(pairs, sems):
        copy.wait()
    total[...] = total_in[...]

    def keep(side, n):
        exists = flag_ref[side] == 1
        return exists & (flag_ref[2] == 1) if n < 2 else exists

    edge_taps(
        keep, lambda side, f: edge_in[side, f], weights, bias_ref, down_ref, acc, rows_in, wide, total
    )
    out_ref[0] = fold(total[0], d_ref) + down_bias_ref[...]
    out_ref[1] = fold(total[1] + late_in[...], d_ref) + down_bias_ref[...]


def on_device(feature, conv_weight, conv_bias, down_weight, down_bias):
    frames, height, width, channels = feature.shape
    z = down_bias.shape[0]
    n_tm, n_row = lax.axis_size("tm"), lax.axis_size("row")
    tm, row = lax.axis_index("tm"), lax.axis_index("row")
    quarter, lanes = width // 4, 8 * z

    def shifted(value, by_tm, by_row):
        pairs = [
            (t * n_row + r, (t + by_tm) % n_tm * n_row + (r + by_row) % n_row) for t in range(n_tm) for r in range(n_row)
        ]
        return lax.ppermute(value, AXES, pairs)

    any_ref, smem = pl.BlockSpec(memory_space=pl.ANY), pl.BlockSpec(memory_space=pltpu.SMEM)
    vmem = pl.BlockSpec(memory_space=pltpu.VMEM)

    def call(kernel, name, units, ins, specs, outs, scratch, copied):
        return pl.pallas_call(
            kernel,
            in_specs=specs,
            out_specs=[any_ref if isinstance(o, jax.ShapeDtypeStruct) else vmem for o in outs],
            out_shape=outs,
            scratch_shapes=[*scratch, pltpu.SemaphoreType.DMA((copied,))],
            compiler_params=pltpu.CompilerParams(vmem_limit_bytes=VMEM_LIMIT),
            cost_estimate=pl.CostEstimate(
                flops=units * width * 6 * channels * channels, bytes_accessed=4_000_000, transcendentals=0
            ),
            name=name,
        )(*ins)

    flags = jnp.stack([row > 0, row < n_row - 1, tm > 0]).astype(jnp.int32)
    edge_rows = jax.ShapeDtypeStruct((frames, 1, width, channels), BF16)
    up, dn, earlier = call(
        send_kernel, "send", 1, (feature,), [any_ref],
        [edge_rows, edge_rows, jax.ShapeDtypeStruct((2, height, width, channels), BF16)], [], 3,
    )
    up = shifted(up, 0, 1)
    dn = shifted(dn, 0, -1)
    earlier = shifted(earlier, 1, 0)

    bias = conv_bias.reshape(1, channels)
    down = down_weight.transpose(0, 1, 2, 4, 3)
    patch_bias = jnp.tile(down_bias, 4).reshape(1, 4 * z)
    totals = pltpu.VMEM((2, lanes, width), F32)
    edges = pltpu.VMEM((2, 2, channels, width), F32)

    acc, weights, total_a = call(
        own_kernel, "own", 90,
        (feature, conv_weight, bias, down), [any_ref, any_ref, vmem, vmem],
        [pltpu.VMEM((height, frames, channels, width), F32), pltpu.VMEM(conv_weight.shape, BF16), totals],
        [pltpu.VMEM(feature.shape, BF16), pltpu.VMEM((height, frames, width, 3 * channels), BF16)], 10,
    )
    edge01, total_b = call(
        earlier_kernel, "earlier", 30,
        (flags, earlier, acc, weights, bias, down), [smem, any_ref, vmem, vmem, vmem, vmem],
        [edges, totals],
        [
            pltpu.VMEM((height, 2, channels, width), F32), pltpu.VMEM(earlier.shape, BF16),
            pltpu.VMEM((height, 2, width, 3 * channels), BF16),
        ], 1,
    )
    up, dn, edge01, acc = lax.optimization_barrier((up, dn, edge01, acc))
    corner = shifted(jnp.concatenate([up[2:], dn[2:]], axis=1), 1, 0)
    edge_scratch = [
        pltpu.VMEM((2, 2, channels, width), F32),
        pltpu.VMEM((2, 4, width, channels), BF16),
        pltpu.VMEM((2, 4, width, 3 * channels), BF16),
        pltpu.VMEM((2, lanes, width), F32),
        pltpu.VMEM((width, lanes), F32),
    ]
    late, carry = call(
        late_edge_kernel, "late_edges", 12,
        (flags, up, dn, acc, total_a, weights, bias, down), [smem, any_ref, any_ref, vmem, vmem, vmem, vmem, vmem],
        [pltpu.VMEM((lanes, width), F32), pltpu.VMEM((quarter, 4 * z), F32)], edge_scratch, 2,
    )
    carry = shifted(carry, 1, 0)
    (out,) = call(
        early_edge_kernel, "early_edges", 12,
        (flags, up, dn, corner, edge01, total_b, late, weights, bias, down, patch_bias),
        [smem, any_ref, any_ref, any_ref, vmem, vmem, vmem, vmem, vmem, vmem, vmem],
        [pltpu.VMEM((2, quarter, 4 * z), F32)], edge_scratch, 4,
    )

    half = n_row // 2

    def routed(value, slot):
        pairs = []
        for t in range(n_tm):
            for r in range(n_row):
                target = r // 2 if (r % 2 == 0) == (slot == 0) else half + r // 2
                pairs.append((t * n_row + r, t * n_row + target))
        return lax.ppermute(value, AXES, pairs)

    first = out[0] + jnp.where(tm > 0, carry, 0.0)
    last = out[1]
    is_even = row % 2 == 0
    got_a = routed(jnp.where(is_even, first, last), 0)
    got_b = routed(jnp.where(is_even, last, first), 1)
    low = row < half
    return jnp.concatenate([jnp.where(low, got_a, got_b), jnp.where(low, got_b, got_a)], axis=0)


def solution(mesh):
    return jax.shard_map(
        on_device,
        mesh=mesh,
        in_specs=(P("tm", "row", None, None), P(), P(), P(), P()),
        out_specs=P(AXES, None),
        check_vma=False,
    )
```

time: 62.6 us -> 73.7 us (1.18)
  the two profiles are of different devices: /device:TPU:1 before, /device:TPU:8 now
where the time goes in v3:
time: 73.7 us; the launch traced here: 72.7 us
  Pallas kernels  34.7 us (47%)
  local copies, waits for them, and re-layouts  19.1 us (26%)
  starting transfers between devices  12.1 us (16%)
  waiting for transfers between devices  5.22 us (7%)
  other arithmetic  1.5 us (2%)
    pallas_call x5, Pallas kernels, call(): pl.pallas_call(kernel, in_specs=specs, out_specs=[any_ref if isinstance(o...  34.7 us
    unnamed x30, local copies, waits for them, and re-layouts  17.4 us
    ppermute x5, starting transfers between devices, shifted(): return lax.ppermute(value, AXES, pairs)  7.7 us
    ppermute x2, waiting for transfers between devices, routed(): return lax.ppermute(value, AXES, pairs)  4.84 us
    ppermute x2, starting transfers between devices, routed(): return lax.ppermute(value, AXES, pairs)  4.36 us
  transfers between devices with their start and end apart: 7, of which 2 were waited for; matrix products, arithmetic and copies ran while one was open for 1% of the time, Pallas kernels for 46%

profile of v3, /device:TPU:8, one launch (start us, length us, event | category | flops | bytes accessed | tf_op | source)
XLA Modules:
  0.0 72.7 jit_solution(14391047864419305115)
XLA Ops:
  0.0 1.4 %copy-done.3 = bf16[4,4,128,384]{3,2,1,0:T(8,128)(2,1)S(1)} copy-done((bf16[4,4,128,384]{3,2,1,0:T(8,128)(2,1)S(1)}, bf16[4,4,128,384]{3,2,1,0:T(8,128)(2,1)}, u32[]{:S(2)}) %copy-start.3) | copy-done | bytes 1572888
  1.4 1.2 %send.1 = (bf16[4,1,128,384]{3,2,1,0:T(8,128)(2,1)}, bf16[4,1,128,384]{3,2,1,0:T(8,128)(2,1)}, bf16[2,4,128,384]{3,2,1,0:T(8,128)(2,1)}) custom-call(bf16[4,4,128,384]{3,2,1,0:T(8,128)(2,1)S(1)} %copy-done.3), custom_call_target="tpu_custom_call" | custom-call | flops 113246208 | bytes 4000000 | tf_op jit(solution)/shard_map/send/pallas_call | solution.py:248
  2.6 0.1 collective-permute-start.2
  2.7 2.4 %collective-permute-start = (bf16[4,1,128,384]{3,2,1,0:T(8,128)(2,1)}, bf16[4,1,128,384]{3,2,1,0:T(8,128)(2,1)S(1)}, u32[]{:S(2)}, u32[]{:S(2)}) collective-permute-start(bf16[4,1,128,384]{3,2,1,0:T(8,128)(2,1)} %get-tuple-element.19), channel_id=1, source_target_pairs={{0,1},{1,2},{2,3},{3,4},{4,5},{5,6},{6,7},{7,0},{8,9},{9,10},{10,1... | collective-permute-start | bytes 1179656 | tf_op jit(solution)/shard_map/ppermute | solution.py:242
  5.1 3.6 %collective-permute-start.1 = (bf16[4,1,128,384]{3,2,1,0:T(8,128)(2,1)}, bf16[4,1,128,384]{3,2,1,0:T(8,128)(2,1)}, u32[]{:S(2)}, u32[]{:S(2)}) collective-permute-start(bf16[4,1,128,384]{3,2,1,0:T(8,128)(2,1)} %get-tuple-element.20), channel_id=1, source_target_pairs={{0,7},{1,0},{2,1},{3,2},{4,3},{5,4},{6,5},{7,6},{8,15},{9,8},{10,9... | collective-permute-start | bytes 1179656 | tf_op jit(solution)/shard_map/ppermute | solution.py:242
  8.6 0.7 reshape.4.bias_ref
  9.3 1.4 %copy-done.4 = bf16[4,4,128,384]{3,2,1,0:T(8,128)(2,1)S(1)} copy-done((bf16[4,4,128,384]{3,2,1,0:T(8,128)(2,1)S(1)}, bf16[4,4,128,384]{3,2,1,0:T(8,128)(2,1)}, u32[]{:S(2)}) %copy-start.4) | copy-done | bytes 1572888
  10.7 0.9 %copy-done.7 = bf16[3,2,2,384,16]{3,4,2,1,0:T(8,128)(2,1)S(1)} copy-done((bf16[3,2,2,384,16]{3,4,2,1,0:T(8,128)(2,1)S(1)}, bf16[3,2,2,384,16]{3,4,2,1,0:T(8,128)(2,1)}, u32[]{:S(2)}) %copy-start.7) | copy-done | bytes 147480
  11.6 3.3 %copy-done.13 = bf16[3,3,3,384,384]{4,3,2,1,0:T(8,128)(2,1)S(1)} copy-done((bf16[3,3,3,384,384]{4,3,2,1,0:T(8,128)(2,1)S(1)}, bf16[3,3,3,384,384]{4,3,2,1,0:T(8,128)(2,1)}, u32[]{:S(2)}) %copy-start.13) | copy-done | bytes 7962648
  14.9 17.5 %own.1 = (f32[4,4,384,128]{3,2,1,0:T(8,128)S(1)}, bf16[3,3,3,384,384]{4,3,2,1,0:T(8,128)(2,1)S(1)}, f32[2,128,128]{2,1,0:T(8,128)S(1)}) custom-call(bf16[4,4,128,384]{3,2,1,0:T(8,128)(2,1)S(1)} %copy-done.4, bf16[3,3,3,384,384]{4,3,2,1,0:T(8,128)(2,1)S(1)} %copy-done.13, f32[1,384]{1,0:T(1,128)S(1)} %reshape.4.bias_ref, bf16[3,2,2,16,384]{4,3,2,1,0:T(8,128)(2,1)S(1)} %bitcast.18), custom_call_target="tpu_custom_call" | custom-call | flops 10192158720 | bytes 4000000 | tf_op jit(solution)/shard_map/own/pallas_call | solution.py:248
  32.4 0.6 copy-done.11
  33.0 0.1 add_convert_fusion.flag_ref
  33.1 0.0 collective-permute-done.2.x_ref
  33.1 7.1 %earlier.1 = (f32[2,2,384,128]{3,2,1,0:T(8,128)S(1)}, f32[2,128,128]{2,1,0:T(8,128)S(1)}) custom-call(s32[3]{0:T(128)S(1)} %add_convert_fusion.flag_ref, bf16[2,4,128,384]{3,2,1,0:T(8,128)(2,1)} %collective-permute-done.2.x_ref, f32[4,4,384,128]{3,2,1,0:T(8,128)S(1)} %get-tuple-element.29.acc_in, bf16[3,3,3,384,384]{4,3,2,1,0:T(8,128)(2,1)S(1)} %get-tuple-element.23.weights, ...), custom_call_target="tpu_custom_call" | custom-call | flops 3397386240 | bytes 4000000 | tf_op jit(solution)/shard_map/earlier/pallas_call | solution.py:248
  40.2 3.1 %copy-done = bf16[3,3,3,384,384]{4,3,2,1,0:T(8,128)(2,1)} copy-done((bf16[3,3,3,384,384]{4,3,2,1,0:T(8,128)(2,1)}, bf16[3,3,3,384,384]{4,3,2,1,0:T(8,128)(2,1)S(1)}, u32[]{:S(2)}) %copy-start) | copy-done | bytes 7962648
  43.3 0.9 %copy-done.5 = f32[2,2,384,128]{3,2,1,0:T(8,128)} copy-done((f32[2,2,384,128]{3,2,1,0:T(8,128)}, f32[2,2,384,128]{3,2,1,0:T(8,128)S(1)}, u32[]{:S(2)}) %copy-start.5) | copy-done | bytes 786456
  44.2 0.7 copy-done.9
  44.9 0.9 %slice.13 = bf16[2,1,128,384]{3,2,1,0:T(8,128)(2,1)S(1)} slice(bf16[4,1,128,384]{3,2,1,0:T(8,128)(2,1)} %collective-permute-done.1.dn), slice={[2:4], [0:1], [0:128], [0:384]} | slice | bytes 393216 | tf_op jit(solution)/shard_map/slice | solution.py:293
  45.9 0.8 %pad_maximum_fusion = bf16[2,2,128,384]{3,2,1,0:T(8,128)(2,1)} fusion(bf16[2,1,128,384]{3,2,1,0:T(8,128)(2,1)S(1)} %slice.13, bf16[2,1,128,384]{3,2,1,0:T(8,128)(2,1)S(1)} %slice.12), kind=kLoop, calls=%fused_computation | loop fusion | flops 196608 | bytes 786432 | tf_op jit(solution)/shard_map/concatenate | solution.py:293
  46.6 1.2 %collective-permute-start.3 = (bf16[2,2,128,384]{3,2,1,0:T(8,128)(2,1)}, bf16[2,2,128,384]{3,2,1,0:T(8,128)(2,1)}, u32[]{:S(2)}, u32[]{:S(2)}) collective-permute-start(bf16[2,2,128,384]{3,2,1,0:T(8,128)(2,1)} %pad_maximum_fusion), channel_id=1, source_target_pairs={{0,8},{1,9},{2,10},{3,11},{4,12},{5,13},{6,14},{7,15},{8,16},{9,17... | collective-permute-start | bytes 1179656 | tf_op jit(solution)/shard_map/ppermute | solution.py:242
  47.8 0.1 reshape_tile.3.down_bias_ref
  47.9 3.3 %copy-done.1 = bf16[3,3,3,384,384]{4,3,2,1,0:T(8,128)(2,1)S(1)} copy-done((bf16[3,3,3,384,384]{4,3,2,1,0:T(8,128)(2,1)S(1)}, bf16[3,3,3,384,384]{4,3,2,1,0:T(8,128)(2,1)}, u32[]{:S(2)}) %copy-start.1) | copy-done | bytes 7962648
  51.2 0.9 %copy-done.8 = bf16[3,2,2,384,16]{3,4,2,1,0:T(8,128)(2,1)S(1)} copy-done((bf16[3,2,2,384,16]{3,4,2,1,0:T(8,128)(2,1)S(1)}, bf16[3,2,2,384,16]{3,4,2,1,0:T(8,128)(2,1)}, u32[]{:S(2)}) %copy-start.8) | copy-done | bytes 147480
  52.1 0.9 %copy-done.12 = f32[2,128,128]{2,1,0:T(8,128)S(1)} copy-done((f32[2,128,128]{2,1,0:T(8,128)S(1)}, f32[2,128,128]{2,1,0:T(8,128)}, u32[]{:S(2)}) %copy-start.12) | copy-done | bytes 131096
  53.0 4.6 %late_edges.1 = (f32[128,128]{1,0:T(8,128)S(1)}, f32[32,64]{1,0:T(8,128)S(1)}) custom-call(s32[3]{0:T(128)S(1)} %add_convert_fusion.flag_ref, bf16[4,1,128,384]{3,2,1,0:T(8,128)(2,1)S(1)} %collective-permute-done.up, bf16[4,1,128,384]{3,2,1,0:T(8,128)(2,1)} %collective-permute-done.1.dn, f32[4,4,384,128]{3,2,1,0:T(8,128)S(1)} %get-tuple-element.29.acc_in, ...), custom_call_target="tpu_custom_call" | custom-call | flops 1358954496 | bytes 4000000 | tf_op jit(solution)/shard_map/late_edges/pallas_call | solution.py:248
  57.6 0.5 collective-permute-start.4
  58.1 4.4 %early_edges.1 = f32[2,32,64]{2,1,0:T(8,128)S(1)} custom-call(s32[3]{0:T(128)S(1)} %add_convert_fusion.flag_ref, bf16[4,1,128,384]{3,2,1,0:T(8,128)(2,1)S(1)} %collective-permute-done.up, bf16[4,1,128,384]{3,2,1,0:T(8,128)(2,1)} %collective-permute-done.1.dn, bf16[2,2,128,384]{3,2,1,0:T(8,128)(2,1)} %collective-permute-done.3.corner, ...), custom_call_target="tpu_custom_call" | custom-call | flops 1358954496 | bytes 4000000 | tf_op jit(solution)/shard_map/early_edges/pallas_call | solution.py:248
  62.5 0.4 collective-permute-done.4
  62.9 0.7 collective-permute-start.5
  63.6 3.7 %collective-permute-start.6 = (f32[32,64]{1,0:T(8,128)S(1)}, f32[32,64]{1,0:T(8,128)S(1)}, u32[]{:S(2)}, u32[]{:S(2)}) collective-permute-start(f32[32,64]{1,0:T(8,128)S(1)} %get-tuple-element.34), channel_id=1, source_target_pairs={{0,4},{1,0},{2,5},{3,1},{4,6},{5,2},{6,7},{7,3},{8,12},{9,8},{10,1... | collective-permute-start | bytes 24584 | tf_op jit(solution)/shard_map/ppermute | solution.py:322
  67.3 4.8 %collective-permute-done.6 = f32[32,64]{1,0:T(8,128)S(1)} collective-permute-done((f32[32,64]{1,0:T(8,128)S(1)}, f32[32,64]{1,0:T(8,128)S(1)}, u32[]{:S(2)}, u32[]{:S(2)}) %collective-permute-start.6) | collective-permute-done | bytes 8224 | tf_op jit(solution)/shard_map/ppermute | solution.py:322
  72.1 0.6 pad_maximum_fusion.1
  (27 shorter events, 0.1 us)
Async XLA Ops:
  0.0 1.4 %copy-start.3 = (bf16[4,4,128,384]{3,2,1,0:T(8,128)(2,1)S(1)}, bf16[4,4,128,384]{3,2,1,0:T(8,128)(2,1)}, u32[]{:S(2)}) copy-start(bf16[4,4,128,384]{3,2,1,0:T(8,128)(2,1)} %x_ref.3) | copy-start | bytes 4718596
  2.6 30.5 %collective-permute-start.2 = (bf16[2,4,128,384]{3,2,1,0:T(8,128)(2,1)}, bf16[2,4,128,384]{3,2,1,0:T(8,128)(2,1)}, u32[]{:S(2)}, u32[]{:S(2)}) collective-permute-start(bf16[2,4,128,384]{3,2,1,0:T(8,128)(2,1)} %get-tuple-element.21), channel_id=1, source_target_pairs={{0,8},{1,9},{2,10},{3,11},{4,12},{5,13},{6,14},{7,15},{8,16},{9,17... | collective-permute-start | bytes 2359304 | tf_op jit(solution)/shard_map/ppermute | solution.py:242
  2.7 42.2 %collective-permute-start = (bf16[4,1,128,384]{3,2,1,0:T(8,128)(2,1)}, bf16[4,1,128,384]{3,2,1,0:T(8,128)(2,1)S(1)}, u32[]{:S(2)}, u32[]{:S(2)}) collective-permute-start(bf16[4,1,128,384]{3,2,1,0:T(8,128)(2,1)} %get-tuple-element.19), channel_id=1, source_target_pairs={{0,1},{1,2},{2,3},{3,4},{4,5},{5,6},{6,7},{7,0},{8,9},{9,10},{10,1... | collective-permute-start | bytes 1179656 | tf_op jit(solution)/shard_map/ppermute | solution.py:242
  5.1 39.8 %collective-permute-start.1 = (bf16[4,1,128,384]{3,2,1,0:T(8,128)(2,1)}, bf16[4,1,128,384]{3,2,1,0:T(8,128)(2,1)}, u32[]{:S(2)}, u32[]{:S(2)}) collective-permute-start(bf16[4,1,128,384]{3,2,1,0:T(8,128)(2,1)} %get-tuple-element.20), channel_id=1, source_target_pairs={{0,7},{1,0},{2,1},{3,2},{4,3},{5,4},{6,5},{7,6},{8,15},{9,8},{10,9... | collective-permute-start | bytes 1179656 | tf_op jit(solution)/shard_map/ppermute | solution.py:242
  9.3 1.4 %copy-start.4 = (bf16[4,4,128,384]{3,2,1,0:T(8,128)(2,1)S(1)}, bf16[4,4,128,384]{3,2,1,0:T(8,128)(2,1)}, u32[]{:S(2)}) copy-start(bf16[4,4,128,384]{3,2,1,0:T(8,128)(2,1)} %x_ref.3) | copy-start | bytes 4718596
  10.7 0.9 %copy-start.7 = (bf16[3,2,2,384,16]{3,4,2,1,0:T(8,128)(2,1)S(1)}, bf16[3,2,2,384,16]{3,4,2,1,0:T(8,128)(2,1)}, u32[]{:S(2)}) copy-start(bf16[3,2,2,384,16]{3,4,2,1,0:T(8,128)(2,1)} %param.8) | copy-start | bytes 442372
  11.6 3.3 %copy-start.13 = (bf16[3,3,3,384,384]{4,3,2,1,0:T(8,128)(2,1)S(1)}, bf16[3,3,3,384,384]{4,3,2,1,0:T(8,128)(2,1)}, u32[]{:S(2)}) copy-start(bf16[3,3,3,384,384]{4,3,2,1,0:T(8,128)(2,1)} %w_ref.1) | copy-start | bytes 23887876
  32.3 0.6 copy-start.11
  33.0 14.8 %copy-start.14 = (f32[16]{0:T(128)S(1)}, f32[16]{0:T(128)}, u32[]{:S(2)}) copy-start(f32[16]{0:T(128)} %param.9) | copy-start | bytes 196
  40.2 3.1 %copy-start = (bf16[3,3,3,384,384]{4,3,2,1,0:T(8,128)(2,1)}, bf16[3,3,3,384,384]{4,3,2,1,0:T(8,128)(2,1)S(1)}, u32[]{:S(2)}) copy-start(bf16[3,3,3,384,384]{4,3,2,1,0:T(8,128)(2,1)S(1)} %get-tuple-element.23.weights) | copy-start | bytes 23887876
  43.3 0.9 %copy-start.5 = (f32[2,2,384,128]{3,2,1,0:T(8,128)}, f32[2,2,384,128]{3,2,1,0:T(8,128)S(1)}, u32[]{:S(2)}) copy-start(f32[2,2,384,128]{3,2,1,0:T(8,128)S(1)} %get-tuple-element.27.edge_in) | copy-start | bytes 2359300
  44.2 0.7 copy-start.9
  46.6 11.5 %collective-permute-start.3 = (bf16[2,2,128,384]{3,2,1,0:T(8,128)(2,1)}, bf16[2,2,128,384]{3,2,1,0:T(8,128)(2,1)}, u32[]{:S(2)}, u32[]{:S(2)}) collective-permute-start(bf16[2,2,128,384]{3,2,1,0:T(8,128)(2,1)} %pad_maximum_fusion), channel_id=1, source_target_pairs={{0,8},{1,9},{2,10},{3,11},{4,12},{5,13},{6,14},{7,15},{8,16},{9,17... | collective-permute-start | bytes 1179656 | tf_op jit(solution)/shard_map/ppermute | solution.py:242
  47.9 3.3 %copy-start.1 = (bf16[3,3,3,384,384]{4,3,2,1,0:T(8,128)(2,1)S(1)}, bf16[3,3,3,384,384]{4,3,2,1,0:T(8,128)(2,1)}, u32[]{:S(2)}) copy-start(bf16[3,3,3,384,384]{4,3,2,1,0:T(8,128)(2,1)} %copy-done) | copy-start | bytes 23887876
  51.2 0.9 %copy-start.8 = (bf16[3,2,2,384,16]{3,4,2,1,0:T(8,128)(2,1)S(1)}, bf16[3,2,2,384,16]{3,4,2,1,0:T(8,128)(2,1)}, u32[]{:S(2)}) copy-start(bf16[3,2,2,384,16]{3,4,2,1,0:T(8,128)(2,1)} %param.8) | copy-start | bytes 442372
  52.1 0.9 %copy-start.12 = (f32[2,128,128]{2,1,0:T(8,128)S(1)}, f32[2,128,128]{2,1,0:T(8,128)}, u32[]{:S(2)}) copy-start(f32[2,128,128]{2,1,0:T(8,128)} %copy-done.11) | copy-start | bytes 393220
  53.0 5.1 %copy-start.2 = (bf16[3,3,3,384,384]{4,3,2,1,0:T(8,128)(2,1)S(1)}, bf16[3,3,3,384,384]{4,3,2,1,0:T(8,128)(2,1)}, u32[]{:S(2)}) copy-start(bf16[3,3,3,384,384]{4,3,2,1,0:T(8,128)(2,1)} %copy-done) | copy-start | bytes 23887876
  53.0 5.1 %copy-start.6 = (f32[2,2,384,128]{3,2,1,0:T(8,128)S(1)}, f32[2,2,384,128]{3,2,1,0:T(8,128)}, u32[]{:S(2)}) copy-start(f32[2,2,384,128]{3,2,1,0:T(8,128)} %copy-done.5) | copy-start | bytes 2359300
  53.0 5.1 %copy-start.10 = (f32[2,128,128]{2,1,0:T(8,128)S(1)}, f32[2,128,128]{2,1,0:T(8,128)}, u32[]{:S(2)}) copy-start(f32[2,128,128]{2,1,0:T(8,128)} %copy-done.9) | copy-start | bytes 393220
  57.6 5.3 %collective-permute-start.4 = (f32[32,64]{1,0:T(8,128)S(1)}, f32[32,64]{1,0:T(8,128)S(1)}, u32[]{:S(2)}, u32[]{:S(2)}) collective-permute-start(f32[32,64]{1,0:T(8,128)S(1)} %get-tuple-element.32), channel_id=1, source_target_pairs={{0,8},{1,9},{2,10},{3,11},{4,12},{5,13},{6,14},{7,15},{8,16},{9,17... | collective-permute-start | bytes 24584 | tf_op jit(solution)/shard_map/ppermute | solution.py:242
  62.9 4.4 %collective-permute-start.5 = (f32[32,64]{1,0:T(8,128)S(1)}, f32[32,64]{1,0:T(8,128)S(1)}, u32[]{:S(2)}, u32[]{:S(2)}) collective-permute-start(f32[32,64]{1,0:T(8,128)S(1)} %get-tuple-element.33), channel_id=1, source_target_pairs={{0,0},{1,4},{2,1},{3,5},{4,2},{5,6},{6,3},{7,7},{8,8},{9,12},{10,9... | collective-permute-start | bytes 24584 | tf_op jit(solution)/shard_map/ppermute | solution.py:322
  63.6 8.5 %collective-permute-start.6 = (f32[32,64]{1,0:T(8,128)S(1)}, f32[32,64]{1,0:T(8,128)S(1)}, u32[]{:S(2)}, u32[]{:S(2)}) collective-permute-start(f32[32,64]{1,0:T(8,128)S(1)} %get-tuple-element.34), channel_id=1, source_target_pairs={{0,4},{1,0},{2,5},{3,1},{4,6},{5,2},{6,7},{7,3},{8,12},{9,8},{10,1... | collective-permute-start | bytes 24584 | tf_op jit(solution)/shard_map/ppermute | solution.py:322

commit v4 on v3

v4 whole, which is shorter than its diff:
```python
import jax
import jax.numpy as jnp
from jax import lax
from jax.experimental import pallas as pl
from jax.experimental.pallas import tpu as pltpu
from jax.sharding import PartitionSpec as P

F32 = jnp.float32
BF16 = jnp.bfloat16
VMEM_LIMIT = 20 * 1024 * 1024
AXES = ("tm", "row")
HALO = pl.ANY


def widen(rows, target, keep=None):
    width, channels = rows.shape
    if keep is not None:
        rows = jnp.where(keep, rows.astype(F32), 0.0).astype(BF16)
    value = rows.astype(F32)
    column = lax.broadcasted_iota(jnp.int32, (width, channels), 0)
    before = jnp.where(column == 0, 0.0, pltpu.roll(value, 1, 0))
    after = jnp.where(column == width - 1, 0.0, pltpu.roll(value, width - 1, 0))
    target[:, 0:channels] = before.astype(BF16)
    target[:, channels : 2 * channels] = rows
    target[:, 2 * channels : 3 * channels] = after.astype(BF16)


def tap_product(weight, positions):
    channels = weight.shape[-1]
    weight = weight.reshape(3 * channels, channels)
    positions = positions.reshape(-1, 3 * channels)
    return lax.dot_general(weight, positions, (((0,), (1,)), ((), ())), preferred_element_type=F32)


def projected(pre, bias, down_ref, f, rows):
    taps = (1,) if f % 2 == 0 else (2, 0)
    act = []
    for value in pre:
        value = value + bias
        act.append((value / (1.0 + jnp.exp(-value))).astype(BF16))
    weight = []
    for a in taps:
        for i in rows:
            parts = [down_ref[a, i % 2, dx] for dx in (0, 0, 1, 1)]
            weight.append(jnp.concatenate(parts, axis=0))
    product = jnp.dot(jnp.concatenate(weight, axis=0), jnp.concatenate(act, axis=1), preferred_element_type=F32)
    width = pre[0].shape[1]
    size = weight[0].shape[0]
    found = {}
    for n, a in enumerate(taps):
        for half in range(2):
            first = (2 * n + half) * size
            found[a, half] = product[first : first + size, half * width : (half + 1) * width]
    return found


def add_products(found, a, total_ref):
    for half in range(2):
        value = found[a, half]
        size = value.shape[0] // 2
        for dx in range(2):
            first = dx * 2 * size + half * size
            total_ref[first : first + size, :] += value[dx * size : (dx + 1) * size]


def fold(total, d_ref):
    d_ref[...] = total.T
    lanes = total.shape[0]
    count = total.shape[1] // 4
    lane = lax.broadcasted_iota(jnp.int32, (count, lanes), 1)
    result = jnp.zeros((count, lanes), F32)
    for s in range(4):
        keep = (lane // (lanes // 2) == s % 2) & ((lane // (lanes // 8)) % 2 == s // 2)
        result = result + jnp.where(keep, d_ref[pl.ds(s, count, stride=4), :], 0.0)
    return (result + pltpu.roll(result, lanes // 2, 1))[:, : lanes // 2]


def exists(side):
    if side == 2:
        return lax.axis_index("tm") > 0
    row = lax.axis_index("row")
    return row > 0 if side == 0 else row < lax.axis_size("row") - 1


def copies(pairs, sems, first=0):
    started = []
    for n, (source, target) in enumerate(pairs):
        started.append(pltpu.make_async_copy(source, target, sems.at[first + n]))
        started[-1].start()
    return started


def tap_rows(tap_row, height):
    return range(max(0, tap_row - 1), min(height, height + tap_row - 1))


def send_kernel(x_ref, up_ref, dn_ref, late_ref, sems):
    height = x_ref.shape[1]
    pairs = [(x_ref.at[:, height - 1 :], up_ref), (x_ref.at[:, :1], dn_ref), (x_ref.at[2:], late_ref)]
    for copy in copies(pairs, sems):
        copy.wait()


def relay_kernel(up, dn, out_ref, sems):
    for copy in copies([(up.at[2:], out_ref.at[:, :1]), (dn.at[2:], out_ref.at[:, 1:])], sems):
        copy.wait()


def own_kernel(x_ref, w_ref, bias_in, down_in, acc, weights, bias_ref, down_ref, totals, rows_in, bias_row, wide, sems):
    frames, height, width, channels = x_ref.shape
    order = [(a, b) for a in (2, 1, 0) for b in (1, 0, 2)]
    fetch = copies(
        [(x_ref, rows_in)] + [(w_ref.at[t], weights.at[t]) for t in order] + [(bias_in, bias_row), (down_in, down_ref)], sems
    )
    fetch[0].wait()

    def one(n, carry):
        f, h = n // height, n % height
        widen(rows_in[f, h], wide.at[h, f])
        return carry

    lax.fori_loop(0, frames * height, one, 0)
    for n, (tap_time, tap_row) in enumerate(order):
        fetch[1 + n].wait()
        count = frames - 2 + tap_time
        rows = tap_rows(tap_row, height)
        product = tap_product(weights[tap_time, tap_row], wide[rows[0] : rows[-1] + 1, :count])
        for m, h in enumerate(rows):
            for g in range(count):
                first = (m * count + g) * width
                value = product[:, first : first + width]
                target = (h + 1 - tap_row, g + 2 - tap_time)
                if n == 0:
                    acc[target] = value
                else:
                    acc[target] += value
    fetch[-2].wait()
    fetch[-1].wait()
    bias_ref[...] = jnp.broadcast_to(bias_row[...].reshape(1, channels), (width, channels)).T
    totals[...] = jnp.zeros_like(totals)
    project_rows(acc, (2, 3), (1, 2), bias_ref, down_ref, totals)


def project_rows(acc, frames, rows, bias_ref, down_ref, totals):
    for f in frames:
        found = projected([acc[i, f] for i in rows], bias_ref[...], down_ref, f, rows)
        add_products(found, 1 + f % 2, totals.at[f // 2])
        if f % 2 == 1:
            add_products(found, 0, totals.at[f // 2 + 1])


def earlier_kernel(x_ref, acc_in, weights, bias_ref, down_ref, totals_in, edge_ref, totals_ref, rows_in, acc, totals, wide, sems):
    frames, height, width, channels = x_ref.shape
    (fetch,) = copies([(x_ref, rows_in)], sems)
    moved = copies([(acc_in.at[side * (height - 1), 2:], edge_ref.at[side, 2:]) for side in range(2)], sems, 1)
    totals[...] = totals_in[...]
    keep = exists(2)
    fetch.wait()

    def one(n, carry):
        f, h = n // height, n % height
        widen(rows_in[f, h], wide.at[h, f], keep)
        return carry

    lax.fori_loop(0, frames * height, one, 0)
    for tap_time in (0, 1):
        for tap_row in (1, 0, 2):
            rows = tap_rows(tap_row, height)
            count = frames - tap_time
            product = tap_product(weights[tap_time, tap_row], wide[rows[0] : rows[-1] + 1, tap_time:])
            for m, h in enumerate(rows):
                for f in range(count):
                    first = (m * count + f) * width
                    target = (h + 1 - tap_row, f)
                    value = acc_in[target] if (tap_time, tap_row) == (0, 1) else acc[target]
                    acc[target] = value + product[:, first : first + width]
    moved += copies([(acc.at[side * (height - 1)], edge_ref.at[side, :2]) for side in range(2)], sems, 3)
    project_rows(acc, (0, 1), (1, 2), bias_ref, down_ref, totals)
    moved += copies([(totals, totals_ref)], sems, 5)
    for copy in moved:
        copy.wait()


def edge_taps(pairs, keep, first, edge_ref, totals_in, w_ref, bias_in, down_in, scratch):
    acc, rows_in, weights, wide, bias_row, down_ref, totals, d_ref, sems = scratch
    width, channels = rows_in.shape[2:]
    taps = [(a, side) for a in range(3) for side in range(2)]
    brought = copies(pairs, sems)
    heavy = copies([(w_ref.at[a, 2 * side], weights.at[n]) for n, (a, side) in enumerate(taps)], sems, 4)
    rest = copies(
        [(edge_ref.at[:, first : first + 2], acc), (totals_in, totals), (bias_in, bias_row), (down_in, down_ref)], sems, 10
    )
    for copy in brought:
        copy.wait()
    for side in range(2):
        for n in range(4):
            widen(rows_in[side, n], wide.at[side, n], keep(side, n))
    rest[0].wait()
    for n, (tap_time, side) in enumerate(taps):
        heavy[n].wait()
        product = tap_product(weights[n], wide[side, tap_time : tap_time + 2])
        for f in range(2):
            acc[side, f] += product[:, f * width : (f + 1) * width]
    for copy in rest[1:]:
        copy.wait()
    bias = jnp.broadcast_to(bias_row[...].reshape(1, channels), (width, channels)).T
    for f in (first, first + 1):
        found = projected([acc[side, f - first] for side in range(2)], bias, down_ref, f, (0, 3))
        add_products(found, 1 + f % 2, totals.at[f // 2])
        if f % 2 == 1:
            add_products(found, 0, totals.at[f // 2 + 1])


def late_edge_kernel(up, dn, edge_ref, totals_in, w_ref, bias_in, down_in, totals_ref, carry_ref, *scratch):
    pairs = [(ref.at[:, 0], scratch[1].at[side]) for side, ref in enumerate((up, dn))]
    edge_taps(pairs, lambda side, n: exists(side), 2, edge_ref, totals_in, w_ref, bias_in, down_in, scratch)
    totals, d_ref, sems = scratch[-3:]
    (moved,) = copies([(totals, totals_ref)], sems)
    carry_ref[...] = fold(totals[2], d_ref)
    moved.wait()


def early_edge_kernel(up, dn, corner, edge_ref, totals_in, w_ref, bias_in, down_in, down_bias_ref, out_ref, *scratch):
    pairs = []
    for side, ref in enumerate((up, dn)):
        pairs += [(corner.at[:, side], scratch[1].at[side, :2]), (ref.at[:2, 0], scratch[1].at[side, 2:])]
    edge_taps(
        pairs, lambda side, n: exists(side) & exists(2) if n < 2 else exists(side), 0, edge_ref, totals_in, w_ref, bias_in,
        down_in, scratch,
    )
    totals, d_ref = scratch[-3:-1]
    latent_bias = down_bias_ref[...].reshape(1, -1)
    latent_bias = jnp.concatenate([latent_bias] * 4, axis=1)
    for t in range(2):
        out_ref[t] = fold(totals[t], d_ref) + latent_bias


def on_device(feature, conv_weight, conv_bias, down_weight, down_bias):
    frames, height, width, channels = feature.shape
    z = down_bias.shape[0]
    n_tm, n_row = lax.axis_size("tm"), lax.axis_size("row")
    tm, row = lax.axis_index("tm"), lax.axis_index("row")
    quarter, lanes = width // 4, 8 * z

    def shifted(value, by_tm, by_row):
        pairs = [
            (t * n_row + r, (t + by_tm) % n_tm * n_row + (r + by_row) % n_row) for t in range(n_tm) for r in range(n_row)
        ]
        return lax.ppermute(value, AXES, pairs)

    hbm_ref, halo_ref = pl.BlockSpec(memory_space=pltpu.HBM), pl.BlockSpec(memory_space=HALO)
    vmem = pl.BlockSpec(memory_space=pltpu.VMEM)

    def in_hbm(value):
        return pltpu.with_memory_space_constraint(value, pltpu.HBM)

    def call(kernel, name, units, ins, specs, outs, out_specs, scratch, copied):
        return pl.pallas_call(
            kernel,
            in_specs=specs,
            out_specs=out_specs,
            out_shape=outs,
            scratch_shapes=[*scratch, pltpu.SemaphoreType.DMA((copied,))],
            compiler_params=pltpu.CompilerParams(vmem_limit_bytes=VMEM_LIMIT),
            cost_estimate=pl.CostEstimate(
                flops=units * width * 6 * channels * channels, bytes_accessed=4_000_000, transcendentals=0
            ),
            name=name,
        )(*[in_hbm(i) if spec is hbm_ref else i for i, spec in zip(ins, specs)])

    up, dn, earlier = call(
        send_kernel, "send", 1, (feature,), [hbm_ref],
        [
            pltpu.HBM((frames, 1, width, channels), BF16), pltpu.HBM((frames, 1, width, channels), BF16),
            pltpu.HBM((2, height, width, channels), BF16),
        ],
        [hbm_ref] * 3, [], 3,
    )
    up = shifted(up, 0, 1)
    dn = shifted(dn, 0, -1)
    earlier = shifted(earlier, 1, 0)

    down = down_weight.transpose(0, 1, 2, 4, 3)
    totals_shape = (3, lanes, width)
    kept = call(
        own_kernel, "own", 90, (feature, conv_weight, conv_bias, down), [hbm_ref] * 4,
        [
            pltpu.VMEM((height, frames, channels, width), F32), pltpu.VMEM(conv_weight.shape, BF16),
            pltpu.VMEM((channels, width), F32), pltpu.VMEM(down.shape, BF16), pltpu.VMEM(totals_shape, F32),
        ],
        [vmem] * 5,
        [
            pltpu.VMEM(feature.shape, BF16), pltpu.VMEM(conv_bias.shape, F32),
            pltpu.VMEM((height, frames, width, 3 * channels), BF16),
        ], 12,
    )
    edges, totals = call(
        earlier_kernel, "earlier", 30, (earlier, *kept), [halo_ref] + [vmem] * 5,
        [pltpu.HBM((2, frames, channels, width), F32), pltpu.HBM(totals_shape, F32)], [hbm_ref] * 2,
        [
            pltpu.VMEM(earlier.shape, BF16), pltpu.VMEM((height, 2, channels, width), F32), pltpu.VMEM(totals_shape, F32),
            pltpu.VMEM((height, 2, width, 3 * channels), BF16),
        ], 6,
    )
    up, dn, totals = lax.optimization_barrier((up, dn, totals))
    (corner,) = call(
        relay_kernel, "relay", 1, (up, dn), [halo_ref, halo_ref],
        [pltpu.HBM((2, 2, width, channels), BF16)], [hbm_ref], [], 2,
    )
    corner = shifted(corner, 1, 0)
    edge_scratch = [
        pltpu.VMEM((2, 2, channels, width), F32), pltpu.VMEM((2, 4, width, channels), BF16),
        pltpu.VMEM((6, 3, channels, channels), BF16), pltpu.VMEM((2, 4, width, 3 * channels), BF16),
        pltpu.VMEM(conv_bias.shape, F32), pltpu.VMEM(down.shape, BF16), pltpu.VMEM(totals_shape, F32),
        pltpu.VMEM((width, lanes), F32),
    ]
    totals, carry = call(
        late_edge_kernel, "late_edges", 12, (up, dn, edges, totals, conv_weight, conv_bias, down),
        [halo_ref, halo_ref] + [hbm_ref] * 5,
        [pltpu.HBM(totals_shape, F32), jax.ShapeDtypeStruct((quarter, 4 * z), F32)], [hbm_ref, vmem], edge_scratch, 14,
    )
    carry = shifted(carry, 1, 0)
    (out,) = call(
        early_edge_kernel, "early_edges", 12, (up, dn, corner, edges, totals, conv_weight, conv_bias, down, down_bias),
        [halo_ref] * 3 + [hbm_ref] * 5 + [vmem],
        [jax.ShapeDtypeStruct((2, quarter, 4 * z), F32)], [vmem], edge_scratch, 14,
    )

    half = n_row // 2

    def routed(value, slot):
        pairs = []
        for t in range(n_tm):
            for r in range(n_row):
                target = r // 2 if (r % 2 == 0) == (slot == 0) else half + r // 2
                pairs.append((t * n_row + r, t * n_row + target))
        return lax.ppermute(value, AXES, pairs)

    first = out[0] + jnp.where(tm > 0, carry, 0.0)
    last = out[1]
    is_even = row % 2 == 0
    got_a = routed(jnp.where(is_even, first, last), 0)
    got_b = routed(jnp.where(is_even, last, first), 1)
    low = row < half
    return jnp.concatenate([jnp.where(low, got_a, got_b), jnp.where(low, got_b, got_a)], axis=0)


def solution(mesh):
    return jax.shard_map(
        on_device,
        mesh=mesh,
        in_specs=(P("tm", "row", None, None), P(), P(), P(), P()),
        out_specs=P(AXES, None),
        check_vma=False,
    )
```

time: 73.7 us -> 110 us (1.49)
  Pallas kernels: 34.7 us -> 88.8 us
  local copies, waits for them, and re-layouts: 19.1 us -> 0.01 us
  waiting for transfers between devices: 5.22 us -> 7.19 us
    pallas_call x5 -> x6, Pallas kernels: 34.7 us -> 88.8 us  [call(): pl.pallas_call(kernel, in_specs=specs, out_specs=out_specs, out_shape=out...]
    unnamed x30 -> x2, local copies, waits for them, and re-layouts: 17.4 us -> 0.01 us
    ppermute x5, waiting for transfers between devices: 0.38 us -> 2.86 us  [shifted(): return lax.ppermute(value, AXES, pairs)]
    ppermute x2, starting transfers between devices: 4.36 us -> 5.99 us  [routed(): return lax.ppermute(value, AXES, pairs)]
    ppermute x5, starting transfers between devices: 7.7 us -> 6.18 us  [shifted(): return lax.ppermute(value, AXES, pairs)]
  transfers between devices with their start and end apart: 7 -> 7, of which waited for: 2 -> 3; matrix products, arithmetic and copies ran while one was open for 1% -> 0% of each run, Pallas kernels for 46% -> 36%
where the time goes in v4:
time: 110 us; the launch traced here: 109 us
  Pallas kernels  88.8 us (81%)
  starting transfers between devices  12.2 us (11%)
  waiting for transfers between devices  7.19 us (7%)
    pallas_call x6, Pallas kernels, call(): pl.pallas_call(kernel, in_specs=specs, out_specs=out_specs, out_shape=out...  88.8 us
    ppermute x5, starting transfers between devices, shifted(): return lax.ppermute(value, AXES, pairs)  6.18 us
    ppermute x2, starting transfers between devices, routed(): return lax.ppermute(value, AXES, pairs)  5.99 us
    ppermute x2, waiting for transfers between devices, routed(): return lax.ppermute(value, AXES, pairs)  4.34 us
    ppermute x5, waiting for transfers between devices, shifted(): return lax.ppermute(value, AXES, pairs)  2.86 us
  transfers between devices with their start and end apart: 7, of which 3 were waited for; matrix products, arithmetic and copies ran while one was open for 0% of the time, Pallas kernels for 36%

profile of v4, /device:TPU:8, one launch (start us, length us, event | category | flops | bytes accessed | tf_op | source)
XLA Modules:
  0.0 108.9 jit_solution(14045555473493279560)
XLA Ops:
  0.0 48.8 %send.1 = (bf16[4,1,128,384]{3,2,1,0:T(8,128)(2,1)}, bf16[4,1,128,384]{3,2,1,0:T(8,128)(2,1)}, bf16[2,4,128,384]{3,2,1,0:T(8,128)(2,1)}) custom-call(bf16[4,4,128,384]{3,2,1,0:T(8,128)(2,1)} %x_ref.3), custom_call_target="tpu_custom_call" | custom-call | flops 113246208 | bytes 4000000 | tf_op jit(solution)/shard_map/send/pallas_call | solution.py:258
  48.8 2.4 %collective-permute-start = (bf16[4,1,128,384]{3,2,1,0:T(8,128)(2,1)}, bf16[4,1,128,384]{3,2,1,0:T(8,128)(2,1)S(1)}, u32[]{:S(2)}, u32[]{:S(2)}) collective-permute-start(bf16[4,1,128,384]{3,2,1,0:T(8,128)(2,1)} %get-tuple-element.20), channel_id=1, source_target_pairs={{0,1},{1,2},{2,3},{3,4},{4,5},{5,6},{6,7},{7,0},{8,9},{9,10},{10,1... | collective-permute-start | bytes 1179656 | tf_op jit(solution)/shard_map/ppermute | solution.py:249
  51.1 3.6 %collective-permute-start.1 = (bf16[4,1,128,384]{3,2,1,0:T(8,128)(2,1)}, bf16[4,1,128,384]{3,2,1,0:T(8,128)(2,1)S(1)}, u32[]{:S(2)}, u32[]{:S(2)}) collective-permute-start(bf16[4,1,128,384]{3,2,1,0:T(8,128)(2,1)} %get-tuple-element.21), channel_id=1, source_target_pairs={{0,7},{1,0},{2,1},{3,2},{4,3},{5,4},{6,5},{7,6},{8,15},{9,8},{10,9... | collective-permute-start | bytes 1179656 | tf_op jit(solution)/shard_map/ppermute | solution.py:249
  54.7 0.0 collective-permute-start.2
  54.7 17.2 %own.1 = (f32[4,4,384,128]{3,2,1,0:T(8,128)S(1)}, bf16[3,3,3,384,384]{4,3,2,1,0:T(8,128)(2,1)S(1)}, f32[384,128]{1,0:T(8,128)S(1)}, bf16[3,2,2,16,384]{4,3,2,1,0:T(8,128)(2,1)S(1)}, f32[3,128,128]{2,1,0:T(8,128)S(1)}) custom-call(bf16[4,4,128,384]{3,2,1,0:T(8,128)(2,1)} %x_ref.3, bf16[3,3,3,384,384]{4,3,2,1,0:T(8,128)(2,1)} %w_ref.5, f32[384]{0:T(512)} %bias_in.5, ...), custom_call_target="tpu_custom_call" | custom-call | flops 10192158720 | bytes 4000000 | tf_op jit(solution)/shard_map/own/pallas_call | solution.py:258
  71.9 0.0 collective-permute-done.2.x_ref
  71.9 6.1 %earlier.1 = (f32[2,4,384,128]{3,2,1,0:T(8,128)}, f32[3,128,128]{2,1,0:T(8,128)}) custom-call(bf16[2,4,128,384]{3,2,1,0:T(8,128)(2,1)S(1)} %collective-permute-done.2.x_ref, f32[4,4,384,128]{3,2,1,0:T(8,128)S(1)} %get-tuple-element.23.acc_in, bf16[3,3,3,384,384]{4,3,2,1,0:T(8,128)(2,1)S(1)} %get-tuple-element.24.weights, ...), custom_call_target="tpu_custom_call" | custom-call | flops 3397386240 | bytes 4000000 | tf_op jit(solution)/shard_map/earlier/pallas_call | solution.py:258
  78.0 0.0 collective-permute-done.up
  78.0 1.6 %collective-permute-done.1.dn = bf16[4,1,128,384]{3,2,1,0:T(8,128)(2,1)S(1)} collective-permute-done((bf16[4,1,128,384]{3,2,1,0:T(8,128)(2,1)}, bf16[4,1,128,384]{3,2,1,0:T(8,128)(2,1)S(1)}, u32[]{:S(2)}, u32[]{:S(2)}) %collective-permute-start.1) | collective-permute-done | bytes 393248 | tf_op jit(solution)/shard_map/ppermute | solution.py:249
  79.6 0.8 relay.1
  80.4 0.1 collective-permute-start.3
  80.5 0.0 copy-start
  80.5 8.1 %late_edges.1 = (f32[3,128,128]{2,1,0:T(8,128)}, f32[32,64]{1,0:T(8,128)S(1)}) custom-call(bf16[4,1,128,384]{3,2,1,0:T(8,128)(2,1)S(1)} %collective-permute-done.up, bf16[4,1,128,384]{3,2,1,0:T(8,128)(2,1)S(1)} %collective-permute-done.1.dn, f32[2,4,384,128]{3,2,1,0:T(8,128)} %get-tuple-element.31.edge_ref, f32[3,128,128]{2,1,0:T(8,128)} %get-tuple-element.32.totals_in, ...), custom_call_target="tpu_custom_call" | custom-call | flops 1358954496 | bytes 4000000 | tf_op jit(solution)/shard_map/late_edges/pallas_call | solution.py:258
  88.6 0.1 collective-permute-start.4
  88.7 1.3 %collective-permute-done.3.corner = bf16[2,2,128,384]{3,2,1,0:T(8,128)(2,1)S(1)} collective-permute-done((bf16[2,2,128,384]{3,2,1,0:T(8,128)(2,1)}, bf16[2,2,128,384]{3,2,1,0:T(8,128)(2,1)S(1)}, u32[]{:S(2)}, u32[]{:S(2)}) %collective-permute-start.3) | collective-permute-done | bytes 393248 | tf_op jit(solution)/shard_map/ppermute | solution.py:249
  90.0 0.0 copy-done
  90.0 7.9 %early_edges.1 = f32[2,32,64]{2,1,0:T(8,128)S(1)} custom-call(bf16[4,1,128,384]{3,2,1,0:T(8,128)(2,1)S(1)} %collective-permute-done.up, bf16[4,1,128,384]{3,2,1,0:T(8,128)(2,1)S(1)} %collective-permute-done.1.dn, bf16[2,2,128,384]{3,2,1,0:T(8,128)(2,1)S(1)} %collective-permute-done.3.corner, f32[2,4,384,128]{3,2,1,0:T(8,128)} %get-tuple-element.31.edge_ref, ...), custom_call_target="tpu_custom_call" | custom-call | flops 1358954496 | bytes 4000000 | tf_op jit(solution)/shard_map/early_edges/pallas_call | solution.py:258
  97.9 0.0 collective-permute-done.4
  97.9 0.7 collective-permute-start.5
  98.6 5.3 %collective-permute-start.6 = (f32[32,64]{1,0:T(8,128)S(1)}, f32[32,64]{1,0:T(8,128)S(1)}, u32[]{:S(2)}, u32[]{:S(2)}) collective-permute-start(f32[32,64]{1,0:T(8,128)S(1)} %get-tuple-element.36), channel_id=1, source_target_pairs={{0,4},{1,0},{2,5},{3,1},{4,6},{5,2},{6,7},{7,3},{8,12},{9,8},{10,1... | collective-permute-start | bytes 24584 | tf_op jit(solution)/shard_map/ppermute | solution.py:337
  103.9 0.0 collective-permute-done.5
  103.9 4.3 %collective-permute-done.6 = f32[32,64]{1,0:T(8,128)S(1)} collective-permute-done((f32[32,64]{1,0:T(8,128)S(1)}, f32[32,64]{1,0:T(8,128)S(1)}, u32[]{:S(2)}, u32[]{:S(2)}) %collective-permute-start.6) | collective-permute-done | bytes 8224 | tf_op jit(solution)/shard_map/ppermute | solution.py:337
  108.3 0.6 pad_maximum_fusion
  (2 shorter events, 0.0 us)
Async XLA Ops:
  48.8 29.3 %collective-permute-start = (bf16[4,1,128,384]{3,2,1,0:T(8,128)(2,1)}, bf16[4,1,128,384]{3,2,1,0:T(8,128)(2,1)S(1)}, u32[]{:S(2)}, u32[]{:S(2)}) collective-permute-start(bf16[4,1,128,384]{3,2,1,0:T(8,128)(2,1)} %get-tuple-element.20), channel_id=1, source_target_pairs={{0,1},{1,2},{2,3},{3,4},{4,5},{5,6},{6,7},{7,0},{8,9},{9,10},{10,1... | collective-permute-start | bytes 1179656 | tf_op jit(solution)/shard_map/ppermute | solution.py:249
  51.1 28.5 %collective-permute-start.1 = (bf16[4,1,128,384]{3,2,1,0:T(8,128)(2,1)}, bf16[4,1,128,384]{3,2,1,0:T(8,128)(2,1)S(1)}, u32[]{:S(2)}, u32[]{:S(2)}) collective-permute-start(bf16[4,1,128,384]{3,2,1,0:T(8,128)(2,1)} %get-tuple-element.21), channel_id=1, source_target_pairs={{0,7},{1,0},{2,1},{3,2},{4,3},{5,4},{6,5},{7,6},{8,15},{9,8},{10,9... | collective-permute-start | bytes 1179656 | tf_op jit(solution)/shard_map/ppermute | solution.py:249
  54.7 17.2 %collective-permute-start.2 = (bf16[2,4,128,384]{3,2,1,0:T(8,128)(2,1)}, bf16[2,4,128,384]{3,2,1,0:T(8,128)(2,1)S(1)}, u32[]{:S(2)}, u32[]{:S(2)}) collective-permute-start(bf16[2,4,128,384]{3,2,1,0:T(8,128)(2,1)} %get-tuple-element.22), channel_id=1, source_target_pairs={{0,8},{1,9},{2,10},{3,11},{4,12},{5,13},{6,14},{7,15},{8,16},{9,17... | collective-permute-start | bytes 2359304 | tf_op jit(solution)/shard_map/ppermute | solution.py:249
  80.4 9.6 %collective-permute-start.3 = (bf16[2,2,128,384]{3,2,1,0:T(8,128)(2,1)}, bf16[2,2,128,384]{3,2,1,0:T(8,128)(2,1)S(1)}, u32[]{:S(2)}, u32[]{:S(2)}) collective-permute-start(bf16[2,2,128,384]{3,2,1,0:T(8,128)(2,1)} %relay.1), channel_id=1, source_target_pairs={{0,8},{1,9},{2,10},{3,11},{4,12},{5,13},{6,14},{7,15},{8,16},{9,17... | collective-permute-start | bytes 1179656 | tf_op jit(solution)/shard_map/ppermute | solution.py:249
  80.5 9.5 %copy-start = (f32[16]{0:T(128)S(1)}, f32[16]{0:T(128)}, u32[]{:S(2)}) copy-start(f32[16]{0:T(128)} %down_bias_ref.1) | copy-start | bytes 196
  88.6 9.3 %collective-permute-start.4 = (f32[32,64]{1,0:T(8,128)S(1)}, f32[32,64]{1,0:T(8,128)S(1)}, u32[]{:S(2)}, u32[]{:S(2)}) collective-permute-start(f32[32,64]{1,0:T(8,128)S(1)} %get-tuple-element.34), channel_id=1, source_target_pairs={{0,8},{1,9},{2,10},{3,11},{4,12},{5,13},{6,14},{7,15},{8,16},{9,17... | collective-permute-start | bytes 24584 | tf_op jit(solution)/shard_map/ppermute | solution.py:249
  97.9 6.0 %collective-permute-start.5 = (f32[32,64]{1,0:T(8,128)S(1)}, f32[32,64]{1,0:T(8,128)S(1)}, u32[]{:S(2)}, u32[]{:S(2)}) collective-permute-start(f32[32,64]{1,0:T(8,128)S(1)} %get-tuple-element.35), channel_id=1, source_target_pairs={{0,0},{1,4},{2,1},{3,5},{4,2},{5,6},{6,3},{7,7},{8,8},{9,12},{10,9... | collective-permute-start | bytes 24584 | tf_op jit(solution)/shard_map/ppermute | solution.py:337
  98.6 9.7 %collective-permute-start.6 = (f32[32,64]{1,0:T(8,128)S(1)}, f32[32,64]{1,0:T(8,128)S(1)}, u32[]{:S(2)}, u32[]{:S(2)}) collective-permute-start(f32[32,64]{1,0:T(8,128)S(1)} %get-tuple-element.36), channel_id=1, source_target_pairs={{0,4},{1,0},{2,5},{3,1},{4,6},{5,2},{6,7},{7,3},{8,12},{9,8},{10,1... | collective-permute-start | bytes 24584 | tf_op jit(solution)/shard_map/ppermute | solution.py:337

commit v5 on v4

--- a/solution.py
+++ b/solution.py
@@ -7,7 +7,7 @@
 
 F32 = jnp.float32
 BF16 = jnp.bfloat16
-VMEM_LIMIT = 20 * 1024 * 1024
+VMEM_LIMIT = 24 * 1024 * 1024
 AXES = ("tm", "row")
 HALO = pl.ANY
 
@@ -26,10 +26,8 @@
 
 
 def tap_product(weight, positions):
-    channels = weight.shape[-1]
-    weight = weight.reshape(3 * channels, channels)
-    positions = positions.reshape(-1, 3 * channels)
-    return lax.dot_general(weight, positions, (((0,), (1,)), ((), ())), preferred_element_type=F32)
+    positions = positions.reshape(-1, weight.shape[1])
+    return lax.dot_general(weight, positions, (((1,), (1,)), ((), ())), preferred_element_type=F32)
 
 
 def projected(pre, bias, down_ref, f, rows):
@@ -106,47 +104,56 @@
         copy.wait()
 
 
-def own_kernel(x_ref, w_ref, bias_in, down_in, acc, weights, bias_ref, down_ref, totals, rows_in, bias_row, wide, sems):
+def own_kernel(
+    x_ref, w_ref, bias_in, down_in, acc, weights, bias_ref, down_ref, totals, edge_weights, rows_in, staged, bias_row, wide, sems
+):
     frames, height, width, channels = x_ref.shape
     order = [(a, b) for a in (2, 1, 0) for b in (1, 0, 2)]
-    fetch = copies(
-        [(x_ref, rows_in)] + [(w_ref.at[t], weights.at[t]) for t in order] + [(bias_in, bias_row), (down_in, down_ref)], sems
-    )
-    fetch[0].wait()
-
-    def one(n, carry):
-        f, h = n // height, n % height
-        widen(rows_in[f, h], wide.at[h, f])
-        return carry
-
-    lax.fori_loop(0, frames * height, one, 0)
+    heavy = copies([(w_ref.at[order[0]], staged.at[order[0]])], sems, frames)
+    fetch = copies([(x_ref.at[f], rows_in.at[f]) for f in range(frames)], sems)
+    small = copies([(bias_in, bias_row), (down_in, down_ref)], sems, frames + 9)
+    heavy += copies([(w_ref.at[order[1]], staged.at[order[1]])], sems, frames + 1)
+    moved = []
     for n, (tap_time, tap_row) in enumerate(order):
-        fetch[1 + n].wait()
+        heavy[n].wait()
+        if n + 2 < len(order):
+            heavy += copies([(w_ref.at[order[n + 2]], staged.at[order[n + 2]])], sems, frames + n + 2)
+        weights[tap_time, tap_row] = staged[tap_time, tap_row].reshape(3 * channels, channels).T
+        if tap_row != 1:
+            moved += copies(
+                [(weights.at[tap_time, tap_row], edge_weights.at[tap_time, tap_row // 2])], sems, frames + 11 + len(moved)
+            )
+        if n == 0:
+            for f in range(frames):
+                fetch[f].wait()
+                for h in range(height):
+                    widen(rows_in[f, h], wide.at[h, f])
+                product = tap_product(weights[tap_time, tap_row], wide[:, f])
+                for h in range(height):
+                    acc[h, f] = product[:, h * width : (h + 1) * width]
+            continue
         count = frames - 2 + tap_time
         rows = tap_rows(tap_row, height)
         product = tap_product(weights[tap_time, tap_row], wide[rows[0] : rows[-1] + 1, :count])
         for m, h in enumerate(rows):
             for g in range(count):
                 first = (m * count + g) * width
-                value = product[:, first : first + width]
-                target = (h + 1 - tap_row, g + 2 - tap_time)
-                if n == 0:
-                    acc[target] = value
-                else:
-                    acc[target] += value
-    fetch[-2].wait()
-    fetch[-1].wait()
+                acc[h + 1 - tap_row, g + 2 - tap_time] += product[:, first : first + width]
+    for copy in small:
+        copy.wait()
     bias_ref[...] = jnp.broadcast_to(bias_row[...].reshape(1, channels), (width, channels)).T
     totals[...] = jnp.zeros_like(totals)
-    project_rows(acc, (2, 3), (1, 2), bias_ref, down_ref, totals)
-
-
-def project_rows(acc, frames, rows, bias_ref, down_ref, totals):
-    for f in frames:
-        found = projected([acc[i, f] for i in rows], bias_ref[...], down_ref, f, rows)
-        add_products(found, 1 + f % 2, totals.at[f // 2])
-        if f % 2 == 1:
-            add_products(found, 0, totals.at[f // 2 + 1])
+    for f in (2, 3):
+        project_rows([acc[i, f] for i in (1, 2)], f, (1, 2), bias_ref[...], down_ref, totals)
+    for copy in moved:
+        copy.wait()
+
+
+def project_rows(pre, f, rows, bias, down_ref, totals):
+    found = projected(pre, bias, down_ref, f, rows)
+    add_products(found, 1 + f % 2, totals.at[f // 2])
+    if f % 2 == 1:
+        add_products(found, 0, totals.at[f // 2 + 1])
 
 
 def earlier_kernel(x_ref, acc_in, weights, bias_ref, down_ref, totals_in, edge_ref, totals_ref, rows_in, acc, totals, wide, sems):
@@ -175,60 +182,74 @@
                     value = acc_in[target] if (tap_time, tap_row) == (0, 1) else acc[target]
                     acc[target] = value + product[:, first : first + width]
     moved += copies([(acc.at[side * (height - 1)], edge_ref.at[side, :2]) for side in range(2)], sems, 3)
-    project_rows(acc, (0, 1), (1, 2), bias_ref, down_ref, totals)
+    for f in (0, 1):
+        project_rows([acc[i, f] for i in (1, 2)], f, (1, 2), bias_ref[...], down_ref, totals)
     moved += copies([(totals, totals_ref)], sems, 5)
     for copy in moved:
         copy.wait()
 
 
-def edge_taps(pairs, keep, first, edge_ref, totals_in, w_ref, bias_in, down_in, scratch):
-    acc, rows_in, weights, wide, bias_row, down_ref, totals, d_ref, sems = scratch
-    width, channels = rows_in.shape[2:]
-    taps = [(a, side) for a in range(3) for side in range(2)]
-    brought = copies(pairs, sems)
-    heavy = copies([(w_ref.at[a, 2 * side], weights.at[n]) for n, (a, side) in enumerate(taps)], sems, 4)
-    rest = copies(
-        [(edge_ref.at[:, first : first + 2], acc), (totals_in, totals), (bias_in, bias_row), (down_in, down_ref)], sems, 10
-    )
+def rows_kernel(
+    up, dn, edge_in, w_ref, totals_in, bias_in, down_in, edge_ref, totals_ref, carry_ref,
+    edge, weights, bias_row, down_ref, totals, sides_in, sides, d_ref, sems,
+):
+    width, channels = sides_in.shape[2:]
+    order = [(a, side) for a in (2, 1, 0) for side in range(2)]
+    brought = copies([(ref.at[:, 0], sides_in.at[side]) for side, ref in enumerate((up, dn))], sems, 6)
+    heavy = copies([(w_ref.at[t], weights.at[n]) for n, t in enumerate(order[:2])], sems)
+    initial = copies([(edge_in.at[side], edge.at[side]) for side in range(2)], sems, 8)
+    heavy += copies([(w_ref.at[t], weights.at[n + 2]) for n, t in enumerate(order[2:])], sems, 2)
+    late = copies([(totals_in, totals), (bias_in, bias_row), (down_in, down_ref)], sems, 10)
+    for n, (tap_time, side) in enumerate(order):
+        count = tap_time + 2
+        if n < 2:
+            brought[side].wait()
+            for f in range(4):
+                widen(sides_in[side, f], sides.at[side, f], exists(side))
+        heavy[n].wait()
+        product = tap_product(weights[n], sides[side, :count])
+        if n < 2:
+            initial[side].wait()
+        for m in range(count):
+            edge[side, m + 2 - tap_time] += product[:, m * width : (m + 1) * width]
+    moved = copies([(edge.at[side, :2], edge_ref.at[side]) for side in range(2)], sems)
+    for copy in late:
+        copy.wait()
+    bias = jnp.broadcast_to(bias_row[...].reshape(1, channels), (width, channels)).T
+    for f in (2, 3):
+        project_rows([edge[side, f] for side in range(2)], f, (0, 3), bias, down_ref, totals)
+    moved += copies([(totals, totals_ref)], sems, 2)
+    carry_ref[...] = fold(totals[2], d_ref)
+    for copy in moved:
+        copy.wait()
+
+
+def corner_kernel(
+    corner, edge_in, w_ref, totals_in, bias_in, down_in, down_bias_ref, out_ref,
+    edge, weights, bias_row, down_ref, totals, sides_in, sides, d_ref, sems,
+):
+    width, channels = sides_in.shape[2:]
+    order = [(a, side) for a in range(2) for side in range(2)]
+    brought = copies([(corner.at[:, side], sides_in.at[side]) for side in range(2)], sems)
+    heavy = copies([(w_ref.at[a, side], weights.at[a, side]) for a, side in order], sems, 2)
+    rest = copies([(edge_in, edge), (totals_in, totals), (bias_in, bias_row), (down_in, down_ref)], sems, 6)
     for copy in brought:
         copy.wait()
     for side in range(2):
-        for n in range(4):
-            widen(rows_in[side, n], wide.at[side, n], keep(side, n))
-    rest[0].wait()
-    for n, (tap_time, side) in enumerate(taps):
+        for n in range(2):
+            widen(sides_in[side, n], sides.at[side, n], exists(side) & exists(2))
+    for n, (tap_time, side) in enumerate(order):
         heavy[n].wait()
-        product = tap_product(weights[n], wide[side, tap_time : tap_time + 2])
-        for f in range(2):
-            acc[side, f] += product[:, f * width : (f + 1) * width]
+        product = tap_product(weights[tap_time, side], sides[side, tap_time:])
+        if n == 0:
+            rest[0].wait()
+        for f in range(2 - tap_time):
+            edge[side, f] += product[:, f * width : (f + 1) * width]
     for copy in rest[1:]:
         copy.wait()
     bias = jnp.broadcast_to(bias_row[...].reshape(1, channels), (width, channels)).T
-    for f in (first, first + 1):
-        found = projected([acc[side, f - first] for side in range(2)], bias, down_ref, f, (0, 3))
-        add_products(found, 1 + f % 2, totals.at[f // 2])
-        if f % 2 == 1:
-            add_products(found, 0, totals.at[f // 2 + 1])
-
-
-def late_edge_kernel(up, dn, edge_ref, totals_in, w_ref, bias_in, down_in, totals_ref, carry_ref, *scratch):
-    pairs = [(ref.at[:, 0], scratch[1].at[side]) for side, ref in enumerate((up, dn))]
-    edge_taps(pairs, lambda side, n: exists(side), 2, edge_ref, totals_in, w_ref, bias_in, down_in, scratch)
-    totals, d_ref, sems = scratch[-3:]
-    (moved,) = copies([(totals, totals_ref)], sems)
-    carry_ref[...] = fold(totals[2], d_ref)
-    moved.wait()
-
-
-def early_edge_kernel(up, dn, corner, edge_ref, totals_in, w_ref, bias_in, down_in, down_bias_ref, out_ref, *scratch):
-    pairs = []
-    for side, ref in enumerate((up, dn)):
-        pairs += [(corner.at[:, side], scratch[1].at[side, :2]), (ref.at[:2, 0], scratch[1].at[side, 2:])]
-    edge_taps(
-        pairs, lambda side, n: exists(side) & exists(2) if n < 2 else exists(side), 0, edge_ref, totals_in, w_ref, bias_in,
-        down_in, scratch,
-    )
-    totals, d_ref = scratch[-3:-1]
+    for f in (0, 1):
+        project_rows([edge[side, f] for side in range(2)], f, (0, 3), bias, down_ref, totals)
     latent_bias = down_bias_ref[...].reshape(1, -1)
     latent_bias = jnp.concatenate([latent_bias] * 4, axis=1)
     for t in range(2):
@@ -271,10 +292,10 @@
     up, dn, earlier = call(
         send_kernel, "send", 1, (feature,), [hbm_ref],
         [
-            pltpu.HBM((frames, 1, width, channels), BF16), pltpu.HBM((frames, 1, width, channels), BF16),
-            pltpu.HBM((2, height, width, channels), BF16),
+            pltpu.VMEM((frames, 1, width, channels), BF16), pltpu.VMEM((frames, 1, width, channels), BF16),
+            pltpu.VMEM((2, height, width, channels), BF16),
         ],
-        [hbm_ref] * 3, [], 3,
+        [vmem] * 3, [], 3,
     )
     up = shifted(up, 0, 1)
     dn = shifted(dn, 0, -1)
@@ -282,17 +303,18 @@
 
     down = down_weight.transpose(0, 1, 2, 4, 3)
     totals_shape = (3, lanes, width)
-    kept = call(
+    *kept, edge_weights = call(
         own_kernel, "own", 90, (feature, conv_weight, conv_bias, down), [hbm_ref] * 4,
         [
-            pltpu.VMEM((height, frames, channels, width), F32), pltpu.VMEM(conv_weight.shape, BF16),
+            pltpu.VMEM((height, frames, channels, width), F32), pltpu.VMEM((3, 3, channels, 3 * channels), BF16),
             pltpu.VMEM((channels, width), F32), pltpu.VMEM(down.shape, BF16), pltpu.VMEM(totals_shape, F32),
+            pltpu.HBM((3, 2, channels, 3 * channels), BF16),
         ],
-        [vmem] * 5,
-        [
-            pltpu.VMEM(feature.shape, BF16), pltpu.VMEM(conv_bias.shape, F32),
+        [vmem] * 5 + [hbm_ref],
+        [
+            pltpu.VMEM(feature.shape, BF16), pltpu.VMEM(conv_weight.shape, BF16), pltpu.VMEM(conv_bias.shape, F32),
             pltpu.VMEM((height, frames, width, 3 * channels), BF16),
-        ], 12,
+        ], frames + 17,
     )
     edges, totals = call(
         earlier_kernel, "earlier", 30, (earlier, *kept), [halo_ref] + [vmem] * 5,
@@ -308,22 +330,27 @@
         [pltpu.HBM((2, 2, width, channels), BF16)], [hbm_ref], [], 2,
     )
     corner = shifted(corner, 1, 0)
-    edge_scratch = [
-        pltpu.VMEM((2, 2, channels, width), F32), pltpu.VMEM((2, 4, width, channels), BF16),
-        pltpu.VMEM((6, 3, channels, channels), BF16), pltpu.VMEM((2, 4, width, 3 * channels), BF16),
-        pltpu.VMEM(conv_bias.shape, F32), pltpu.VMEM(down.shape, BF16), pltpu.VMEM(totals_shape, F32),
-        pltpu.VMEM((width, lanes), F32),
-    ]
-    totals, carry = call(
-        late_edge_kernel, "late_edges", 12, (up, dn, edges, totals, conv_weight, conv_bias, down),
-        [halo_ref, halo_ref] + [hbm_ref] * 5,
-        [pltpu.HBM(totals_shape, F32), jax.ShapeDtypeStruct((quarter, 4 * z), F32)], [hbm_ref, vmem], edge_scratch, 14,
+    edge_shape = (2, 2, channels, width)
+    small = [pltpu.VMEM(conv_bias.shape, F32), pltpu.VMEM(down.shape, BF16), pltpu.VMEM(totals_shape, F32)]
+    fold_space = pltpu.VMEM((width, lanes), F32)
+    edges, totals, carry = call(
+        rows_kernel, "rows", 18, (up, dn, edges, edge_weights, totals, conv_bias, down), [halo_ref] * 2 + [hbm_ref] * 5,
+        [pltpu.HBM(edge_shape, F32), pltpu.HBM(totals_shape, F32), jax.ShapeDtypeStruct((quarter, 4 * z), F32)],
+        [hbm_ref, hbm_ref, vmem],
+        [
+            pltpu.VMEM((2, frames, channels, width), F32), pltpu.VMEM((6, channels, 3 * channels), BF16), *small,
+            pltpu.VMEM((2, frames, width, channels), BF16), pltpu.VMEM((2, frames, width, 3 * channels), BF16), fold_space,
+        ], 13,
     )
     carry = shifted(carry, 1, 0)
     (out,) = call(
-        early_edge_kernel, "early_edges", 12, (up, dn, corner, edges, totals, conv_weight, conv_bias, down, down_bias),
-        [halo_ref] * 3 + [hbm_ref] * 5 + [vmem],
-        [jax.ShapeDtypeStruct((2, quarter, 4 * z), F32)], [vmem], edge_scratch, 14,
+        corner_kernel, "corners", 6, (corner, edges, edge_weights, totals, conv_bias, down, down_bias),
+        [halo_ref] + [hbm_ref] * 5 + [vmem],
+        [jax.ShapeDtypeStruct((2, quarter, 4 * z), F32)], [vmem],
+        [
+            pltpu.VMEM(edge_shape, F32), pltpu.VMEM((2, 2, channels, 3 * channels), BF16), *small,
+            pltpu.VMEM((2, 2, width, channels), BF16), pltpu.VMEM((2, 2, width, 3 * channels), BF16), fold_space,
+        ], 10,
     )
 
     half = n_row // 2

time: 110 us -> 59.2 us (0.54)
  Pallas kernels: 88.8 us -> 38.4 us
    pallas_call x6, Pallas kernels: 88.8 us -> 38.4 us  [call(): pl.pallas_call(kernel, in_specs=specs, out_specs=out_specs, out_shape=out...]
  transfers between devices with their start and end apart: 7 -> 7, of which waited for: 3 -> 3; matrix products, arithmetic and copies ran while one was open for 0% -> 0% of each run, Pallas kernels for 36% -> 62%
where the time goes in v5:
time: 59.2 us; the launch traced here: 58.5 us
  Pallas kernels  38.4 us (65%)
  starting transfers between devices  12.5 us (21%)
  waiting for transfers between devices  6.82 us (12%)
  other arithmetic  0.64 us (1%)
    pallas_call x6, Pallas kernels, call(): pl.pallas_call(kernel, in_specs=specs, out_specs=out_specs, out_shape=out...  38.4 us
    ppermute x5, starting transfers between devices, shifted(): return lax.ppermute(value, AXES, pairs)  6.56 us
    ppermute x2, starting transfers between devices, routed(): return lax.ppermute(value, AXES, pairs)  5.98 us
    ppermute x2, waiting for transfers between devices, routed(): return lax.ppermute(value, AXES, pairs)  4.34 us
    ppermute x5, waiting for transfers between devices, shifted(): return lax.ppermute(value, AXES, pairs)  2.48 us
  transfers between devices with their start and end apart: 7, of which 3 were waited for; matrix products, arithmetic and copies ran while one was open for 0% of the time, Pallas kernels for 62%

profile of v5, /device:TPU:8, one launch (start us, length us, event | category | flops | bytes accessed | tf_op | source)
XLA Modules:
  0.0 58.5 jit_solution(6921012074475717770)
XLA Ops:
  0.0 1.4 %send.1 = (bf16[4,1,128,384]{3,2,1,0:T(8,128)(2,1)S(1)}, bf16[4,1,128,384]{3,2,1,0:T(8,128)(2,1)S(1)}, bf16[2,4,128,384]{3,2,1,0:T(8,128)(2,1)S(1)}) custom-call(bf16[4,4,128,384]{3,2,1,0:T(8,128)(2,1)} %x_ref.3), custom_call_target="tpu_custom_call" | custom-call | flops 113246208 | bytes 4000000 | tf_op jit(solution)/shard_map/send/pallas_call | solution.py:279
  1.4 2.4 %collective-permute-start = (bf16[4,1,128,384]{3,2,1,0:T(8,128)(2,1)S(1)}, bf16[4,1,128,384]{3,2,1,0:T(8,128)(2,1)S(1)}, u32[]{:S(2)}, u32[]{:S(2)}) collective-permute-start(bf16[4,1,128,384]{3,2,1,0:T(8,128)(2,1)S(1)} %get-tuple-element.22), channel_id=1, source_target_pairs={{0,1},{1,2},{2,3},{3,4},{4,5},{5,6},{6,7},{7,0},{8,9},{9,10},{10,1... | collective-permute-start | bytes 1179656 | tf_op jit(solution)/shard_map/ppermute | solution.py:270
  3.8 3.6 %collective-permute-start.1 = (bf16[4,1,128,384]{3,2,1,0:T(8,128)(2,1)S(1)}, bf16[4,1,128,384]{3,2,1,0:T(8,128)(2,1)S(1)}, u32[]{:S(2)}, u32[]{:S(2)}) collective-permute-start(bf16[4,1,128,384]{3,2,1,0:T(8,128)(2,1)S(1)} %get-tuple-element.23), channel_id=1, source_target_pairs={{0,7},{1,0},{2,1},{3,2},{4,3},{5,4},{6,5},{7,6},{8,15},{9,8},{10,9... | collective-permute-start | bytes 1179656 | tf_op jit(solution)/shard_map/ppermute | solution.py:270
  7.3 0.0 collective-permute-start.2
  7.3 17.4 %own.1 = (f32[4,4,384,128]{3,2,1,0:T(8,128)S(1)}, bf16[3,3,384,1152]{3,2,1,0:T(8,128)(2,1)S(1)}, f32[384,128]{1,0:T(8,128)S(1)}, bf16[3,2,2,16,384]{4,3,2,1,0:T(...) custom-call(bf16[4,4,128,384]{3,2,1,0:T(8,128)(2,1)} %x_ref.3, ...), custom_call_target="tpu_custom_call" | custom-call | flops 10192158720 | bytes 4000000 | tf_op jit(solution)/shard_map/own/pallas_call | solution.py:279
  24.7 0.0 collective-permute-done.2.x_ref
  24.7 6.1 %earlier.1 = (f32[2,4,384,128]{3,2,1,0:T(8,128)}, f32[3,128,128]{2,1,0:T(8,128)}) custom-call(bf16[2,4,128,384]{3,2,1,0:T(8,128)(2,1)S(1)} %collective-permute-done.2.x_ref, f32[4,4,384,128]{3,2,1,0:T(8,128)S(1)} %get-tuple-element.25.acc_in, bf16[3,3,384,1152]{3,2,1,0:T(8,128)(2,1)S(1)} %get-tuple-element.26.weights, ...), custom_call_target="tpu_custom_call" | custom-call | flops 3397386240 | bytes 4000000 | tf_op jit(solution)/shard_map/earlier/pallas_call | solution.py:279
  30.9 0.0 copy-start
  30.9 0.0 collective-permute-done.up
  30.9 1.1 %collective-permute-done.1.dn = bf16[4,1,128,384]{3,2,1,0:T(8,128)(2,1)S(1)} collective-permute-done((bf16[4,1,128,384]{3,2,1,0:T(8,128)(2,1)S(1)}, bf16[4,1,128,384]{3,2,1,0:T(8,128)(2,1)S(1)}, u32[]{:S(2)}, u32[]{:S(2)}) %collective-permute-start.1) | collective-permute-done | bytes 393248 | tf_op jit(solution)/shard_map/ppermute | solution.py:270
  32.0 0.8 %relay.1 = bf16[2,2,128,384]{3,2,1,0:T(8,128)(2,1)} custom-call(bf16[4,1,128,384]{3,2,1,0:T(8,128)(2,1)S(1)} %collective-permute-done.up, bf16[4,1,128,384]{3,2,1,0:T(8,128)(2,1)S(1)} %collective-permute-done.1.dn), custom_call_target="tpu_custom_call" | custom-call | flops 113246208 | bytes 4000000 | tf_op jit(solution)/shard_map/relay/pallas_call | solution.py:279
  32.8 0.5 collective-permute-start.3
  33.3 7.6 %rows.1 = (f32[2,2,384,128]{3,2,1,0:T(8,128)}, f32[3,128,128]{2,1,0:T(8,128)}, f32[32,64]{1,0:T(8,128)S(1)}) custom-call(bf16[4,1,128,384]{3,2,1,0:T(8,128)(2,1)S(1)} %collective-permute-done.up, bf16[4,1,128,384]{3,2,1,0:T(8,128)(2,1)S(1)} %collective-permute-done.1.dn, f32[2,4,384,128]{3,2,1,0:T(8,128)} %get-tuple-element.33.edge_in, ...), custom_call_target="tpu_custom_call" | custom-call | flops 2038431744 | bytes 4000000 | tf_op jit(solution)/shard_map/rows/pallas_call | solution.py:279
  41.0 0.1 collective-permute-start.4
  41.1 1.3 %collective-permute-done.3.corner = bf16[2,2,128,384]{3,2,1,0:T(8,128)(2,1)S(1)} collective-permute-done((bf16[2,2,128,384]{3,2,1,0:T(8,128)(2,1)}, bf16[2,2,128,384]{3,2,1,0:T(8,128)(2,1)S(1)}, u32[]{:S(2)}, u32[]{:S(2)}) %collective-permute-start.3) | collective-permute-done | bytes 393248 | tf_op jit(solution)/shard_map/ppermute | solution.py:270
  42.4 0.0 copy-done
  42.4 5.1 %corners.1 = f32[2,32,64]{2,1,0:T(8,128)S(1)} custom-call(bf16[2,2,128,384]{3,2,1,0:T(8,128)(2,1)S(1)} %collective-permute-done.3.corner, f32[2,2,384,128]{3,2,1,0:T(8,128)} %get-tuple-element.36.edge_in, bf16[3,2,384,1152]{3,2,1,0:T(8,128)(2,1)} %get-tuple-element.34.w_ref, f32[3,128,128]{2,1,0:T(8,128)} %get-tuple-element.37.totals_in, f32[384]{0:T(512)} %bias_in.5, ...), custom_call_target="tpu_custom_call" | custom-call | flops 679477248 | bytes 4000000 | tf_op jit(solution)/shard_map/corners/pallas_call | solution.py:279
  47.5 0.0 collective-permute-done.4
  47.5 0.7 %collective-permute-start.5 = (f32[32,64]{1,0:T(8,128)S(1)}, f32[32,64]{1,0:T(8,128)S(1)}, u32[]{:S(2)}, u32[]{:S(2)}) collective-permute-start(f32[32,64]{1,0:T(8,128)S(1)} %get-tuple-element.39), channel_id=1, source_target_pairs={{0,0},{1,4},{2,1},{3,5},{4,2},{5,6},{6,3},{7,7},{8,8},{9,12},{10,9... | collective-permute-start | bytes 24584 | tf_op jit(solution)/shard_map/ppermute | solution.py:364
  48.2 5.3 %collective-permute-start.6 = (f32[32,64]{1,0:T(8,128)S(1)}, f32[32,64]{1,0:T(8,128)S(1)}, u32[]{:S(2)}, u32[]{:S(2)}) collective-permute-start(f32[32,64]{1,0:T(8,128)S(1)} %get-tuple-element.40), channel_id=1, source_target_pairs={{0,4},{1,0},{2,5},{3,1},{4,6},{5,2},{6,7},{7,3},{8,12},{9,8},{10,1... | collective-permute-start | bytes 24584 | tf_op jit(solution)/shard_map/ppermute | solution.py:364
  53.5 0.0 collective-permute-done.5
  53.5 4.3 %collective-permute-done.6 = f32[32,64]{1,0:T(8,128)S(1)} collective-permute-done((f32[32,64]{1,0:T(8,128)S(1)}, f32[32,64]{1,0:T(8,128)S(1)}, u32[]{:S(2)}, u32[]{:S(2)}) %collective-permute-start.6) | collective-permute-done | bytes 8224 | tf_op jit(solution)/shard_map/ppermute | solution.py:364
  57.9 0.6 %pad_maximum_fusion = f32[64,64]{1,0:T(8,128)} fusion(f32[32,64]{1,0:T(8,128)S(1)} %get-tuple-element.42, f32[32,64]{1,0:T(8,128)S(1)} %get-tuple-element.41), kind=kLoop, calls=%fused_computation | loop fusion | flops 4096 | bytes 32768 | tf_op jit(solution)/shard_map/concatenate | solution.py:372
  (2 shorter events, 0.0 us)
Async XLA Ops:
  1.4 29.5 %collective-permute-start = (bf16[4,1,128,384]{3,2,1,0:T(8,128)(2,1)S(1)}, bf16[4,1,128,384]{3,2,1,0:T(8,128)(2,1)S(1)}, u32[]{:S(2)}, u32[]{:S(2)}) collective-permute-start(bf16[4,1,128,384]{3,2,1,0:T(8,128)(2,1)S(1)} %get-tuple-element.22), channel_id=1, source_target_pairs={{0,1},{1,2},{2,3},{3,4},{4,5},{5,6},{6,7},{7,0},{8,9},{9,10},{10,1... | collective-permute-start | bytes 1179656 | tf_op jit(solution)/shard_map/ppermute | solution.py:270
  3.8 28.3 %collective-permute-start.1 = (bf16[4,1,128,384]{3,2,1,0:T(8,128)(2,1)S(1)}, bf16[4,1,128,384]{3,2,1,0:T(8,128)(2,1)S(1)}, u32[]{:S(2)}, u32[]{:S(2)}) collective-permute-start(bf16[4,1,128,384]{3,2,1,0:T(8,128)(2,1)S(1)} %get-tuple-element.23), channel_id=1, source_target_pairs={{0,7},{1,0},{2,1},{3,2},{4,3},{5,4},{6,5},{7,6},{8,15},{9,8},{10,9... | collective-permute-start | bytes 1179656 | tf_op jit(solution)/shard_map/ppermute | solution.py:270
  7.3 17.4 %collective-permute-start.2 = (bf16[2,4,128,384]{3,2,1,0:T(8,128)(2,1)S(1)}, bf16[2,4,128,384]{3,2,1,0:T(8,128)(2,1)S(1)}, u32[]{:S(2)}, u32[]{:S(2)}) collective-permute-start(bf16[2,4,128,384]{3,2,1,0:T(8,128)(2,1)S(1)} %get-tuple-element.24), channel_id=1, source_target_pairs={{0,8},{1,9},{2,10},{3,11},{4,12},{5,13},{6,14},{7,15},{8,16},{9,17... | collective-permute-start | bytes 2359304 | tf_op jit(solution)/shard_map/ppermute | solution.py:270
  30.9 11.5 %copy-start = (f32[16]{0:T(128)S(1)}, f32[16]{0:T(128)}, u32[]{:S(2)}) copy-start(f32[16]{0:T(128)} %down_bias_ref.1) | copy-start | bytes 196
  32.8 9.6 %collective-permute-start.3 = (bf16[2,2,128,384]{3,2,1,0:T(8,128)(2,1)}, bf16[2,2,128,384]{3,2,1,0:T(8,128)(2,1)S(1)}, u32[]{:S(2)}, u32[]{:S(2)}) collective-permute-start(bf16[2,2,128,384]{3,2,1,0:T(8,128)(2,1)} %relay.1), channel_id=1, source_target_pairs={{0,8},{1,9},{2,10},{3,11},{4,12},{5,13},{6,14},{7,15},{8,16},{9,17... | collective-permute-start | bytes 1179656 | tf_op jit(solution)/shard_map/ppermute | solution.py:270
  41.0 6.5 %collective-permute-start.4 = (f32[32,64]{1,0:T(8,128)S(1)}, f32[32,64]{1,0:T(8,128)S(1)}, u32[]{:S(2)}, u32[]{:S(2)}) collective-permute-start(f32[32,64]{1,0:T(8,128)S(1)} %get-tuple-element.38), channel_id=1, source_target_pairs={{0,8},{1,9},{2,10},{3,11},{4,12},{5,13},{6,14},{7,15},{8,16},{9,17... | collective-permute-start | bytes 24584 | tf_op jit(solution)/shard_map/ppermute | solution.py:270
  47.5 6.0 %collective-permute-start.5 = (f32[32,64]{1,0:T(8,128)S(1)}, f32[32,64]{1,0:T(8,128)S(1)}, u32[]{:S(2)}, u32[]{:S(2)}) collective-permute-start(f32[32,64]{1,0:T(8,128)S(1)} %get-tuple-element.39), channel_id=1, source_target_pairs={{0,0},{1,4},{2,1},{3,5},{4,2},{5,6},{6,3},{7,7},{8,8},{9,12},{10,9... | collective-permute-start | bytes 24584 | tf_op jit(solution)/shard_map/ppermute | solution.py:364
  48.2 9.7 %collective-permute-start.6 = (f32[32,64]{1,0:T(8,128)S(1)}, f32[32,64]{1,0:T(8,128)S(1)}, u32[]{:S(2)}, u32[]{:S(2)}) collective-permute-start(f32[32,64]{1,0:T(8,128)S(1)} %get-tuple-element.40), channel_id=1, source_target_pairs={{0,4},{1,0},{2,5},{3,1},{4,6},{5,2},{6,7},{7,3},{8,12},{9,8},{10,1... | collective-permute-start | bytes 24584 | tf_op jit(solution)/shard_map/ppermute | solution.py:364

commit v6 on v5

--- a/solution.py
+++ b/solution.py
@@ -92,10 +92,13 @@
     return range(max(0, tap_row - 1), min(height, height + tap_row - 1))
 
 
+def up_kernel(x_ref, up_ref, sems):
+    (copy,) = copies([(x_ref.at[:, x_ref.shape[1] - 1 :], up_ref)], sems)
+    copy.wait()
+
+
 def send_kernel(x_ref, up_ref, dn_ref, late_ref, sems):
-    height = x_ref.shape[1]
-    pairs = [(x_ref.at[:, height - 1 :], up_ref), (x_ref.at[:, :1], dn_ref), (x_ref.at[2:], late_ref)]
-    for copy in copies(pairs, sems):
+    for copy in copies([(x_ref.at[:, :1], dn_ref), (x_ref.at[2:], late_ref)], sems):
         copy.wait()
 
 
@@ -191,15 +194,15 @@
 
 def rows_kernel(
     up, dn, edge_in, w_ref, totals_in, bias_in, down_in, edge_ref, totals_ref, carry_ref,
-    edge, weights, bias_row, down_ref, totals, sides_in, sides, d_ref, sems,
+    initial, edge, weights, bias_row, down_ref, totals, sides_in, sides, d_ref, sems,
 ):
     width, channels = sides_in.shape[2:]
     order = [(a, side) for a in (2, 1, 0) for side in range(2)]
-    brought = copies([(ref.at[:, 0], sides_in.at[side]) for side, ref in enumerate((up, dn))], sems, 6)
-    heavy = copies([(w_ref.at[t], weights.at[n]) for n, t in enumerate(order[:2])], sems)
-    initial = copies([(edge_in.at[side], edge.at[side]) for side in range(2)], sems, 8)
-    heavy += copies([(w_ref.at[t], weights.at[n + 2]) for n, t in enumerate(order[2:])], sems, 2)
-    late = copies([(totals_in, totals), (bias_in, bias_row), (down_in, down_ref)], sems, 10)
+    brought = copies([(up.at[:, 0], sides_in.at[0])], sems, 6)
+    heavy = copies([(w_ref.at[order[0]], weights.at[0])], sems)
+    brought += copies([(dn.at[:, 0], sides_in.at[1])], sems, 7)
+    heavy += copies([(w_ref.at[t], weights.at[n + 1]) for n, t in enumerate(order[1:3])], sems, 1)
+    late = []
     for n, (tap_time, side) in enumerate(order):
         count = tap_time + 2
         if n < 2:
@@ -207,17 +210,27 @@
             for f in range(4):
                 widen(sides_in[side, f], sides.at[side, f], exists(side))
         heavy[n].wait()
+        if n + 3 < len(order):
+            heavy += copies([(w_ref.at[order[n + 3]], weights.at[n + 3])], sems, n + 3)
+        if n == 1:
+            late = copies([(edge_in, initial), (totals_in, totals), (bias_in, bias_row), (down_in, down_ref)], sems, 8)
         product = tap_product(weights[n], sides[side, :count])
-        if n < 2:
-            initial[side].wait()
         for m in range(count):
-            edge[side, m + 2 - tap_time] += product[:, m * width : (m + 1) * width]
-    moved = copies([(edge.at[side, :2], edge_ref.at[side]) for side in range(2)], sems)
-    for copy in late:
-        copy.wait()
+            value = product[:, m * width : (m + 1) * width]
+            if n < 2:
+                edge[side, m] = value
+            else:
+                edge[side, m + 2 - tap_time] += value
+        if n == 3:
+            for copy in late:
+                copy.wait()
+            for s in range(2):
+                for f in range(2):
+                    edge[s, f] += initial[s, f]
+            moved = copies([(edge.at[s, :2], edge_ref.at[s]) for s in range(2)], sems)
     bias = jnp.broadcast_to(bias_row[...].reshape(1, channels), (width, channels)).T
     for f in (2, 3):
-        project_rows([edge[side, f] for side in range(2)], f, (0, 3), bias, down_ref, totals)
+        project_rows([edge[side, f] + initial[side, f] for side in range(2)], f, (0, 3), bias, down_ref, totals)
     moved += copies([(totals, totals_ref)], sems, 2)
     carry_ref[...] = fold(totals[2], d_ref)
     for copy in moved:
@@ -226,30 +239,34 @@
 
 def corner_kernel(
     corner, edge_in, w_ref, totals_in, bias_in, down_in, down_bias_ref, out_ref,
-    edge, weights, bias_row, down_ref, totals, sides_in, sides, d_ref, sems,
+    initial, edge, weights, bias_row, down_ref, totals, sides_in, sides, d_ref, sems,
 ):
     width, channels = sides_in.shape[2:]
     order = [(a, side) for a in range(2) for side in range(2)]
-    brought = copies([(corner.at[:, side], sides_in.at[side]) for side in range(2)], sems)
-    heavy = copies([(w_ref.at[a, side], weights.at[a, side]) for a, side in order], sems, 2)
-    rest = copies([(edge_in, edge), (totals_in, totals), (bias_in, bias_row), (down_in, down_ref)], sems, 6)
-    for copy in brought:
-        copy.wait()
-    for side in range(2):
-        for n in range(2):
-            widen(sides_in[side, n], sides.at[side, n], exists(side) & exists(2))
+    brought = copies([(corner.at[:, 0], sides_in.at[0])], sems)
+    heavy = copies([(w_ref.at[order[0]], weights.at[order[0]])], sems, 2)
+    brought += copies([(corner.at[:, 1], sides_in.at[1])], sems, 1)
+    heavy += copies([(w_ref.at[order[1]], weights.at[order[1]])], sems, 3)
+    heavy += copies([(w_ref.at[t], weights.at[t]) for t in order[2:]], sems, 4)
+    late = copies([(edge_in, initial), (totals_in, totals), (bias_in, bias_row), (down_in, down_ref)], sems, 6)
     for n, (tap_time, side) in enumerate(order):
+        if n < 2:
+            brought[side].wait()
+            for f in range(2):
+                widen(sides_in[side, f], sides.at[side, f], exists(side) & exists(2))
         heavy[n].wait()
         product = tap_product(weights[tap_time, side], sides[side, tap_time:])
-        if n == 0:
-            rest[0].wait()
         for f in range(2 - tap_time):
-            edge[side, f] += product[:, f * width : (f + 1) * width]
-    for copy in rest[1:]:
+            value = product[:, f * width : (f + 1) * width]
+            if tap_time == 0:
+                edge[side, f] = value
+            else:
+                edge[side, f] += value
+    for copy in late:
         copy.wait()
     bias = jnp.broadcast_to(bias_row[...].reshape(1, channels), (width, channels)).T
     for f in (0, 1):
-        project_rows([edge[side, f] for side in range(2)], f, (0, 3), bias, down_ref, totals)
+        project_rows([edge[side, f] + initial[side, f] for side in range(2)], f, (0, 3), bias, down_ref, totals)
     latent_bias = down_bias_ref[...].reshape(1, -1)
     latent_bias = jnp.concatenate([latent_bias] * 4, axis=1)
     for t in range(2):
@@ -289,15 +306,13 @@
             name=name,
         )(*[in_hbm(i) if spec is hbm_ref else i for i, spec in zip(ins, specs)])
 
-    up, dn, earlier = call(
-        send_kernel, "send", 1, (feature,), [hbm_ref],
-        [
-            pltpu.VMEM((frames, 1, width, channels), BF16), pltpu.VMEM((frames, 1, width, channels), BF16),
-            pltpu.VMEM((2, height, width, channels), BF16),
-        ],
-        [vmem] * 3, [], 3,
-    )
-    up = shifted(up, 0, 1)
+    edge_row = pltpu.VMEM((frames, 1, width, channels), BF16)
+    (up_row,) = call(up_kernel, "send_up", 0, (feature,), [hbm_ref], [edge_row], [vmem], [], 1)
+    up = shifted(up_row, 0, 1)
+    dn, earlier = call(
+        send_kernel, "send", 1, (feature, up_row), [hbm_ref, halo_ref],
+        [edge_row, pltpu.VMEM((2, height, width, channels), BF16)], [vmem] * 2, [], 2,
+    )
     dn = shifted(dn, 0, -1)
     earlier = shifted(earlier, 1, 0)
 
@@ -338,7 +353,7 @@
         [pltpu.HBM(edge_shape, F32), pltpu.HBM(totals_shape, F32), jax.ShapeDtypeStruct((quarter, 4 * z), F32)],
         [hbm_ref, hbm_ref, vmem],
         [
-            pltpu.VMEM((2, frames, channels, width), F32), pltpu.VMEM((6, channels, 3 * channels), BF16), *small,
+            *[pltpu.VMEM((2, frames, channels, width), F32)] * 2, pltpu.VMEM((6, channels, 3 * channels), BF16), *small,
             pltpu.VMEM((2, frames, width, channels), BF16), pltpu.VMEM((2, frames, width, 3 * channels), BF16), fold_space,
         ], 13,
     )
@@ -348,7 +363,7 @@
         [halo_ref] + [hbm_ref] * 5 + [vmem],
         [jax.ShapeDtypeStruct((2, quarter, 4 * z), F32)], [vmem],
         [
-            pltpu.VMEM(edge_shape, F32), pltpu.VMEM((2, 2, channels, 3 * channels), BF16), *small,
+            *[pltpu.VMEM(edge_shape, F32)] * 2, pltpu.VMEM((2, 2, channels, 3 * channels), BF16), *small,
             pltpu.VMEM((2, 2, width, channels), BF16), pltpu.VMEM((2, 2, width, 3 * channels), BF16), fold_space,
         ], 10,
     )

time: 59.2 us -> 58.3 us (0.985)
  waiting for transfers between devices: 6.82 us -> 5.03 us
  starting transfers between devices: 12.5 us -> 13.5 us
    ppermute x5, waiting for transfers between devices: 2.48 us -> 0.69 us  [shifted(): return lax.ppermute(value, AXES, pairs)]
    ppermute x5, starting transfers between devices: 6.56 us -> 7.7 us  [shifted(): return lax.ppermute(value, AXES, pairs)]
    pallas_call x6 -> x7, Pallas kernels: 38.4 us -> 38.3 us  [call(): pl.pallas_call(kernel, in_specs=specs, out_specs=out_specs, out_shape=out...]
  transfers between devices with their start and end apart: 7 -> 7, of which waited for: 3 -> 2; matrix products, arithmetic and copies ran while one was open for 0% -> 0% of each run, Pallas kernels for 62% -> 61%
where the time goes in v6:
time: 58.3 us; the launch traced here: 57.6 us
  Pallas kernels  38.3 us (66%)
  starting transfers between devices  13.5 us (23%)
  waiting for transfers between devices  5.03 us (9%)
  other arithmetic  0.64 us (1%)
    pallas_call x7, Pallas kernels, call(): pl.pallas_call(kernel, in_specs=specs, out_specs=out_specs, out_shape=out...  38.3 us
    ppermute x5, starting transfers between devices, shifted(): return lax.ppermute(value, AXES, pairs)  7.7 us
    ppermute x2, starting transfers between devices, routed(): return lax.ppermute(value, AXES, pairs)  5.84 us
    ppermute x2, waiting for transfers between devices, routed(): return lax.ppermute(value, AXES, pairs)  4.33 us
  transfers between devices with their start and end apart: 7, of which 2 were waited for; matrix products, arithmetic and copies ran while one was open for 0% of the time, Pallas kernels for 61%

profile of v6, /device:TPU:8, one launch (start us, length us, event | category | flops | bytes accessed | tf_op | source)
XLA Modules:
  0.0 57.6 jit_solution(9275202484375516624)
XLA Ops:
  0.0 1.0 %send_up.1.up_ref = bf16[4,1,128,384]{3,2,1,0:T(8,128)(2,1)S(1)} custom-call(bf16[4,4,128,384]{3,2,1,0:T(8,128)(2,1)} %x_ref.5), custom_call_target="tpu_custom_call" | custom-call | bytes 4000000 | tf_op jit(solution)/shard_map/send_up/pallas_call | solution.py:296
  1.0 2.4 %collective-permute-start = (bf16[4,1,128,384]{3,2,1,0:T(8,128)(2,1)S(1)}, bf16[4,1,128,384]{3,2,1,0:T(8,128)(2,1)S(1)}, u32[]{:S(2)}, u32[]{:S(2)}) collective-permute-start(bf16[4,1,128,384]{3,2,1,0:T(8,128)(2,1)S(1)} %send_up.1.up_ref), channel_id=1, source_target_pairs={{0,1},{1,2},{2,3},{3,4},{4,5},{5,6},{6,7},{7,0},{8,9},{9,10},{10,1... | collective-permute-start | bytes 1179656 | tf_op jit(solution)/shard_map/ppermute | solution.py:287
  3.4 1.3 %send.1 = (bf16[4,1,128,384]{3,2,1,0:T(8,128)(2,1)S(1)}, bf16[2,4,128,384]{3,2,1,0:T(8,128)(2,1)S(1)}) custom-call(bf16[4,4,128,384]{3,2,1,0:T(8,128)(2,1)} %x_ref.5, bf16[4,1,128,384]{3,2,1,0:T(8,128)(2,1)S(1)} %send_up.1.up_ref), custom_call_target="tpu_custom_call" | custom-call | flops 113246208 | bytes 4000000 | tf_op jit(solution)/shard_map/send/pallas_call | solution.py:296
  4.7 3.6 %collective-permute-start.1 = (bf16[4,1,128,384]{3,2,1,0:T(8,128)(2,1)S(1)}, bf16[4,1,128,384]{3,2,1,0:T(8,128)(2,1)S(1)}, u32[]{:S(2)}, u32[]{:S(2)}) collective-permute-start(bf16[4,1,128,384]{3,2,1,0:T(8,128)(2,1)S(1)} %get-tuple-element.21), channel_id=1, source_target_pairs={{0,7},{1,0},{2,1},{3,2},{4,3},{5,4},{6,5},{7,6},{8,15},{9,8},{10,9... | collective-permute-start | bytes 1179656 | tf_op jit(solution)/shard_map/ppermute | solution.py:287
  8.2 0.0 collective-permute-start.2
  8.2 17.4 %own.1 = (f32[4,4,384,128]{3,2,1,0:T(8,128)S(1)}, bf16[3,3,384,1152]{3,2,1,0:T(8,128)(2,1)S(1)}, f32[384,128]{1,0:T(8,128)S(1)}, bf16[3,2,2,16,384]{4,3,2,1,0:T(...) custom-call(bf16[4,4,128,384]{3,2,1,0:T(8,128)(2,1)} %x_ref.5, ...), custom_call_target="tpu_custom_call" | custom-call | flops 10192158720 | bytes 4000000 | tf_op jit(solution)/shard_map/own/pallas_call | solution.py:296
  25.6 0.0 collective-permute-done.2.x_ref
  25.6 6.1 %earlier.1 = (f32[2,4,384,128]{3,2,1,0:T(8,128)}, f32[3,128,128]{2,1,0:T(8,128)}) custom-call(bf16[2,4,128,384]{3,2,1,0:T(8,128)(2,1)S(1)} %collective-permute-done.2.x_ref, f32[4,4,384,128]{3,2,1,0:T(8,128)S(1)} %get-tuple-element.23.acc_in, bf16[3,3,384,1152]{3,2,1,0:T(8,128)(2,1)S(1)} %get-tuple-element.24.weights, ...), custom_call_target="tpu_custom_call" | custom-call | flops 3397386240 | bytes 4000000 | tf_op jit(solution)/shard_map/earlier/pallas_call | solution.py:296
  31.8 0.0 copy-start
  31.8 0.0 collective-permute-done.up
  31.8 0.0 collective-permute-done.1.dn
  31.8 0.8 %relay.1 = bf16[2,2,128,384]{3,2,1,0:T(8,128)(2,1)} custom-call(bf16[4,1,128,384]{3,2,1,0:T(8,128)(2,1)S(1)} %collective-permute-done.up, bf16[4,1,128,384]{3,2,1,0:T(8,128)(2,1)S(1)} %collective-permute-done.1.dn), custom_call_target="tpu_custom_call" | custom-call | flops 113246208 | bytes 4000000 | tf_op jit(solution)/shard_map/relay/pallas_call | solution.py:296
  32.6 1.7 %collective-permute-start.3 = (bf16[2,2,128,384]{3,2,1,0:T(8,128)(2,1)}, bf16[2,2,128,384]{3,2,1,0:T(8,128)(2,1)S(1)}, u32[]{:S(2)}, u32[]{:S(2)}) collective-permute-start(bf16[2,2,128,384]{3,2,1,0:T(8,128)(2,1)} %relay.1), channel_id=1, source_target_pairs={{0,8},{1,9},{2,10},{3,11},{4,12},{5,13},{6,14},{7,15},{8,16},{9,17... | collective-permute-start | bytes 1179656 | tf_op jit(solution)/shard_map/ppermute | solution.py:287
  34.2 7.1 %rows.1 = (f32[2,2,384,128]{3,2,1,0:T(8,128)}, f32[3,128,128]{2,1,0:T(8,128)}, f32[32,64]{1,0:T(8,128)S(1)}) custom-call(bf16[4,1,128,384]{3,2,1,0:T(8,128)(2,1)S(1)} %collective-permute-done.up, bf16[4,1,128,384]{3,2,1,0:T(8,128)(2,1)S(1)} %collective-permute-done.1.dn, f32[2,4,384,128]{3,2,1,0:T(8,128)} %get-tuple-element.31.edge_in, ...), custom_call_target="tpu_custom_call" | custom-call | flops 2038431744 | bytes 4000000 | tf_op jit(solution)/shard_map/rows/pallas_call | solution.py:296
  41.4 0.1 collective-permute-start.4
  41.5 0.7 %collective-permute-done.3.corner = bf16[2,2,128,384]{3,2,1,0:T(8,128)(2,1)S(1)} collective-permute-done((bf16[2,2,128,384]{3,2,1,0:T(8,128)(2,1)}, bf16[2,2,128,384]{3,2,1,0:T(8,128)(2,1)S(1)}, u32[]{:S(2)}, u32[]{:S(2)}) %collective-permute-start.3) | collective-permute-done | bytes 393248 | tf_op jit(solution)/shard_map/ppermute | solution.py:287
  42.2 0.0 copy-done
  42.2 4.6 %corners.1 = f32[2,32,64]{2,1,0:T(8,128)S(1)} custom-call(bf16[2,2,128,384]{3,2,1,0:T(8,128)(2,1)S(1)} %collective-permute-done.3.corner, f32[2,2,384,128]{3,2,1,0:T(8,128)} %get-tuple-element.34.edge_in, bf16[3,2,384,1152]{3,2,1,0:T(8,128)(2,1)} %get-tuple-element.32.w_ref, f32[3,128,128]{2,1,0:T(8,128)} %get-tuple-element.35.totals_in, f32[384]{0:T(512)} %bias_in.5, ...), custom_call_target="tpu_custom_call" | custom-call | flops 679477248 | bytes 4000000 | tf_op jit(solution)/shard_map/corners/pallas_call | solution.py:296
  46.8 0.0 collective-permute-done.4
  46.8 0.7 %collective-permute-start.5 = (f32[32,64]{1,0:T(8,128)S(1)}, f32[32,64]{1,0:T(8,128)S(1)}, u32[]{:S(2)}, u32[]{:S(2)}) collective-permute-start(f32[32,64]{1,0:T(8,128)S(1)} %get-tuple-element.37), channel_id=1, source_target_pairs={{0,0},{1,4},{2,1},{3,5},{4,2},{5,6},{6,3},{7,7},{8,8},{9,12},{10,9... | collective-permute-start | bytes 24584 | tf_op jit(solution)/shard_map/ppermute | solution.py:379
  47.5 5.2 %collective-permute-start.6 = (f32[32,64]{1,0:T(8,128)S(1)}, f32[32,64]{1,0:T(8,128)S(1)}, u32[]{:S(2)}, u32[]{:S(2)}) collective-permute-start(f32[32,64]{1,0:T(8,128)S(1)} %get-tuple-element.38), channel_id=1, source_target_pairs={{0,4},{1,0},{2,5},{3,1},{4,6},{5,2},{6,7},{7,3},{8,12},{9,8},{10,1... | collective-permute-start | bytes 24584 | tf_op jit(solution)/shard_map/ppermute | solution.py:379
  52.6 0.0 collective-permute-done.5
  52.6 4.3 %collective-permute-done.6 = f32[32,64]{1,0:T(8,128)S(1)} collective-permute-done((f32[32,64]{1,0:T(8,128)S(1)}, f32[32,64]{1,0:T(8,128)S(1)}, u32[]{:S(2)}, u32[]{:S(2)}) %collective-permute-start.6) | collective-permute-done | bytes 8224 | tf_op jit(solution)/shard_map/ppermute | solution.py:379
  57.0 0.6 %pad_maximum_fusion = f32[64,64]{1,0:T(8,128)} fusion(f32[32,64]{1,0:T(8,128)S(1)} %get-tuple-element.40, f32[32,64]{1,0:T(8,128)S(1)} %get-tuple-element.39), kind=kLoop, calls=%fused_computation | loop fusion | flops 4096 | bytes 32768 | tf_op jit(solution)/shard_map/concatenate | solution.py:387
  (2 shorter events, 0.0 us)
Async XLA Ops:
  1.0 30.8 %collective-permute-start = (bf16[4,1,128,384]{3,2,1,0:T(8,128)(2,1)S(1)}, bf16[4,1,128,384]{3,2,1,0:T(8,128)(2,1)S(1)}, u32[]{:S(2)}, u32[]{:S(2)}) collective-permute-start(bf16[4,1,128,384]{3,2,1,0:T(8,128)(2,1)S(1)} %send_up.1.up_ref), channel_id=1, source_target_pairs={{0,1},{1,2},{2,3},{3,4},{4,5},{5,6},{6,7},{7,0},{8,9},{9,10},{10,1... | collective-permute-start | bytes 1179656 | tf_op jit(solution)/shard_map/ppermute | solution.py:287
  4.7 27.1 %collective-permute-start.1 = (bf16[4,1,128,384]{3,2,1,0:T(8,128)(2,1)S(1)}, bf16[4,1,128,384]{3,2,1,0:T(8,128)(2,1)S(1)}, u32[]{:S(2)}, u32[]{:S(2)}) collective-permute-start(bf16[4,1,128,384]{3,2,1,0:T(8,128)(2,1)S(1)} %get-tuple-element.21), channel_id=1, source_target_pairs={{0,7},{1,0},{2,1},{3,2},{4,3},{5,4},{6,5},{7,6},{8,15},{9,8},{10,9... | collective-permute-start | bytes 1179656 | tf_op jit(solution)/shard_map/ppermute | solution.py:287
  8.2 17.4 %collective-permute-start.2 = (bf16[2,4,128,384]{3,2,1,0:T(8,128)(2,1)S(1)}, bf16[2,4,128,384]{3,2,1,0:T(8,128)(2,1)S(1)}, u32[]{:S(2)}, u32[]{:S(2)}) collective-permute-start(bf16[2,4,128,384]{3,2,1,0:T(8,128)(2,1)S(1)} %get-tuple-element.22), channel_id=1, source_target_pairs={{0,8},{1,9},{2,10},{3,11},{4,12},{5,13},{6,14},{7,15},{8,16},{9,17... | collective-permute-start | bytes 2359304 | tf_op jit(solution)/shard_map/ppermute | solution.py:287
  31.8 10.4 %copy-start = (f32[16]{0:T(128)S(1)}, f32[16]{0:T(128)}, u32[]{:S(2)}) copy-start(f32[16]{0:T(128)} %down_bias_ref.1) | copy-start | bytes 196
  32.6 9.6 %collective-permute-start.3 = (bf16[2,2,128,384]{3,2,1,0:T(8,128)(2,1)}, bf16[2,2,128,384]{3,2,1,0:T(8,128)(2,1)S(1)}, u32[]{:S(2)}, u32[]{:S(2)}) collective-permute-start(bf16[2,2,128,384]{3,2,1,0:T(8,128)(2,1)} %relay.1), channel_id=1, source_target_pairs={{0,8},{1,9},{2,10},{3,11},{4,12},{5,13},{6,14},{7,15},{8,16},{9,17... | collective-permute-start | bytes 1179656 | tf_op jit(solution)/shard_map/ppermute | solution.py:287
  41.4 5.4 %collective-permute-start.4 = (f32[32,64]{1,0:T(8,128)S(1)}, f32[32,64]{1,0:T(8,128)S(1)}, u32[]{:S(2)}, u32[]{:S(2)}) collective-permute-start(f32[32,64]{1,0:T(8,128)S(1)} %get-tuple-element.36), channel_id=1, source_target_pairs={{0,8},{1,9},{2,10},{3,11},{4,12},{5,13},{6,14},{7,15},{8,16},{9,17... | collective-permute-start | bytes 24584 | tf_op jit(solution)/shard_map/ppermute | solution.py:287
  46.8 5.8 %collective-permute-start.5 = (f32[32,64]{1,0:T(8,128)S(1)}, f32[32,64]{1,0:T(8,128)S(1)}, u32[]{:S(2)}, u32[]{:S(2)}) collective-permute-start(f32[32,64]{1,0:T(8,128)S(1)} %get-tuple-element.37), channel_id=1, source_target_pairs={{0,0},{1,4},{2,1},{3,5},{4,2},{5,6},{6,3},{7,7},{8,8},{9,12},{10,9... | collective-permute-start | bytes 24584 | tf_op jit(solution)/shard_map/ppermute | solution.py:379
  47.5 9.5 %collective-permute-start.6 = (f32[32,64]{1,0:T(8,128)S(1)}, f32[32,64]{1,0:T(8,128)S(1)}, u32[]{:S(2)}, u32[]{:S(2)}) collective-permute-start(f32[32,64]{1,0:T(8,128)S(1)} %get-tuple-element.38), channel_id=1, source_target_pairs={{0,4},{1,0},{2,5},{3,1},{4,6},{5,2},{6,7},{7,3},{8,12},{9,8},{10,1... | collective-permute-start | bytes 24584 | tf_op jit(solution)/shard_map/ppermute | solution.py:379

commit v7 on v6

--- a/solution.py
+++ b/solution.py
@@ -111,7 +111,7 @@
     x_ref, w_ref, bias_in, down_in, acc, weights, bias_ref, down_ref, totals, edge_weights, rows_in, staged, bias_row, wide, sems
 ):
     frames, height, width, channels = x_ref.shape
-    order = [(a, b) for a in (2, 1, 0) for b in (1, 0, 2)]
+    order = [(2, 1), (2, 0), (2, 2), (1, 0), (1, 2), (1, 1), (0, 0), (0, 2), (0, 1)]
     heavy = copies([(w_ref.at[order[0]], staged.at[order[0]])], sems, frames)
     fetch = copies([(x_ref.at[f], rows_in.at[f]) for f in range(frames)], sems)
     small = copies([(bias_in, bias_row), (down_in, down_ref)], sems, frames + 9)
@@ -193,16 +193,15 @@
 
 
 def rows_kernel(
-    up, dn, edge_in, w_ref, totals_in, bias_in, down_in, edge_ref, totals_ref, carry_ref,
-    initial, edge, weights, bias_row, down_ref, totals, sides_in, sides, d_ref, sems,
+    up, dn, edge_in, w_ref, totals_in, bias_in, down_in, edge, weights, bias_ref, down_ref, totals, carry_ref,
+    initial, bias_row, sides_in, sides, d_ref, sems,
 ):
     width, channels = sides_in.shape[2:]
     order = [(a, side) for a in (2, 1, 0) for side in range(2)]
     brought = copies([(up.at[:, 0], sides_in.at[0])], sems, 6)
-    heavy = copies([(w_ref.at[order[0]], weights.at[0])], sems)
+    heavy = copies([(w_ref.at[order[0]], weights.at[order[0]])], sems)
     brought += copies([(dn.at[:, 0], sides_in.at[1])], sems, 7)
-    heavy += copies([(w_ref.at[t], weights.at[n + 1]) for n, t in enumerate(order[1:3])], sems, 1)
-    late = []
+    heavy += copies([(w_ref.at[t], weights.at[t]) for t in order[1:3]], sems, 1)
     for n, (tap_time, side) in enumerate(order):
         count = tap_time + 2
         if n < 2:
@@ -211,62 +210,46 @@
                 widen(sides_in[side, f], sides.at[side, f], exists(side))
         heavy[n].wait()
         if n + 3 < len(order):
-            heavy += copies([(w_ref.at[order[n + 3]], weights.at[n + 3])], sems, n + 3)
+            heavy += copies([(w_ref.at[order[n + 3]], weights.at[order[n + 3]])], sems, n + 3)
         if n == 1:
             late = copies([(edge_in, initial), (totals_in, totals), (bias_in, bias_row), (down_in, down_ref)], sems, 8)
-        product = tap_product(weights[n], sides[side, :count])
+        product = tap_product(weights[tap_time, side], sides[side, :count])
         for m in range(count):
             value = product[:, m * width : (m + 1) * width]
             if n < 2:
                 edge[side, m] = value
             else:
                 edge[side, m + 2 - tap_time] += value
-        if n == 3:
-            for copy in late:
-                copy.wait()
-            for s in range(2):
-                for f in range(2):
-                    edge[s, f] += initial[s, f]
-            moved = copies([(edge.at[s, :2], edge_ref.at[s]) for s in range(2)], sems)
+    for copy in late:
+        copy.wait()
+    for side in range(2):
+        for f in range(2):
+            edge[side, f] += initial[side, f]
     bias = jnp.broadcast_to(bias_row[...].reshape(1, channels), (width, channels)).T
+    bias_ref[...] = bias
     for f in (2, 3):
         project_rows([edge[side, f] + initial[side, f] for side in range(2)], f, (0, 3), bias, down_ref, totals)
-    moved += copies([(totals, totals_ref)], sems, 2)
     carry_ref[...] = fold(totals[2], d_ref)
-    for copy in moved:
-        copy.wait()
 
 
 def corner_kernel(
-    corner, edge_in, w_ref, totals_in, bias_in, down_in, down_bias_ref, out_ref,
-    initial, edge, weights, bias_row, down_ref, totals, sides_in, sides, d_ref, sems,
+    corner, edge_in, weights, bias_ref, down_ref, totals_in, down_bias_ref, out_ref, edge, totals, sides_in, sides, d_ref, sems
 ):
-    width, channels = sides_in.shape[2:]
-    order = [(a, side) for a in range(2) for side in range(2)]
-    brought = copies([(corner.at[:, 0], sides_in.at[0])], sems)
-    heavy = copies([(w_ref.at[order[0]], weights.at[order[0]])], sems, 2)
-    brought += copies([(corner.at[:, 1], sides_in.at[1])], sems, 1)
-    heavy += copies([(w_ref.at[order[1]], weights.at[order[1]])], sems, 3)
-    heavy += copies([(w_ref.at[t], weights.at[t]) for t in order[2:]], sems, 4)
-    late = copies([(edge_in, initial), (totals_in, totals), (bias_in, bias_row), (down_in, down_ref)], sems, 6)
-    for n, (tap_time, side) in enumerate(order):
-        if n < 2:
-            brought[side].wait()
-            for f in range(2):
-                widen(sides_in[side, f], sides.at[side, f], exists(side) & exists(2))
-        heavy[n].wait()
-        product = tap_product(weights[tap_time, side], sides[side, tap_time:])
-        for f in range(2 - tap_time):
-            value = product[:, f * width : (f + 1) * width]
+    width = sides_in.shape[2]
+    brought = copies([(corner.at[:, side], sides_in.at[side]) for side in range(2)], sems)
+    totals[...] = totals_in[...]
+    for tap_time in range(2):
+        for side in range(2):
             if tap_time == 0:
-                edge[side, f] = value
-            else:
-                edge[side, f] += value
-    for copy in late:
-        copy.wait()
-    bias = jnp.broadcast_to(bias_row[...].reshape(1, channels), (width, channels)).T
+                brought[side].wait()
+                for f in range(2):
+                    widen(sides_in[side, f], sides.at[side, f], exists(side) & exists(2))
+            product = tap_product(weights[tap_time, side], sides[side, tap_time:])
+            for f in range(2 - tap_time):
+                value = product[:, f * width : (f + 1) * width]
+                edge[side, f] = value + (edge_in[side, f] if tap_time == 0 else edge[side, f])
     for f in (0, 1):
-        project_rows([edge[side, f] + initial[side, f] for side in range(2)], f, (0, 3), bias, down_ref, totals)
+        project_rows([edge[side, f] for side in range(2)], f, (0, 3), bias_ref[...], down_ref, totals)
     latent_bias = down_bias_ref[...].reshape(1, -1)
     latent_bias = jnp.concatenate([latent_bias] * 4, axis=1)
     for t in range(2):
@@ -346,26 +329,28 @@
     )
     corner = shifted(corner, 1, 0)
     edge_shape = (2, 2, channels, width)
-    small = [pltpu.VMEM(conv_bias.shape, F32), pltpu.VMEM(down.shape, BF16), pltpu.VMEM(totals_shape, F32)]
     fold_space = pltpu.VMEM((width, lanes), F32)
-    edges, totals, carry = call(
+    *kept, carry = call(
         rows_kernel, "rows", 18, (up, dn, edges, edge_weights, totals, conv_bias, down), [halo_ref] * 2 + [hbm_ref] * 5,
-        [pltpu.HBM(edge_shape, F32), pltpu.HBM(totals_shape, F32), jax.ShapeDtypeStruct((quarter, 4 * z), F32)],
-        [hbm_ref, hbm_ref, vmem],
-        [
-            *[pltpu.VMEM((2, frames, channels, width), F32)] * 2, pltpu.VMEM((6, channels, 3 * channels), BF16), *small,
+        [
+            pltpu.VMEM((2, frames, channels, width), F32), pltpu.VMEM((3, 2, channels, 3 * channels), BF16),
+            pltpu.VMEM((channels, width), F32), pltpu.VMEM(down.shape, BF16), pltpu.VMEM(totals_shape, F32),
+            jax.ShapeDtypeStruct((quarter, 4 * z), F32),
+        ],
+        [vmem] * 6,
+        [
+            pltpu.VMEM((2, frames, channels, width), F32), pltpu.VMEM(conv_bias.shape, F32),
             pltpu.VMEM((2, frames, width, channels), BF16), pltpu.VMEM((2, frames, width, 3 * channels), BF16), fold_space,
-        ], 13,
+        ], 12,
     )
     carry = shifted(carry, 1, 0)
     (out,) = call(
-        corner_kernel, "corners", 6, (corner, edges, edge_weights, totals, conv_bias, down, down_bias),
-        [halo_ref] + [hbm_ref] * 5 + [vmem],
+        corner_kernel, "corners", 6, (corner, *kept, down_bias), [halo_ref] + [vmem] * 6,
         [jax.ShapeDtypeStruct((2, quarter, 4 * z), F32)], [vmem],
         [
-            *[pltpu.VMEM(edge_shape, F32)] * 2, pltpu.VMEM((2, 2, channels, 3 * channels), BF16), *small,
-            pltpu.VMEM((2, 2, width, channels), BF16), pltpu.VMEM((2, 2, width, 3 * channels), BF16), fold_space,
-        ], 10,
+            pltpu.VMEM(edge_shape, F32), pltpu.VMEM(totals_shape, F32), pltpu.VMEM((2, 2, width, channels), BF16),
+            pltpu.VMEM((2, 2, width, 3 * channels), BF16), fold_space,
+        ], 2,
     )
 
     half = n_row // 2

time: 58.3 us -> 56.4 us (0.967)
  Pallas kernels: 38.3 us -> 35.8 us
  waiting for transfers between devices: 5.03 us -> 7.3 us
  starting transfers between devices: 13.5 us -> 12.3 us
    pallas_call x7, Pallas kernels: 38.3 us -> 35.8 us  [call(): pl.pallas_call(kernel, in_specs=specs, out_specs=out_specs, out_shape=out...]
    ppermute x5, waiting for transfers between devices: 0.69 us -> 2.66 us  [shifted(): return lax.ppermute(value, AXES, pairs)]
    ppermute x2, starting transfers between devices: 5.84 us -> 4.61 us  [routed(): return lax.ppermute(value, AXES, pairs)]
  transfers between devices with their start and end apart: 7 -> 7, of which waited for: 2 -> 3; matrix products, arithmetic and copies ran while one was open for 0% -> 0% of each run, Pallas kernels for 61% -> 58%
where the time goes in v7:
time: 56.4 us; the launch traced here: 56.1 us
  Pallas kernels  35.8 us (63%)
  starting transfers between devices  12.3 us (22%)
  waiting for transfers between devices  7.3 us (13%)
  other arithmetic  0.63 us (1%)
    pallas_call x7, Pallas kernels, call(): pl.pallas_call(kernel, in_specs=specs, out_specs=out_specs, out_shape=out...  35.8 us
    ppermute x5, starting transfers between devices, shifted(): return lax.ppermute(value, AXES, pairs)  7.7 us
    ppermute x2, waiting for transfers between devices, routed(): return lax.ppermute(value, AXES, pairs)  4.64 us
    ppermute x2, starting transfers between devices, routed(): return lax.ppermute(value, AXES, pairs)  4.61 us
    ppermute x5, waiting for transfers between devices, shifted(): return lax.ppermute(value, AXES, pairs)  2.66 us
  transfers between devices with their start and end apart: 7, of which 3 were waited for; matrix products, arithmetic and copies ran while one was open for 0% of the time, Pallas kernels for 58%

profile of v7, /device:TPU:8, one launch (start us, length us, event | category | flops | bytes accessed | tf_op | source)
XLA Modules:
  0.0 56.1 jit_solution(1701131519347034997)
XLA Ops:
  0.0 1.0 %send_up.1.up_ref = bf16[4,1,128,384]{3,2,1,0:T(8,128)(2,1)S(1)} custom-call(bf16[4,4,128,384]{3,2,1,0:T(8,128)(2,1)} %x_ref.5), custom_call_target="tpu_custom_call" | custom-call | bytes 4000000 | tf_op jit(solution)/shard_map/send_up/pallas_call | solution.py:279
  1.0 2.4 %collective-permute-start = (bf16[4,1,128,384]{3,2,1,0:T(8,128)(2,1)S(1)}, bf16[4,1,128,384]{3,2,1,0:T(8,128)(2,1)S(1)}, u32[]{:S(2)}, u32[]{:S(2)}) collective-permute-start(bf16[4,1,128,384]{3,2,1,0:T(8,128)(2,1)S(1)} %send_up.1.up_ref), channel_id=1, source_target_pairs={{0,1},{1,2},{2,3},{3,4},{4,5},{5,6},{6,7},{7,0},{8,9},{9,10},{10,1... | collective-permute-start | bytes 1179656 | tf_op jit(solution)/shard_map/ppermute | solution.py:270
  3.4 1.3 %send.1 = (bf16[4,1,128,384]{3,2,1,0:T(8,128)(2,1)S(1)}, bf16[2,4,128,384]{3,2,1,0:T(8,128)(2,1)S(1)}) custom-call(bf16[4,4,128,384]{3,2,1,0:T(8,128)(2,1)} %x_ref.5, bf16[4,1,128,384]{3,2,1,0:T(8,128)(2,1)S(1)} %send_up.1.up_ref), custom_call_target="tpu_custom_call" | custom-call | flops 113246208 | bytes 4000000 | tf_op jit(solution)/shard_map/send/pallas_call | solution.py:279
  4.7 3.6 %collective-permute-start.1 = (bf16[4,1,128,384]{3,2,1,0:T(8,128)(2,1)S(1)}, bf16[4,1,128,384]{3,2,1,0:T(8,128)(2,1)S(1)}, u32[]{:S(2)}, u32[]{:S(2)}) collective-permute-start(bf16[4,1,128,384]{3,2,1,0:T(8,128)(2,1)S(1)} %get-tuple-element.24), channel_id=1, source_target_pairs={{0,7},{1,0},{2,1},{3,2},{4,3},{5,4},{6,5},{7,6},{8,15},{9,8},{10,9... | collective-permute-start | bytes 1179656 | tf_op jit(solution)/shard_map/ppermute | solution.py:270
  8.2 0.0 collective-permute-start.2
  8.2 17.3 %own.1 = (f32[4,4,384,128]{3,2,1,0:T(8,128)S(1)}, bf16[3,3,384,1152]{3,2,1,0:T(8,128)(2,1)S(1)}, f32[384,128]{1,0:T(8,128)S(1)}, bf16[3,2,2,16,384]{4,3,2,1,0:T(...) custom-call(bf16[4,4,128,384]{3,2,1,0:T(8,128)(2,1)} %x_ref.5, ...), custom_call_target="tpu_custom_call" | custom-call | flops 10192158720 | bytes 4000000 | tf_op jit(solution)/shard_map/own/pallas_call | solution.py:279
  25.5 0.0 collective-permute-done.2.x_ref
  25.5 6.1 %earlier.1 = (f32[2,4,384,128]{3,2,1,0:T(8,128)}, f32[3,128,128]{2,1,0:T(8,128)}) custom-call(bf16[2,4,128,384]{3,2,1,0:T(8,128)(2,1)S(1)} %collective-permute-done.2.x_ref, f32[4,4,384,128]{3,2,1,0:T(8,128)S(1)} %get-tuple-element.26.acc_in, bf16[3,3,384,1152]{3,2,1,0:T(8,128)(2,1)S(1)} %get-tuple-element.27.weights, ...), custom_call_target="tpu_custom_call" | custom-call | flops 3397386240 | bytes 4000000 | tf_op jit(solution)/shard_map/earlier/pallas_call | solution.py:279
  31.7 0.0 copy-start
  31.7 0.0 collective-permute-done.up
  31.7 0.0 collective-permute-done.1.dn
  31.7 0.8 %relay.1 = bf16[2,2,128,384]{3,2,1,0:T(8,128)(2,1)} custom-call(bf16[4,1,128,384]{3,2,1,0:T(8,128)(2,1)S(1)} %collective-permute-done.up, bf16[4,1,128,384]{3,2,1,0:T(8,128)(2,1)S(1)} %collective-permute-done.1.dn), custom_call_target="tpu_custom_call" | custom-call | flops 113246208 | bytes 4000000 | tf_op jit(solution)/shard_map/relay/pallas_call | solution.py:279
  32.5 1.7 %collective-permute-start.3 = (bf16[2,2,128,384]{3,2,1,0:T(8,128)(2,1)}, bf16[2,2,128,384]{3,2,1,0:T(8,128)(2,1)S(1)}, u32[]{:S(2)}, u32[]{:S(2)}) collective-permute-start(bf16[2,2,128,384]{3,2,1,0:T(8,128)(2,1)} %relay.1), channel_id=1, source_target_pairs={{0,8},{1,9},{2,10},{3,11},{4,12},{5,13},{6,14},{7,15},{8,16},{9,17... | collective-permute-start | bytes 1179656 | tf_op jit(solution)/shard_map/ppermute | solution.py:270
  34.1 6.7 %rows.1 = (f32[2,4,384,128]{3,2,1,0:T(8,128)S(1)}, bf16[3,2,384,1152]{3,2,1,0:T(8,128)(2,1)S(1)}, f32[384,128]{1,0:T(8,128)S(1)}, bf16[3,2,2,16,384]{4,3,2,1,0:T...) custom-call(bf16[4,1,128,384]{3,2,1,0:T(8,128)(2,1)S(1)} %collective-permute-done.up, ...), custom_call_target="tpu_custom_call" | custom-call | flops 2038431744 | bytes 4000000 | tf_op jit(solution)/shard_map/rows/pallas_call | solution.py:279
  40.9 0.1 collective-permute-start.4
  41.0 1.1 %collective-permute-done.3.corner = bf16[2,2,128,384]{3,2,1,0:T(8,128)(2,1)S(1)} collective-permute-done((bf16[2,2,128,384]{3,2,1,0:T(8,128)(2,1)}, bf16[2,2,128,384]{3,2,1,0:T(8,128)(2,1)S(1)}, u32[]{:S(2)}, u32[]{:S(2)}) %collective-permute-start.3) | collective-permute-done | bytes 393248 | tf_op jit(solution)/shard_map/ppermute | solution.py:270
  42.1 0.0 copy-done
  42.1 2.6 %corners.1 = f32[2,32,64]{2,1,0:T(8,128)S(1)} custom-call(bf16[2,2,128,384]{3,2,1,0:T(8,128)(2,1)S(1)} %collective-permute-done.3.corner, f32[2,4,384,128]{3,2,1,0:T(8,128)S(1)} %get-tuple-element.37.edge_in, bf16[3,2,384,1152]{3,2,1,0:T(8,128)(2,1)S(1)} %get-tuple-element.38.weights, f32[384,128]{1,0:T(8,128)S(1)} %get-tuple-element.39.bias_ref, ...), custom_call_target="tpu_custom_call" | custom-call | flops 679477248 | bytes 4000000 | tf_op jit(solution)/shard_map/corners/pallas_call | solution.py:279
  44.6 1.6 %collective-permute-done.4 = f32[32,64]{1,0:T(8,128)S(1)} collective-permute-done((f32[32,64]{1,0:T(8,128)S(1)}, f32[32,64]{1,0:T(8,128)S(1)}, u32[]{:S(2)}, u32[]{:S(2)}) %collective-permute-start.4) | collective-permute-done | bytes 8224 | tf_op jit(solution)/shard_map/ppermute | solution.py:270
  46.2 0.7 %collective-permute-start.5 = (f32[32,64]{1,0:T(8,128)S(1)}, f32[32,64]{1,0:T(8,128)S(1)}, u32[]{:S(2)}, u32[]{:S(2)}) collective-permute-start(f32[32,64]{1,0:T(8,128)S(1)} %get-tuple-element.43), channel_id=1, source_target_pairs={{0,0},{1,4},{2,1},{3,5},{4,2},{5,6},{6,3},{7,7},{8,8},{9,12},{10,9... | collective-permute-start | bytes 24584 | tf_op jit(solution)/shard_map/ppermute | solution.py:364
  46.9 4.0 %collective-permute-start.6 = (f32[32,64]{1,0:T(8,128)S(1)}, f32[32,64]{1,0:T(8,128)S(1)}, u32[]{:S(2)}, u32[]{:S(2)}) collective-permute-start(f32[32,64]{1,0:T(8,128)S(1)} %get-tuple-element.44), channel_id=1, source_target_pairs={{0,4},{1,0},{2,5},{3,1},{4,6},{5,2},{6,7},{7,3},{8,12},{9,8},{10,1... | collective-permute-start | bytes 24584 | tf_op jit(solution)/shard_map/ppermute | solution.py:364
  50.9 0.0 collective-permute-done.5
  50.9 4.6 %collective-permute-done.6 = f32[32,64]{1,0:T(8,128)S(1)} collective-permute-done((f32[32,64]{1,0:T(8,128)S(1)}, f32[32,64]{1,0:T(8,128)S(1)}, u32[]{:S(2)}, u32[]{:S(2)}) %collective-permute-start.6) | collective-permute-done | bytes 8224 | tf_op jit(solution)/shard_map/ppermute | solution.py:364
  55.5 0.6 %pad_maximum_fusion = f32[64,64]{1,0:T(8,128)} fusion(f32[32,64]{1,0:T(8,128)S(1)} %get-tuple-element.46, f32[32,64]{1,0:T(8,128)S(1)} %get-tuple-element.45), kind=kLoop, calls=%fused_computation | loop fusion | flops 4096 | bytes 32768 | tf_op jit(solution)/shard_map/concatenate | solution.py:372
  (2 shorter events, 0.0 us)
Async XLA Ops:
  1.0 30.7 %collective-permute-start = (bf16[4,1,128,384]{3,2,1,0:T(8,128)(2,1)S(1)}, bf16[4,1,128,384]{3,2,1,0:T(8,128)(2,1)S(1)}, u32[]{:S(2)}, u32[]{:S(2)}) collective-permute-start(bf16[4,1,128,384]{3,2,1,0:T(8,128)(2,1)S(1)} %send_up.1.up_ref), channel_id=1, source_target_pairs={{0,1},{1,2},{2,3},{3,4},{4,5},{5,6},{6,7},{7,0},{8,9},{9,10},{10,1... | collective-permute-start | bytes 1179656 | tf_op jit(solution)/shard_map/ppermute | solution.py:270
  4.7 27.0 %collective-permute-start.1 = (bf16[4,1,128,384]{3,2,1,0:T(8,128)(2,1)S(1)}, bf16[4,1,128,384]{3,2,1,0:T(8,128)(2,1)S(1)}, u32[]{:S(2)}, u32[]{:S(2)}) collective-permute-start(bf16[4,1,128,384]{3,2,1,0:T(8,128)(2,1)S(1)} %get-tuple-element.24), channel_id=1, source_target_pairs={{0,7},{1,0},{2,1},{3,2},{4,3},{5,4},{6,5},{7,6},{8,15},{9,8},{10,9... | collective-permute-start | bytes 1179656 | tf_op jit(solution)/shard_map/ppermute | solution.py:270
  8.2 17.3 %collective-permute-start.2 = (bf16[2,4,128,384]{3,2,1,0:T(8,128)(2,1)S(1)}, bf16[2,4,128,384]{3,2,1,0:T(8,128)(2,1)S(1)}, u32[]{:S(2)}, u32[]{:S(2)}) collective-permute-start(bf16[2,4,128,384]{3,2,1,0:T(8,128)(2,1)S(1)} %get-tuple-element.25), channel_id=1, source_target_pairs={{0,8},{1,9},{2,10},{3,11},{4,12},{5,13},{6,14},{7,15},{8,16},{9,17... | collective-permute-start | bytes 2359304 | tf_op jit(solution)/shard_map/ppermute | solution.py:270
  31.7 10.4 %copy-start = (f32[16]{0:T(128)S(1)}, f32[16]{0:T(128)}, u32[]{:S(2)}) copy-start(f32[16]{0:T(128)} %down_bias_ref.1) | copy-start | bytes 196
  32.5 9.6 %collective-permute-start.3 = (bf16[2,2,128,384]{3,2,1,0:T(8,128)(2,1)}, bf16[2,2,128,384]{3,2,1,0:T(8,128)(2,1)S(1)}, u32[]{:S(2)}, u32[]{:S(2)}) collective-permute-start(bf16[2,2,128,384]{3,2,1,0:T(8,128)(2,1)} %relay.1), channel_id=1, source_target_pairs={{0,8},{1,9},{2,10},{3,11},{4,12},{5,13},{6,14},{7,15},{8,16},{9,17... | collective-permute-start | bytes 1179656 | tf_op jit(solution)/shard_map/ppermute | solution.py:270
  40.9 5.3 %collective-permute-start.4 = (f32[32,64]{1,0:T(8,128)S(1)}, f32[32,64]{1,0:T(8,128)S(1)}, u32[]{:S(2)}, u32[]{:S(2)}) collective-permute-start(f32[32,64]{1,0:T(8,128)S(1)} %get-tuple-element.42), channel_id=1, source_target_pairs={{0,8},{1,9},{2,10},{3,11},{4,12},{5,13},{6,14},{7,15},{8,16},{9,17... | collective-permute-start | bytes 24584 | tf_op jit(solution)/shard_map/ppermute | solution.py:270
  46.2 4.6 %collective-permute-start.5 = (f32[32,64]{1,0:T(8,128)S(1)}, f32[32,64]{1,0:T(8,128)S(1)}, u32[]{:S(2)}, u32[]{:S(2)}) collective-permute-start(f32[32,64]{1,0:T(8,128)S(1)} %get-tuple-element.43), channel_id=1, source_target_pairs={{0,0},{1,4},{2,1},{3,5},{4,2},{5,6},{6,3},{7,7},{8,8},{9,12},{10,9... | collective-permute-start | bytes 24584 | tf_op jit(solution)/shard_map/ppermute | solution.py:364
  46.9 8.6 %collective-permute-start.6 = (f32[32,64]{1,0:T(8,128)S(1)}, f32[32,64]{1,0:T(8,128)S(1)}, u32[]{:S(2)}, u32[]{:S(2)}) collective-permute-start(f32[32,64]{1,0:T(8,128)S(1)} %get-tuple-element.44), channel_id=1, source_target_pairs={{0,4},{1,0},{2,5},{3,1},{4,6},{5,2},{6,7},{7,3},{8,12},{9,8},{10,1... | collective-permute-start | bytes 24584 | tf_op jit(solution)/shard_map/ppermute | solution.py:364

commit v8 on v7

--- a/solution.py
+++ b/solution.py
@@ -159,11 +159,13 @@
         add_products(found, 0, totals.at[f // 2 + 1])
 
 
-def earlier_kernel(x_ref, acc_in, weights, bias_ref, down_ref, totals_in, edge_ref, totals_ref, rows_in, acc, totals, wide, sems):
+def earlier_kernel(
+    x_ref, acc, weights, bias_ref, down_ref, totals_in, edge_ref, totals_ref, edge, totals, rows_in, inner, wide, sems
+):
     frames, height, width, channels = x_ref.shape
     (fetch,) = copies([(x_ref, rows_in)], sems)
-    moved = copies([(acc_in.at[side * (height - 1), 2:], edge_ref.at[side, 2:]) for side in range(2)], sems, 1)
-    totals[...] = totals_in[...]
+    moved = copies([(acc.at[side * (height - 1), 2:], edge_ref.at[side]) for side in range(2)] + [(totals_in, totals_ref)], sems, 1)
+    totals[...] = jnp.zeros_like(totals)
     keep = exists(2)
     fetch.wait()
 
@@ -181,13 +183,12 @@
             for m, h in enumerate(rows):
                 for f in range(count):
                     first = (m * count + f) * width
-                    target = (h + 1 - tap_row, f)
-                    value = acc_in[target] if (tap_time, tap_row) == (0, 1) else acc[target]
-                    acc[target] = value + product[:, first : first + width]
-    moved += copies([(acc.at[side * (height - 1)], edge_ref.at[side, :2]) for side in range(2)], sems, 3)
+                    value = product[:, first : first + width]
+                    i = h + 1 - tap_row
+                    ref, target = (edge, (i // (height - 1), f)) if i in (0, height - 1) else (inner, (i - 1, f))
+                    ref[target] = value + (acc[i, f] if (tap_time, tap_row) == (0, 1) else ref[target])
     for f in (0, 1):
-        project_rows([acc[i, f] for i in (1, 2)], f, (1, 2), bias_ref[...], down_ref, totals)
-    moved += copies([(totals, totals_ref)], sems, 5)
+        project_rows([inner[i, f] for i in range(2)], f, (1, 2), bias_ref[...], down_ref, totals)
     for copy in moved:
         copy.wait()
 
@@ -222,22 +223,20 @@
                 edge[side, m + 2 - tap_time] += value
     for copy in late:
         copy.wait()
-    for side in range(2):
-        for f in range(2):
-            edge[side, f] += initial[side, f]
     bias = jnp.broadcast_to(bias_row[...].reshape(1, channels), (width, channels)).T
     bias_ref[...] = bias
     for f in (2, 3):
-        project_rows([edge[side, f] + initial[side, f] for side in range(2)], f, (0, 3), bias, down_ref, totals)
+        project_rows([edge[side, f] + initial[side, f - 2] for side in range(2)], f, (0, 3), bias, down_ref, totals)
     carry_ref[...] = fold(totals[2], d_ref)
 
 
 def corner_kernel(
-    corner, edge_in, weights, bias_ref, down_ref, totals_in, down_bias_ref, out_ref, edge, totals, sides_in, sides, d_ref, sems
+    corner, edge_in, weights, bias_ref, down_ref, totals_in, edge_early, totals_early, down_bias_ref, out_ref,
+    edge, totals, sides_in, sides, d_ref, sems,
 ):
     width = sides_in.shape[2]
     brought = copies([(corner.at[:, side], sides_in.at[side]) for side in range(2)], sems)
-    totals[...] = totals_in[...]
+    totals[...] = totals_in[...] + totals_early[...]
     for tap_time in range(2):
         for side in range(2):
             if tap_time == 0:
@@ -247,7 +246,7 @@
             product = tap_product(weights[tap_time, side], sides[side, tap_time:])
             for f in range(2 - tap_time):
                 value = product[:, f * width : (f + 1) * width]
-                edge[side, f] = value + (edge_in[side, f] if tap_time == 0 else edge[side, f])
+                edge[side, f] = value + (edge_in[side, f] + edge_early[side, f] if tap_time == 0 else edge[side, f])
     for f in (0, 1):
         project_rows([edge[side, f] for side in range(2)], f, (0, 3), bias_ref[...], down_ref, totals)
     latent_bias = down_bias_ref[...].reshape(1, -1)
@@ -314,13 +313,14 @@
             pltpu.VMEM((height, frames, width, 3 * channels), BF16),
         ], frames + 17,
     )
-    edges, totals = call(
+    edge_shape = (2, 2, channels, width)
+    edges, totals, *from_earlier = call(
         earlier_kernel, "earlier", 30, (earlier, *kept), [halo_ref] + [vmem] * 5,
-        [pltpu.HBM((2, frames, channels, width), F32), pltpu.HBM(totals_shape, F32)], [hbm_ref] * 2,
-        [
-            pltpu.VMEM(earlier.shape, BF16), pltpu.VMEM((height, 2, channels, width), F32), pltpu.VMEM(totals_shape, F32),
-            pltpu.VMEM((height, 2, width, 3 * channels), BF16),
-        ], 6,
+        [pltpu.HBM(edge_shape, F32), pltpu.HBM(totals_shape, F32), pltpu.VMEM(edge_shape, F32), pltpu.VMEM(totals_shape, F32)],
+        [hbm_ref, hbm_ref, vmem, vmem],
+        [
+            pltpu.VMEM(earlier.shape, BF16), pltpu.VMEM(edge_shape, F32), pltpu.VMEM((height, 2, width, 3 * channels), BF16),
+        ], 4,
     )
     up, dn, totals = lax.optimization_barrier((up, dn, totals))
     (corner,) = call(
@@ -339,13 +339,13 @@
         ],
         [vmem] * 6,
         [
-            pltpu.VMEM((2, frames, channels, width), F32), pltpu.VMEM(conv_bias.shape, F32),
+            pltpu.VMEM(edge_shape, F32), pltpu.VMEM(conv_bias.shape, F32),
             pltpu.VMEM((2, frames, width, channels), BF16), pltpu.VMEM((2, frames, width, 3 * channels), BF16), fold_space,
         ], 12,
     )
     carry = shifted(carry, 1, 0)
     (out,) = call(
-        corner_kernel, "corners", 6, (corner, *kept, down_bias), [halo_ref] + [vmem] * 6,
+        corner_kernel, "corners", 6, (corner, *kept, *from_earlier, down_bias), [halo_ref] + [vmem] * 8,
         [jax.ShapeDtypeStruct((2, quarter, 4 * z), F32)], [vmem],
         [
             pltpu.VMEM(edge_shape, F32), pltpu.VMEM(totals_shape, F32), pltpu.VMEM((2, 2, width, channels), BF16),

time: 56.4 us -> 56.3 us (level)
  Pallas kernels: 35.8 us -> 35 us
    pallas_call x7, Pallas kernels: 35.8 us -> 35 us  [call(): pl.pallas_call(kernel, in_specs=specs, out_specs=out_specs, out_shape=out...]
    ppermute x5, waiting for transfers between devices: 2.66 us -> 3.35 us  [shifted(): return lax.ppermute(value, AXES, pairs)]
    ppermute x5, starting transfers between devices: 7.7 us -> 7.02 us  [shifted(): return lax.ppermute(value, AXES, pairs)]
    ppermute x2, starting transfers between devices: 4.61 us -> 5.2 us  [routed(): return lax.ppermute(value, AXES, pairs)]
  transfers between devices with their start and end apart: 7 -> 7, of which waited for: 3 -> 4; matrix products, arithmetic and copies ran while one was open for 0% -> 0% of each run, Pallas kernels for 58% -> 57%
where the time goes in v8:
time: 56.3 us; the launch traced here: 55.6 us
  Pallas kernels  35 us (62%)
  starting transfers between devices  12.2 us (22%)
  waiting for transfers between devices  7.69 us (14%)
  other arithmetic  0.63 us (1%)
    pallas_call x7, Pallas kernels, call(): pl.pallas_call(kernel, in_specs=specs, out_specs=out_specs, out_shape=out...  35 us
    ppermute x5, starting transfers between devices, shifted(): return lax.ppermute(value, AXES, pairs)  7.02 us
    ppermute x2, starting transfers between devices, routed(): return lax.ppermute(value, AXES, pairs)  5.2 us
    ppermute x2, waiting for transfers between devices, routed(): return lax.ppermute(value, AXES, pairs)  4.34 us
    ppermute x5, waiting for transfers between devices, shifted(): return lax.ppermute(value, AXES, pairs)  3.35 us
  transfers between devices with their start and end apart: 7, of which 4 were waited for; matrix products, arithmetic and copies ran while one was open for 0% of the time, Pallas kernels for 57%

profile of v8, /device:TPU:8, one launch (start us, length us, event | category | flops | bytes accessed | tf_op | source)
XLA Modules:
  0.0 55.6 jit_solution(3760195661051937254)
XLA Ops:
  0.0 1.0 %send_up.1.up_ref = bf16[4,1,128,384]{3,2,1,0:T(8,128)(2,1)S(1)} custom-call(bf16[4,4,128,384]{3,2,1,0:T(8,128)(2,1)} %x_ref.5), custom_call_target="tpu_custom_call" | custom-call | bytes 4000000 | tf_op jit(solution)/shard_map/send_up/pallas_call | solution.py:278
  1.0 2.4 %collective-permute-start = (bf16[4,1,128,384]{3,2,1,0:T(8,128)(2,1)S(1)}, bf16[4,1,128,384]{3,2,1,0:T(8,128)(2,1)S(1)}, u32[]{:S(2)}, u32[]{:S(2)}) collective-permute-start(bf16[4,1,128,384]{3,2,1,0:T(8,128)(2,1)S(1)} %send_up.1.up_ref), channel_id=1, source_target_pairs={{0,1},{1,2},{2,3},{3,4},{4,5},{5,6},{6,7},{7,0},{8,9},{9,10},{10,1... | collective-permute-start | bytes 1179656 | tf_op jit(solution)/shard_map/ppermute | solution.py:269
  3.4 1.3 %send.1 = (bf16[4,1,128,384]{3,2,1,0:T(8,128)(2,1)S(1)}, bf16[2,4,128,384]{3,2,1,0:T(8,128)(2,1)S(1)}) custom-call(bf16[4,4,128,384]{3,2,1,0:T(8,128)(2,1)} %x_ref.5, bf16[4,1,128,384]{3,2,1,0:T(8,128)(2,1)S(1)} %send_up.1.up_ref), custom_call_target="tpu_custom_call" | custom-call | flops 113246208 | bytes 4000000 | tf_op jit(solution)/shard_map/send/pallas_call | solution.py:278
  4.7 3.6 %collective-permute-start.1 = (bf16[4,1,128,384]{3,2,1,0:T(8,128)(2,1)S(1)}, bf16[4,1,128,384]{3,2,1,0:T(8,128)(2,1)S(1)}, u32[]{:S(2)}, u32[]{:S(2)}) collective-permute-start(bf16[4,1,128,384]{3,2,1,0:T(8,128)(2,1)S(1)} %get-tuple-element.26), channel_id=1, source_target_pairs={{0,7},{1,0},{2,1},{3,2},{4,3},{5,4},{6,5},{7,6},{8,15},{9,8},{10,9... | collective-permute-start | bytes 1179656 | tf_op jit(solution)/shard_map/ppermute | solution.py:269
  8.2 0.0 collective-permute-start.2
  8.2 17.3 %own.1 = (f32[4,4,384,128]{3,2,1,0:T(8,128)S(1)}, bf16[3,3,384,1152]{3,2,1,0:T(8,128)(2,1)S(1)}, f32[384,128]{1,0:T(8,128)S(1)}, bf16[3,2,2,16,384]{4,3,2,1,0:T(...) custom-call(bf16[4,4,128,384]{3,2,1,0:T(8,128)(2,1)} %x_ref.5, ...), custom_call_target="tpu_custom_call" | custom-call | flops 10192158720 | bytes 4000000 | tf_op jit(solution)/shard_map/own/pallas_call | solution.py:278
  25.5 0.0 collective-permute-done.2.x_ref
  25.5 5.4 %earlier.1 = (f32[2,2,384,128]{3,2,1,0:T(8,128)}, f32[3,128,128]{2,1,0:T(8,128)}, f32[2,2,384,128]{3,2,1,0:T(8,128)S(1)}, f32[3,128,128]{2,1,0:T(8,128)S(1)}) custom-call(bf16[2,4,128,384]{3,2,1,0:T(8,128)(2,1)S(1)} %collective-permute-done.2.x_ref, f32[4,4,384,128]{3,2,1,0:T(8,128)S(1)} %get-tuple-element.28.acc, ...), custom_call_target="tpu_custom_call" | custom-call | flops 3397386240 | bytes 4000000 | tf_op jit(solution)/shard_map/earlier/pallas_call | solution.py:278
  30.9 0.0 copy-start
  30.9 0.0 collective-permute-done.up
  31.0 0.7 %collective-permute-done.1.dn = bf16[4,1,128,384]{3,2,1,0:T(8,128)(2,1)S(1)} collective-permute-done((bf16[4,1,128,384]{3,2,1,0:T(8,128)(2,1)S(1)}, bf16[4,1,128,384]{3,2,1,0:T(8,128)(2,1)S(1)}, u32[]{:S(2)}, u32[]{:S(2)}) %collective-permute-start.1) | collective-permute-done | bytes 393248 | tf_op jit(solution)/shard_map/ppermute | solution.py:269
  31.6 0.8 %relay.1 = bf16[2,2,128,384]{3,2,1,0:T(8,128)(2,1)} custom-call(bf16[4,1,128,384]{3,2,1,0:T(8,128)(2,1)S(1)} %collective-permute-done.up, bf16[4,1,128,384]{3,2,1,0:T(8,128)(2,1)S(1)} %collective-permute-done.1.dn), custom_call_target="tpu_custom_call" | custom-call | flops 113246208 | bytes 4000000 | tf_op jit(solution)/shard_map/relay/pallas_call | solution.py:278
  32.4 1.0 %collective-permute-start.3 = (bf16[2,2,128,384]{3,2,1,0:T(8,128)(2,1)}, bf16[2,2,128,384]{3,2,1,0:T(8,128)(2,1)S(1)}, u32[]{:S(2)}, u32[]{:S(2)}) collective-permute-start(bf16[2,2,128,384]{3,2,1,0:T(8,128)(2,1)} %relay.1), channel_id=1, source_target_pairs={{0,8},{1,9},{2,10},{3,11},{4,12},{5,13},{6,14},{7,15},{8,16},{9,17... | collective-permute-start | bytes 1179656 | tf_op jit(solution)/shard_map/ppermute | solution.py:269
  33.4 6.7 %rows.1 = (f32[2,4,384,128]{3,2,1,0:T(8,128)S(1)}, bf16[3,2,384,1152]{3,2,1,0:T(8,128)(2,1)S(1)}, f32[384,128]{1,0:T(8,128)S(1)}, bf16[3,2,2,16,384]{4,3,2,1,0:T...) custom-call(bf16[4,1,128,384]{3,2,1,0:T(8,128)(2,1)S(1)} %collective-permute-done.up, ...), custom_call_target="tpu_custom_call" | custom-call | flops 2038431744 | bytes 4000000 | tf_op jit(solution)/shard_map/rows/pallas_call | solution.py:278
  40.1 0.1 collective-permute-start.4
  40.2 1.8 %collective-permute-done.3.corner = bf16[2,2,128,384]{3,2,1,0:T(8,128)(2,1)S(1)} collective-permute-done((bf16[2,2,128,384]{3,2,1,0:T(8,128)(2,1)}, bf16[2,2,128,384]{3,2,1,0:T(8,128)(2,1)S(1)}, u32[]{:S(2)}, u32[]{:S(2)}) %collective-permute-start.3) | collective-permute-done | bytes 393248 | tf_op jit(solution)/shard_map/ppermute | solution.py:269
  42.0 0.0 copy-done
  42.0 2.6 %corners.1 = f32[2,32,64]{2,1,0:T(8,128)S(1)} custom-call(bf16[2,2,128,384]{3,2,1,0:T(8,128)(2,1)S(1)} %collective-permute-done.3.corner, f32[2,4,384,128]{3,2,1,0:T(8,128)S(1)} %get-tuple-element.39.edge_in, bf16[3,2,384,1152]{3,2,1,0:T(8,128)(2,1)S(1)} %get-tuple-element.40.weights, f32[384,128]{1,0:T(8,128)S(1)} %get-tuple-element.41.bias_ref, ...), custom_call_target="tpu_custom_call" | custom-call | flops 679477248 | bytes 4000000 | tf_op jit(solution)/shard_map/corners/pallas_call | solution.py:278
  44.6 0.8 %collective-permute-done.4 = f32[32,64]{1,0:T(8,128)S(1)} collective-permute-done((f32[32,64]{1,0:T(8,128)S(1)}, f32[32,64]{1,0:T(8,128)S(1)}, u32[]{:S(2)}, u32[]{:S(2)}) %collective-permute-start.4) | collective-permute-done | bytes 8224 | tf_op jit(solution)/shard_map/ppermute | solution.py:269
  45.4 0.7 %collective-permute-start.5 = (f32[32,64]{1,0:T(8,128)S(1)}, f32[32,64]{1,0:T(8,128)S(1)}, u32[]{:S(2)}, u32[]{:S(2)}) collective-permute-start(f32[32,64]{1,0:T(8,128)S(1)} %get-tuple-element.47), channel_id=1, source_target_pairs={{0,0},{1,4},{2,1},{3,5},{4,2},{5,6},{6,3},{7,7},{8,8},{9,12},{10,9... | collective-permute-start | bytes 24584 | tf_op jit(solution)/shard_map/ppermute | solution.py:364
  46.1 4.5 %collective-permute-start.6 = (f32[32,64]{1,0:T(8,128)S(1)}, f32[32,64]{1,0:T(8,128)S(1)}, u32[]{:S(2)}, u32[]{:S(2)}) collective-permute-start(f32[32,64]{1,0:T(8,128)S(1)} %get-tuple-element.48), channel_id=1, source_target_pairs={{0,4},{1,0},{2,5},{3,1},{4,6},{5,2},{6,7},{7,3},{8,12},{9,8},{10,1... | collective-permute-start | bytes 24584 | tf_op jit(solution)/shard_map/ppermute | solution.py:364
  50.6 0.0 collective-permute-done.5
  50.6 4.3 %collective-permute-done.6 = f32[32,64]{1,0:T(8,128)S(1)} collective-permute-done((f32[32,64]{1,0:T(8,128)S(1)}, f32[32,64]{1,0:T(8,128)S(1)}, u32[]{:S(2)}, u32[]{:S(2)}) %collective-permute-start.6) | collective-permute-done | bytes 8224 | tf_op jit(solution)/shard_map/ppermute | solution.py:364
  55.0 0.6 %pad_maximum_fusion = f32[64,64]{1,0:T(8,128)} fusion(f32[32,64]{1,0:T(8,128)S(1)} %get-tuple-element.50, f32[32,64]{1,0:T(8,128)S(1)} %get-tuple-element.49), kind=kLoop, calls=%fused_computation | loop fusion | flops 4096 | bytes 32768 | tf_op jit(solution)/shard_map/concatenate | solution.py:372
  (2 shorter events, 0.0 us)
Async XLA Ops:
  1.0 29.9 %collective-permute-start = (bf16[4,1,128,384]{3,2,1,0:T(8,128)(2,1)S(1)}, bf16[4,1,128,384]{3,2,1,0:T(8,128)(2,1)S(1)}, u32[]{:S(2)}, u32[]{:S(2)}) collective-permute-start(bf16[4,1,128,384]{3,2,1,0:T(8,128)(2,1)S(1)} %send_up.1.up_ref), channel_id=1, source_target_pairs={{0,1},{1,2},{2,3},{3,4},{4,5},{5,6},{6,7},{7,0},{8,9},{9,10},{10,1... | collective-permute-start | bytes 1179656 | tf_op jit(solution)/shard_map/ppermute | solution.py:269
  4.7 27.0 %collective-permute-start.1 = (bf16[4,1,128,384]{3,2,1,0:T(8,128)(2,1)S(1)}, bf16[4,1,128,384]{3,2,1,0:T(8,128)(2,1)S(1)}, u32[]{:S(2)}, u32[]{:S(2)}) collective-permute-start(bf16[4,1,128,384]{3,2,1,0:T(8,128)(2,1)S(1)} %get-tuple-element.26), channel_id=1, source_target_pairs={{0,7},{1,0},{2,1},{3,2},{4,3},{5,4},{6,5},{7,6},{8,15},{9,8},{10,9... | collective-permute-start | bytes 1179656 | tf_op jit(solution)/shard_map/ppermute | solution.py:269
  8.2 17.3 %collective-permute-start.2 = (bf16[2,4,128,384]{3,2,1,0:T(8,128)(2,1)S(1)}, bf16[2,4,128,384]{3,2,1,0:T(8,128)(2,1)S(1)}, u32[]{:S(2)}, u32[]{:S(2)}) collective-permute-start(bf16[2,4,128,384]{3,2,1,0:T(8,128)(2,1)S(1)} %get-tuple-element.27), channel_id=1, source_target_pairs={{0,8},{1,9},{2,10},{3,11},{4,12},{5,13},{6,14},{7,15},{8,16},{9,17... | collective-permute-start | bytes 2359304 | tf_op jit(solution)/shard_map/ppermute | solution.py:269
  30.9 11.1 %copy-start = (f32[16]{0:T(128)S(1)}, f32[16]{0:T(128)}, u32[]{:S(2)}) copy-start(f32[16]{0:T(128)} %down_bias_ref.1) | copy-start | bytes 196
  32.4 9.6 %collective-permute-start.3 = (bf16[2,2,128,384]{3,2,1,0:T(8,128)(2,1)}, bf16[2,2,128,384]{3,2,1,0:T(8,128)(2,1)S(1)}, u32[]{:S(2)}, u32[]{:S(2)}) collective-permute-start(bf16[2,2,128,384]{3,2,1,0:T(8,128)(2,1)} %relay.1), channel_id=1, source_target_pairs={{0,8},{1,9},{2,10},{3,11},{4,12},{5,13},{6,14},{7,15},{8,16},{9,17... | collective-permute-start | bytes 1179656 | tf_op jit(solution)/shard_map/ppermute | solution.py:269
  40.1 5.3 %collective-permute-start.4 = (f32[32,64]{1,0:T(8,128)S(1)}, f32[32,64]{1,0:T(8,128)S(1)}, u32[]{:S(2)}, u32[]{:S(2)}) collective-permute-start(f32[32,64]{1,0:T(8,128)S(1)} %get-tuple-element.46), channel_id=1, source_target_pairs={{0,8},{1,9},{2,10},{3,11},{4,12},{5,13},{6,14},{7,15},{8,16},{9,17... | collective-permute-start | bytes 24584 | tf_op jit(solution)/shard_map/ppermute | solution.py:269
  45.4 5.2 %collective-permute-start.5 = (f32[32,64]{1,0:T(8,128)S(1)}, f32[32,64]{1,0:T(8,128)S(1)}, u32[]{:S(2)}, u32[]{:S(2)}) collective-permute-start(f32[32,64]{1,0:T(8,128)S(1)} %get-tuple-element.47), channel_id=1, source_target_pairs={{0,0},{1,4},{2,1},{3,5},{4,2},{5,6},{6,3},{7,7},{8,8},{9,12},{10,9... | collective-permute-start | bytes 24584 | tf_op jit(solution)/shard_map/ppermute | solution.py:364
  46.1 8.9 %collective-permute-start.6 = (f32[32,64]{1,0:T(8,128)S(1)}, f32[32,64]{1,0:T(8,128)S(1)}, u32[]{:S(2)}, u32[]{:S(2)}) collective-permute-start(f32[32,64]{1,0:T(8,128)S(1)} %get-tuple-element.48), channel_id=1, source_target_pairs={{0,4},{1,0},{2,5},{3,1},{4,6},{5,2},{6,7},{7,3},{8,12},{9,8},{10,1... | collective-permute-start | bytes 24584 | tf_op jit(solution)/shard_map/ppermute | solution.py:364

commit v9 on v8

--- a/solution.py
+++ b/solution.py
@@ -169,12 +169,9 @@
     keep = exists(2)
     fetch.wait()
 
-    def one(n, carry):
-        f, h = n // height, n % height
-        widen(rows_in[f, h], wide.at[h, f], keep)
-        return carry
-
-    lax.fori_loop(0, frames * height, one, 0)
+    for h in range(height):
+        for f in range(frames):
+            widen(rows_in[f, h], wide.at[h, f], keep)
     for tap_time in (0, 1):
         for tap_row in (1, 0, 2):
             rows = tap_rows(tap_row, height)

time: 56.3 us -> 56.3 us (level)
  no operation moved by 1% of the time
where the time goes in v9:
time: 56.3 us; the launch traced here: 55.6 us
  Pallas kernels  34.5 us (61%)
  starting transfers between devices  12.2 us (22%)
  waiting for transfers between devices  8.13 us (14%)
  other arithmetic  0.63 us (1%)
    pallas_call x7, Pallas kernels, call(): pl.pallas_call(kernel, in_specs=specs, out_specs=out_specs, out_shape=out...  34.5 us
    ppermute x5, starting transfers between devices, shifted(): return lax.ppermute(value, AXES, pairs)  6.58 us
    ppermute x2, starting transfers between devices, routed(): return lax.ppermute(value, AXES, pairs)  5.62 us
    ppermute x2, waiting for transfers between devices, routed(): return lax.ppermute(value, AXES, pairs)  4.34 us
    ppermute x5, waiting for transfers between devices, shifted(): return lax.ppermute(value, AXES, pairs)  3.79 us
  transfers between devices with their start and end apart: 7, of which 4 were waited for; matrix products, arithmetic and copies ran while one was open for 0% of the time, Pallas kernels for 57%

profile of v9, /device:TPU:8, one launch (start us, length us, event | category | flops | bytes accessed | tf_op | source)
XLA Modules:
  0.0 55.6 jit_solution(6070173406998592821)
XLA Ops:
  0.0 1.0 %send_up.1.up_ref = bf16[4,1,128,384]{3,2,1,0:T(8,128)(2,1)S(1)} custom-call(bf16[4,4,128,384]{3,2,1,0:T(8,128)(2,1)} %x_ref.5), custom_call_target="tpu_custom_call" | custom-call | bytes 4000000 | tf_op jit(solution)/shard_map/send_up/pallas_call | solution.py:275
  1.0 2.4 %collective-permute-start = (bf16[4,1,128,384]{3,2,1,0:T(8,128)(2,1)S(1)}, bf16[4,1,128,384]{3,2,1,0:T(8,128)(2,1)S(1)}, u32[]{:S(2)}, u32[]{:S(2)}) collective-permute-start(bf16[4,1,128,384]{3,2,1,0:T(8,128)(2,1)S(1)} %send_up.1.up_ref), channel_id=1, source_target_pairs={{0,1},{1,2},{2,3},{3,4},{4,5},{5,6},{6,7},{7,0},{8,9},{9,10},{10,1... | collective-permute-start | bytes 1179656 | tf_op jit(solution)/shard_map/ppermute | solution.py:266
  3.4 1.3 %send.1 = (bf16[4,1,128,384]{3,2,1,0:T(8,128)(2,1)S(1)}, bf16[2,4,128,384]{3,2,1,0:T(8,128)(2,1)S(1)}) custom-call(bf16[4,4,128,384]{3,2,1,0:T(8,128)(2,1)} %x_ref.5, bf16[4,1,128,384]{3,2,1,0:T(8,128)(2,1)S(1)} %send_up.1.up_ref), custom_call_target="tpu_custom_call" | custom-call | flops 113246208 | bytes 4000000 | tf_op jit(solution)/shard_map/send/pallas_call | solution.py:275
  4.7 3.6 %collective-permute-start.1 = (bf16[4,1,128,384]{3,2,1,0:T(8,128)(2,1)S(1)}, bf16[4,1,128,384]{3,2,1,0:T(8,128)(2,1)S(1)}, u32[]{:S(2)}, u32[]{:S(2)}) collective-permute-start(bf16[4,1,128,384]{3,2,1,0:T(8,128)(2,1)S(1)} %get-tuple-element.26), channel_id=1, source_target_pairs={{0,7},{1,0},{2,1},{3,2},{4,3},{5,4},{6,5},{7,6},{8,15},{9,8},{10,9... | collective-permute-start | bytes 1179656 | tf_op jit(solution)/shard_map/ppermute | solution.py:266
  8.2 0.0 collective-permute-start.2
  8.2 17.3 %own.1 = (f32[4,4,384,128]{3,2,1,0:T(8,128)S(1)}, bf16[3,3,384,1152]{3,2,1,0:T(8,128)(2,1)S(1)}, f32[384,128]{1,0:T(8,128)S(1)}, bf16[3,2,2,16,384]{4,3,2,1,0:T(...) custom-call(bf16[4,4,128,384]{3,2,1,0:T(8,128)(2,1)} %x_ref.5, ...), custom_call_target="tpu_custom_call" | custom-call | flops 10192158720 | bytes 4000000 | tf_op jit(solution)/shard_map/own/pallas_call | solution.py:275
  25.5 0.0 collective-permute-done.2.x_ref
  25.5 5.0 %earlier.1 = (f32[2,2,384,128]{3,2,1,0:T(8,128)}, f32[3,128,128]{2,1,0:T(8,128)}, f32[2,2,384,128]{3,2,1,0:T(8,128)S(1)}, f32[3,128,128]{2,1,0:T(8,128)S(1)}) custom-call(bf16[2,4,128,384]{3,2,1,0:T(8,128)(2,1)S(1)} %collective-permute-done.2.x_ref, f32[4,4,384,128]{3,2,1,0:T(8,128)S(1)} %get-tuple-element.28.acc, ...), custom_call_target="tpu_custom_call" | custom-call | flops 3397386240 | bytes 4000000 | tf_op jit(solution)/shard_map/earlier/pallas_call | solution.py:275
  30.5 0.0 copy-start
  30.5 0.0 collective-permute-done.up
  30.5 1.1 %collective-permute-done.1.dn = bf16[4,1,128,384]{3,2,1,0:T(8,128)(2,1)S(1)} collective-permute-done((bf16[4,1,128,384]{3,2,1,0:T(8,128)(2,1)S(1)}, bf16[4,1,128,384]{3,2,1,0:T(8,128)(2,1)S(1)}, u32[]{:S(2)}, u32[]{:S(2)}) %collective-permute-start.1) | collective-permute-done | bytes 393248 | tf_op jit(solution)/shard_map/ppermute | solution.py:266
  31.6 0.8 %relay.1 = bf16[2,2,128,384]{3,2,1,0:T(8,128)(2,1)} custom-call(bf16[4,1,128,384]{3,2,1,0:T(8,128)(2,1)S(1)} %collective-permute-done.up, bf16[4,1,128,384]{3,2,1,0:T(8,128)(2,1)S(1)} %collective-permute-done.1.dn), custom_call_target="tpu_custom_call" | custom-call | flops 113246208 | bytes 4000000 | tf_op jit(solution)/shard_map/relay/pallas_call | solution.py:275
  32.4 0.6 collective-permute-start.3
  33.0 6.7 %rows.1 = (f32[2,4,384,128]{3,2,1,0:T(8,128)S(1)}, bf16[3,2,384,1152]{3,2,1,0:T(8,128)(2,1)S(1)}, f32[384,128]{1,0:T(8,128)S(1)}, bf16[3,2,2,16,384]{4,3,2,1,0:T...) custom-call(bf16[4,1,128,384]{3,2,1,0:T(8,128)(2,1)S(1)} %collective-permute-done.up, ...), custom_call_target="tpu_custom_call" | custom-call | flops 2038431744 | bytes 4000000 | tf_op jit(solution)/shard_map/rows/pallas_call | solution.py:275
  39.7 0.1 collective-permute-start.4
  39.8 2.3 %collective-permute-done.3.corner = bf16[2,2,128,384]{3,2,1,0:T(8,128)(2,1)S(1)} collective-permute-done((bf16[2,2,128,384]{3,2,1,0:T(8,128)(2,1)}, bf16[2,2,128,384]{3,2,1,0:T(8,128)(2,1)S(1)}, u32[]{:S(2)}, u32[]{:S(2)}) %collective-permute-start.3) | collective-permute-done | bytes 393248 | tf_op jit(solution)/shard_map/ppermute | solution.py:266
  42.0 0.0 copy-done
  42.0 2.6 %corners.1 = f32[2,32,64]{2,1,0:T(8,128)S(1)} custom-call(bf16[2,2,128,384]{3,2,1,0:T(8,128)(2,1)S(1)} %collective-permute-done.3.corner, f32[2,4,384,128]{3,2,1,0:T(8,128)S(1)} %get-tuple-element.39.edge_in, bf16[3,2,384,1152]{3,2,1,0:T(8,128)(2,1)S(1)} %get-tuple-element.40.weights, f32[384,128]{1,0:T(8,128)S(1)} %get-tuple-element.41.bias_ref, ...), custom_call_target="tpu_custom_call" | custom-call | flops 679477248 | bytes 4000000 | tf_op jit(solution)/shard_map/corners/pallas_call | solution.py:275
  44.6 0.4 collective-permute-done.4
  45.0 0.7 %collective-permute-start.5 = (f32[32,64]{1,0:T(8,128)S(1)}, f32[32,64]{1,0:T(8,128)S(1)}, u32[]{:S(2)}, u32[]{:S(2)}) collective-permute-start(f32[32,64]{1,0:T(8,128)S(1)} %get-tuple-element.47), channel_id=1, source_target_pairs={{0,0},{1,4},{2,1},{3,5},{4,2},{5,6},{6,3},{7,7},{8,8},{9,12},{10,9... | collective-permute-start | bytes 24584 | tf_op jit(solution)/shard_map/ppermute | solution.py:361
  45.7 5.0 %collective-permute-start.6 = (f32[32,64]{1,0:T(8,128)S(1)}, f32[32,64]{1,0:T(8,128)S(1)}, u32[]{:S(2)}, u32[]{:S(2)}) collective-permute-start(f32[32,64]{1,0:T(8,128)S(1)} %get-tuple-element.48), channel_id=1, source_target_pairs={{0,4},{1,0},{2,5},{3,1},{4,6},{5,2},{6,7},{7,3},{8,12},{9,8},{10,1... | collective-permute-start | bytes 24584 | tf_op jit(solution)/shard_map/ppermute | solution.py:361
  50.6 0.0 collective-permute-done.5
  50.6 4.3 %collective-permute-done.6 = f32[32,64]{1,0:T(8,128)S(1)} collective-permute-done((f32[32,64]{1,0:T(8,128)S(1)}, f32[32,64]{1,0:T(8,128)S(1)}, u32[]{:S(2)}, u32[]{:S(2)}) %collective-permute-start.6) | collective-permute-done | bytes 8224 | tf_op jit(solution)/shard_map/ppermute | solution.py:361
  55.0 0.6 %pad_maximum_fusion = f32[64,64]{1,0:T(8,128)} fusion(f32[32,64]{1,0:T(8,128)S(1)} %get-tuple-element.50, f32[32,64]{1,0:T(8,128)S(1)} %get-tuple-element.49), kind=kLoop, calls=%fused_computation | loop fusion | flops 4096 | bytes 32768 | tf_op jit(solution)/shard_map/concatenate | solution.py:369
  (2 shorter events, 0.0 us)
Async XLA Ops:
  1.0 29.5 %collective-permute-start = (bf16[4,1,128,384]{3,2,1,0:T(8,128)(2,1)S(1)}, bf16[4,1,128,384]{3,2,1,0:T(8,128)(2,1)S(1)}, u32[]{:S(2)}, u32[]{:S(2)}) collective-permute-start(bf16[4,1,128,384]{3,2,1,0:T(8,128)(2,1)S(1)} %send_up.1.up_ref), channel_id=1, source_target_pairs={{0,1},{1,2},{2,3},{3,4},{4,5},{5,6},{6,7},{7,0},{8,9},{9,10},{10,1... | collective-permute-start | bytes 1179656 | tf_op jit(solution)/shard_map/ppermute | solution.py:266
  4.7 27.0 %collective-permute-start.1 = (bf16[4,1,128,384]{3,2,1,0:T(8,128)(2,1)S(1)}, bf16[4,1,128,384]{3,2,1,0:T(8,128)(2,1)S(1)}, u32[]{:S(2)}, u32[]{:S(2)}) collective-permute-start(bf16[4,1,128,384]{3,2,1,0:T(8,128)(2,1)S(1)} %get-tuple-element.26), channel_id=1, source_target_pairs={{0,7},{1,0},{2,1},{3,2},{4,3},{5,4},{6,5},{7,6},{8,15},{9,8},{10,9... | collective-permute-start | bytes 1179656 | tf_op jit(solution)/shard_map/ppermute | solution.py:266
  8.2 17.3 %collective-permute-start.2 = (bf16[2,4,128,384]{3,2,1,0:T(8,128)(2,1)S(1)}, bf16[2,4,128,384]{3,2,1,0:T(8,128)(2,1)S(1)}, u32[]{:S(2)}, u32[]{:S(2)}) collective-permute-start(bf16[2,4,128,384]{3,2,1,0:T(8,128)(2,1)S(1)} %get-tuple-element.27), channel_id=1, source_target_pairs={{0,8},{1,9},{2,10},{3,11},{4,12},{5,13},{6,14},{7,15},{8,16},{9,17... | collective-permute-start | bytes 2359304 | tf_op jit(solution)/shard_map/ppermute | solution.py:266
  30.5 11.5 %copy-start = (f32[16]{0:T(128)S(1)}, f32[16]{0:T(128)}, u32[]{:S(2)}) copy-start(f32[16]{0:T(128)} %down_bias_ref.1) | copy-start | bytes 196
  32.4 9.6 %collective-permute-start.3 = (bf16[2,2,128,384]{3,2,1,0:T(8,128)(2,1)}, bf16[2,2,128,384]{3,2,1,0:T(8,128)(2,1)S(1)}, u32[]{:S(2)}, u32[]{:S(2)}) collective-permute-start(bf16[2,2,128,384]{3,2,1,0:T(8,128)(2,1)} %relay.1), channel_id=1, source_target_pairs={{0,8},{1,9},{2,10},{3,11},{4,12},{5,13},{6,14},{7,15},{8,16},{9,17... | collective-permute-start | bytes 1179656 | tf_op jit(solution)/shard_map/ppermute | solution.py:266
  39.7 5.3 %collective-permute-start.4 = (f32[32,64]{1,0:T(8,128)S(1)}, f32[32,64]{1,0:T(8,128)S(1)}, u32[]{:S(2)}, u32[]{:S(2)}) collective-permute-start(f32[32,64]{1,0:T(8,128)S(1)} %get-tuple-element.46), channel_id=1, source_target_pairs={{0,8},{1,9},{2,10},{3,11},{4,12},{5,13},{6,14},{7,15},{8,16},{9,17... | collective-permute-start | bytes 24584 | tf_op jit(solution)/shard_map/ppermute | solution.py:266
  45.0 5.6 %collective-permute-start.5 = (f32[32,64]{1,0:T(8,128)S(1)}, f32[32,64]{1,0:T(8,128)S(1)}, u32[]{:S(2)}, u32[]{:S(2)}) collective-permute-start(f32[32,64]{1,0:T(8,128)S(1)} %get-tuple-element.47), channel_id=1, source_target_pairs={{0,0},{1,4},{2,1},{3,5},{4,2},{5,6},{6,3},{7,7},{8,8},{9,12},{10,9... | collective-permute-start | bytes 24584 | tf_op jit(solution)/shard_map/ppermute | solution.py:361
  45.7 9.3 %collective-permute-start.6 = (f32[32,64]{1,0:T(8,128)S(1)}, f32[32,64]{1,0:T(8,128)S(1)}, u32[]{:S(2)}, u32[]{:S(2)}) collective-permute-start(f32[32,64]{1,0:T(8,128)S(1)} %get-tuple-element.48), channel_id=1, source_target_pairs={{0,4},{1,0},{2,5},{3,1},{4,6},{5,2},{6,7},{7,3},{8,12},{9,8},{10,1... | collective-permute-start | bytes 24584 | tf_op jit(solution)/shard_map/ppermute | solution.py:361
